TPU v7x, 32 devices: a whole 2x2x4 slice. The times are simulated.
32 devices in a mesh: fsdp: 8 (over z, core), seq: 4 (over y, x).
Axes of the slice: x: 2, y: 2, z: 4, core: 2. Of those that a mesh axis runs over, the one named last changes fastest.
Arguments:
- tokens: bfloat16 [8, 1024, 2048], P('fsdp', 'seq'), may hold values from -6 to 6
- segments: int32 [8, 1024], P('fsdp'), may hold values from -1 to 513, as said below
- buckets: int32 [2047], replicated, may hold values from 0 to 31, as said below
- w_query: bfloat16 [2048, 2048], P('fsdp'), may hold values from -0.0625 to 0.0625
- w_key: bfloat16 [2048, 2048], P('fsdp'), may hold values from -0.0625 to 0.0625
- w_value: bfloat16 [2048, 2048], P('fsdp'), may hold values from -0.125 to 0.125
- w_attn_out: bfloat16 [2048, 2048], P('fsdp'), may hold values from -0.5 to 0.5
- gain_attn: bfloat16 [2048], P('fsdp'), may hold values from 0.25 to 1.75
- rel_table: float32 [32, 32], replicated, may hold values from -4 to 4
- w_gate: bfloat16 [2048, 5120], P('fsdp'), may hold values from -0.125 to 0.125
- w_up: bfloat16 [2048, 5120], P('fsdp'), may hold values from -0.125 to 0.125
- w_down: bfloat16 [2048, 5120], P('fsdp'), may hold values from -0.078125 to 0.078125
- gain_ffn: bfloat16 [2048], P('fsdp'), may hold values from 0.25 to 1.75
- out_grad: bfloat16 [8, 1024, 2048], P('fsdp', 'seq'), may hold values from -6 to 6
Outputs:
- layer_out: bfloat16 [8, 1024, 2048], P('fsdp', 'seq')
- input_grad: bfloat16 [8, 1024, 2048], P('fsdp', 'seq')
- w_query_grad: float32 [2048, 2048], P('fsdp')
- w_key_grad: float32 [2048, 2048], P('fsdp')
- w_value_grad: float32 [2048, 2048], P('fsdp')
- w_attn_out_grad: float32 [2048, 2048], P('fsdp')
- gain_attn_grad: float32 [2048], P('fsdp')
- rel_table_grad: float32 [32, 32], P('fsdp')
- w_gate_grad: float32 [2048, 5120], P('fsdp')
- w_up_grad: float32 [2048, 5120], P('fsdp')
- w_down_grad: float32 [2048, 5120], P('fsdp')
- gain_ffn_grad: float32 [2048], P('fsdp')
- rms_stats: float32 [3], replicated
Inputs may be any that keep to these rules, and one draw needn't show every extreme that they name: `segments`: in each row the numbers never decrease before the padding, which is the last 1 to 128 tokens with -1; each row's last document before the padding has the number 2 * 256 + 1. One document of each row begins within the row's first 256 tokens and ends within its last 257 tokens, with at least one short document after it; the other documents are short, of heavy-tailed lengths. Entry 1023 + r holds the bucket of the offset r = key position - query position: buckets 0 to 15 for r <= 0, the others for r > 0, not falling as |r| grows on each side; every bucket occurs.
All inputs are finite; a program needn't handle non-finite values.
Results may differ from a plain program's by a relative error of at most 0.019.
Values may be sent and summed in bfloat16 or wider, within the bound.
No kernel may reach another device: no remote copies, remote signals or barrier semaphores. Data moves between devices by JAX's collectives and lax.ppermute only.
A program may use at most 704 MiB of HBM per device.

v0:
```python
import jax
import jax.numpy as jnp
from jax import lax
from jax.sharding import PartitionSpec as P

DH = 64


EPSILON = 1e-06
PRECISE = lax.Precision.HIGHEST
MASKED_SCORE = -1e30


def rows_dot(left, right):
    return lax.dot_general(
        left, right, (((0,), (0,)), ((), ())), preferred_element_type=jnp.float32
    )


def cols_dot(left, right):
    return lax.dot_general(
        left, right, (((1,), (1,)), ((), ())), preferred_element_type=jnp.float32
    )


def norm_back(grad_hat, normed, scale):
    return scale * (grad_hat - normed * jnp.mean(grad_hat * normed, axis=-1, keepdims=True))


def gated_unit(gate, up_proj):
    return jax.nn.gelu(gate, approximate=True) * up_proj


def toeplitz_bias(relative, first_row, block_rows, row_length):
    width = row_length + block_rows - 1
    begin = row_length - first_row - block_rows
    window = lax.dynamic_slice_in_dim(relative, begin, width, 1)
    turned = jnp.concatenate([window[:, block_rows - 1 :], window[:, : block_rows - 1]], axis=1)
    tiled = jnp.tile(turned, (1, block_rows))[:, : block_rows * (width - 1)]
    return tiled.reshape(relative.shape[0], block_rows, width - 1)[:, :, :row_length]


def offset_sums(score_grad, block_rows, row_length):
    head_count = score_grad.shape[0]
    width = row_length + block_rows - 1
    padded = jnp.pad(score_grad, ((0, 0), (0, 0), (0, width - 1 - row_length)))
    flat = jnp.pad(padded.reshape(head_count, block_rows * (width - 1)), ((0, 0), (0, block_rows)))
    folded = jnp.sum(flat.reshape(head_count, block_rows, width), axis=1)
    return jnp.concatenate([folded[:, row_length:], folded[:, :row_length]], axis=1)


def block_scores(query_block, key_rows, segment_block, segment_row, first_row, relative):
    row_length = segment_row.shape[0]
    block_rows = query_block.shape[0]
    scores = jnp.einsum(
        "qhd,khd->hqk", query_block, key_rows, preferred_element_type=jnp.float32
    ) + toeplitz_bias(relative, first_row, block_rows, row_length)
    allowed = segment_block[:, None] == segment_row[None, :]
    return jnp.where(allowed[None, :, :], scores, MASKED_SCORE)


def attention_forward(query_rows, key_rows, value_rows, segment_row, relative, block_rows):
    blocks = query_rows.shape[0] // block_rows

    def one_block(block_index):
        first_row = block_index * block_rows
        query_block = lax.dynamic_slice_in_dim(query_rows, first_row, block_rows, 0)
        segment_block = lax.dynamic_slice_in_dim(segment_row, first_row, block_rows, 0)
        scores = block_scores(
            query_block, key_rows, segment_block, segment_row, first_row, relative
        )
        highest = jnp.max(scores, axis=-1, keepdims=True)
        exponent = jnp.exp(scores - highest)
        totals = jnp.sum(exponent, axis=-1, keepdims=True)
        attention = (exponent / totals).astype(jnp.bfloat16)
        context = jnp.einsum(
            "hqk,khd->qhd", attention, value_rows, preferred_element_type=jnp.float32
        )
        return (context.astype(jnp.bfloat16), (highest + jnp.log(totals))[:, :, 0])

    return lax.map(one_block, jnp.arange(blocks, dtype=jnp.int32))


def attention_backward(
    query_rows, key_rows, value_rows, segment_row, relative, log_total, context_grad, block_rows
):
    row_length, head_count, head_size = query_rows.shape
    blocks = row_length // block_rows
    width = row_length + block_rows - 1

    def one_block(carry, pieces):
        key_grad, value_grad, relative_grad = carry
        block_index, block_total = pieces
        first_row = block_index * block_rows
        query_block = lax.dynamic_slice_in_dim(query_rows, first_row, block_rows, 0)
        segment_block = lax.dynamic_slice_in_dim(segment_row, first_row, block_rows, 0)
        grad_block = lax.dynamic_slice_in_dim(context_grad, first_row, block_rows, 0)
        scores = block_scores(
            query_block, key_rows, segment_block, segment_row, first_row, relative
        )
        attention = jnp.exp(scores - block_total[:, :, None])
        attention_grad = jnp.einsum(
            "qhd,khd->hqk", grad_block, value_rows, preferred_element_type=jnp.float32
        )
        centre = jnp.sum(attention * attention_grad, axis=-1, keepdims=True)
        score_grad = attention * (attention_grad - centre)
        begin = row_length - first_row - block_rows
        current = lax.dynamic_slice_in_dim(relative_grad, begin, width, 1)
        relative_grad = lax.dynamic_update_slice_in_dim(
            relative_grad, current + offset_sums(score_grad, block_rows, row_length), begin, 1
        )
        score_low = score_grad.astype(jnp.bfloat16)
        attention_low = attention.astype(jnp.bfloat16)
        query_grad = jnp.einsum(
            "hqk,khd->qhd", score_low, key_rows, preferred_element_type=jnp.float32
        )
        key_grad = key_grad + jnp.einsum(
            "hqk,qhd->khd", score_low, query_block, preferred_element_type=jnp.float32
        )
        value_grad = value_grad + jnp.einsum(
            "hqk,qhd->khd", attention_low, grad_block, preferred_element_type=jnp.float32
        )
        return ((key_grad, value_grad, relative_grad), query_grad)

    zero_rows = jnp.zeros((row_length, head_count, head_size), jnp.float32)
    start_carry = (zero_rows, zero_rows, jnp.zeros((head_count, 2 * row_length - 1), jnp.float32))
    carried, query_grad = lax.scan(
        one_block, start_carry, (jnp.arange(blocks, dtype=jnp.int32), log_total)
    )
    key_grad, value_grad, relative_grad = carried
    return (
        query_grad.reshape(row_length, -1),
        key_grad.reshape(row_length, -1),
        value_grad.reshape(row_length, -1),
        relative_grad,
    )


def on_device(
    tokens,
    segments,
    buckets,
    w_query,
    w_key,
    w_value,
    w_attn_out,
    gain_attn,
    rel_table,
    w_gate,
    w_up,
    w_down,
    gain_ffn,
    out_grad,
):
    token_rows = tokens.shape[1]
    model_width = tokens.shape[2]
    ffn_width = w_gate.shape[1]
    segment_row = segments[0]
    row_length = segment_row.shape[0]
    block_rows = min(512, row_length)
    seq_count = lax.axis_size("seq")
    fsdp_count = lax.axis_size("fsdp")
    seq_place = lax.axis_index("seq")
    fsdp_place = lax.axis_index("fsdp")
    head_count = model_width // seq_count // DH
    head_shape = (row_length, head_count, DH)
    bucket_table = (
        buckets[:, None] == jnp.arange(rel_table.shape[1], dtype=jnp.int32)[None, :]
    ).astype(jnp.float32)
    local_table = lax.dynamic_slice_in_dim(rel_table, seq_place * head_count, head_count, 0)
    relative = jnp.dot(local_table, jnp.transpose(bucket_table), precision=PRECISE)
    stream = tokens[0].astype(jnp.float32)
    scale_attn = lax.rsqrt(jnp.mean(stream * stream, axis=-1, keepdims=True) + EPSILON)
    normed_attn = stream * scale_attn
    upstream = out_grad[0].astype(jnp.float32)
    ff_grad = upstream.astype(jnp.bfloat16)
    column_count = model_width // seq_count
    unit_count = ffn_width // seq_count

    def columns(weight, count):
        return lax.dynamic_slice_in_dim(weight, seq_place * count, count, 1)

    sliced = (
        lax.all_gather(gain_attn, "fsdp", axis=0, tiled=True),
        lax.all_gather(gain_ffn, "fsdp", axis=0, tiled=True),
        lax.all_gather(columns(w_query, column_count), "fsdp", axis=0, tiled=True),
        lax.all_gather(columns(w_key, column_count), "fsdp", axis=0, tiled=True),
        lax.all_gather(columns(w_value, column_count), "fsdp", axis=0, tiled=True),
        lax.all_gather(columns(w_attn_out, column_count), "fsdp", axis=0, tiled=True),
        lax.all_gather(columns(w_gate, unit_count), "fsdp", axis=0, tiled=True),
        lax.all_gather(columns(w_up, unit_count), "fsdp", axis=0, tiled=True),
        lax.all_gather(columns(w_down, unit_count), "fsdp", axis=0, tiled=True),
    )
    attn_gain, ffn_gain, query_w, key_w, value_w, output_w, gate_w, up_w, down_w = sliced

    def whole_row(piece):
        return lax.all_gather(piece, "seq", axis=0, tiled=True)

    def token_sum(term):
        return lax.psum_scatter(
            term(jnp.int32(0), lax.axis_size("seq") * token_rows),
            "seq",
            scatter_dimension=0,
            tiled=True,
        )

    attn_input = (normed_attn * attn_gain.astype(jnp.float32)).astype(jnp.bfloat16)
    attn_rows = whole_row(attn_input)
    query_rows = (
        jnp.dot(attn_rows, query_w, preferred_element_type=jnp.float32)
        .astype(jnp.bfloat16)
        .reshape(head_shape)
    )
    key_rows = (
        jnp.dot(attn_rows, key_w, preferred_element_type=jnp.float32)
        .astype(jnp.bfloat16)
        .reshape(head_shape)
    )
    value_rows = (
        jnp.dot(attn_rows, value_w, preferred_element_type=jnp.float32)
        .astype(jnp.bfloat16)
        .reshape(head_shape)
    )
    context_heads, log_total = attention_forward(
        query_rows, key_rows, value_rows, segment_row, relative, block_rows
    )
    context = context_heads.reshape(row_length, -1)

    def attn_term(first_row, row_count):
        return cols_dot(context, output_w)

    attn_out = token_sum(attn_term)
    resid = stream + attn_out
    scale_ffn = lax.rsqrt(jnp.mean(resid * resid, axis=-1, keepdims=True) + EPSILON)
    normed_ffn = resid * scale_ffn
    ffn_input = (normed_ffn * ffn_gain.astype(jnp.float32)).astype(jnp.bfloat16)
    ffn_rows = whole_row(ffn_input)
    gate = jnp.dot(ffn_rows, gate_w, preferred_element_type=jnp.float32)
    up_proj = jnp.dot(ffn_rows, up_w, preferred_element_type=jnp.float32)
    hidden = gated_unit(gate, up_proj).astype(jnp.bfloat16)

    def down_term(first_row, row_count):
        return cols_dot(hidden, down_w)

    ff_out = token_sum(down_term)
    result = resid + ff_out
    ff_grad_rows = whole_row(ff_grad)
    hidden_grad = jnp.dot(ff_grad_rows, down_w, preferred_element_type=jnp.float32)
    unused, pull = jax.vjp(gated_unit, gate, up_proj)
    gate_grad, up_grad = pull(hidden_grad)
    gate_grad = gate_grad.astype(jnp.bfloat16)
    up_grad = up_grad.astype(jnp.bfloat16)

    def pair_term(first_row, row_count):
        return cols_dot(gate_grad, gate_w) + cols_dot(up_grad, up_w)

    ffn_in_grad = token_sum(pair_term)
    gain_ffn_part = jnp.sum(ffn_in_grad * normed_ffn, axis=0)
    resid_grad = upstream + norm_back(
        ffn_in_grad * ffn_gain.astype(jnp.float32), normed_ffn, scale_ffn
    )
    attn_grad = resid_grad.astype(jnp.bfloat16)
    attn_grad_rows = whole_row(attn_grad)
    context_grad = jnp.dot(attn_grad_rows, output_w, preferred_element_type=jnp.float32).astype(
        jnp.bfloat16
    )
    query_grad, key_grad, value_grad, relative_grad = attention_backward(
        query_rows,
        key_rows,
        value_rows,
        segment_row,
        relative,
        log_total,
        context_grad.reshape(head_shape),
        block_rows,
    )
    query_back = query_grad.astype(jnp.bfloat16)
    key_back = key_grad.astype(jnp.bfloat16)
    value_back = value_grad.astype(jnp.bfloat16)

    def triple_term(first_row, row_count):
        return (
            cols_dot(query_back, query_w)
            + cols_dot(key_back, key_w)
            + cols_dot(value_back, value_w)
        )

    attn_in_grad = token_sum(triple_term)
    gain_attn_part = jnp.sum(attn_in_grad * normed_attn, axis=0)
    stream_grad = resid_grad + norm_back(
        attn_in_grad * attn_gain.astype(jnp.float32), normed_attn, scale_attn
    )
    owned = lax.psum_scatter(
        jnp.concatenate(
            [
                rows_dot(attn_rows, query_back),
                rows_dot(attn_rows, key_back),
                rows_dot(attn_rows, value_back),
                rows_dot(attn_grad_rows, context),
                rows_dot(ffn_rows, gate_grad),
                rows_dot(ffn_rows, up_grad),
                rows_dot(ff_grad_rows, hidden),
            ],
            axis=1,
        ).astype(jnp.bfloat16),
        "fsdp",
        scatter_dimension=0,
        tiled=True,
    ).astype(jnp.float32)
    widths = [column_count] * 4 + [unit_count] * 3
    edges = [0]
    for width in widths:
        edges.append(edges[-1] + width)
    pieces = tuple((owned[:, edges[place] : edges[place + 1]] for place in range(7)))
    gathered = (
        lax.all_gather(pieces[0].astype(jnp.bfloat16), "seq", axis=1, tiled=True).astype(
            jnp.float32
        ),
        lax.all_gather(pieces[1].astype(jnp.bfloat16), "seq", axis=1, tiled=True).astype(
            jnp.float32
        ),
        lax.all_gather(pieces[2].astype(jnp.bfloat16), "seq", axis=1, tiled=True).astype(
            jnp.float32
        ),
        lax.all_gather(pieces[3].astype(jnp.bfloat16), "seq", axis=1, tiled=True).astype(
            jnp.float32
        ),
        lax.all_gather(pieces[4].astype(jnp.bfloat16), "seq", axis=1, tiled=True).astype(
            jnp.float32
        ),
        lax.all_gather(pieces[5].astype(jnp.bfloat16), "seq", axis=1, tiled=True).astype(
            jnp.float32
        ),
        lax.all_gather(pieces[6].astype(jnp.bfloat16), "seq", axis=1, tiled=True).astype(
            jnp.float32
        ),
    )
    weight_grads = list(gathered)
    own_segments = lax.dynamic_slice_in_dim(segment_row, seq_place * token_rows, token_rows, 0)
    valid = (own_segments >= 0).astype(jnp.float32)
    stat_terms = jnp.stack(
        [
            jnp.sum(valid * jnp.sum(result * result, axis=-1)),
            jnp.sum(valid * jnp.sum(attn_out * attn_out, axis=-1)),
            jnp.sum(valid * jnp.sum(ff_out * ff_out, axis=-1)),
            jnp.sum(valid),
        ]
    )
    table_part = jnp.dot(relative_grad, bucket_table, precision=PRECISE)
    full_table = lax.dynamic_update_slice_in_dim(
        jnp.zeros(rel_table.shape, jnp.float32), table_part, seq_place * head_count, 0
    )
    summed = lax.psum((gain_attn_part, gain_ffn_part, full_table, stat_terms), ("fsdp", "seq"))
    stat_totals = summed[3]
    rms_stats = jnp.sqrt(stat_totals[0:3] / (stat_totals[3] * model_width))
    gain_rows = model_width // fsdp_count
    table_rows = rel_table.shape[0] // fsdp_count
    gain_attn_grad = lax.dynamic_slice_in_dim(summed[0], fsdp_place * gain_rows, gain_rows, 0)
    gain_ffn_grad = lax.dynamic_slice_in_dim(summed[1], fsdp_place * gain_rows, gain_rows, 0)
    rel_table_grad = lax.dynamic_slice_in_dim(summed[2], fsdp_place * table_rows, table_rows, 0)
    return (
        result.astype(jnp.bfloat16)[None],
        stream_grad.astype(jnp.bfloat16)[None],
        weight_grads[0],
        weight_grads[1],
        weight_grads[2],
        weight_grads[3],
        gain_attn_grad,
        rel_table_grad,
        weight_grads[4],
        weight_grads[5],
        weight_grads[6],
        gain_ffn_grad,
        rms_stats,
    )


def solution(mesh):
    in_specs = (
        P("fsdp", "seq", None),
        P("fsdp", None),
        P(),
        P("fsdp", None),
        P("fsdp", None),
        P("fsdp", None),
        P("fsdp", None),
        P("fsdp"),
        P(),
        P("fsdp", None),
        P("fsdp", None),
        P("fsdp", None),
        P("fsdp"),
        P("fsdp", "seq", None),
    )
    out_specs = (
        P("fsdp", "seq", None),
        P("fsdp", "seq", None),
        P("fsdp", None),
        P("fsdp", None),
        P("fsdp", None),
        P("fsdp", None),
        P("fsdp"),
        P("fsdp", None),
        P("fsdp", None),
        P("fsdp", None),
        P("fsdp", None),
        P("fsdp"),
        P(),
    )
    return jax.shard_map(
        on_device, mesh=mesh, in_specs=in_specs, out_specs=out_specs, check_vma=False
    )
```

profile of v0, /device:TPU:0, one launch (start us, length us, event | category | flops | bytes accessed | tf_op | source)
XLA Modules:
  0.0 2478.9 jit_solution(7415109027298716983)
XLA Ops:
  42.0 54.6 %all-gather.22.cloned.1.call-done = bf16[1024,2048]{1,0:T(8,128)(2,1)} async-done(((bf16[256,2048]{1,0:T(8,128)(2,1)}), bf16[1024,2048]{1,0:T(8,128)(2,1)}) %all-gather.22.cloned.1.call-update) | async-done | bytes 4194320 | tf_op jit(solution)/shard_map/all_gather | solution.py:197
  164.9 334.9 %while.37 = (s32[]{:T(128)}, bf16[2,512,8,64]{1,3,2,0:T(8,128)(2,1)}, f32[2,8,512]{2,1,0:T(8,128)S(1)}, s32[2]{0:T(128)S(1)}, s32[1024]{0:T(1024)S(1)}, /*index=...) while((s32[]{:T(128)}, ...), condition=%wide.region_4.5_spmd, body=%wide.region_1.4_spmd.sunk | while | flops 1108090880 | bytes 427927744 | solution.py:81
  178.2 37.9 %reshape.275 = f32[6287360]{0:T(1024)} reshape(f32[8,512,1535]{2,1,0:T(8,128)} %tile.36) | data formatting | bytes 50298880 | tf_op jit(solution)/shard_map/while
  345.3 37.8 %reshape.275 = f32[6287360]{0:T(1024)} reshape(f32[8,512,1535]{2,1,0:T(8,128)} %tile.36) | data formatting | bytes 50298880 | tf_op jit(solution)/shard_map/while
  522.4 74.7 %reduce-scatter.6.cloned.1.call-done = f32[256,2048]{1,0:T(8,128)} async-done(((f32[1024,2048]{1,0:T(8,128)}), f32[256,2048]{1,0:T(8,128)}) %reduce-scatter.6.cloned.1.call-update) | async-done | bytes 2097168 | tf_op jit(solution)/shard_map/reduce_scatter | solution.py:200
  606.2 49.2 %all-gather.34.cloned.1.call-done = bf16[2048,1280]{1,0:T(8,128)(2,1)} async-done(((bf16[256,1280]{1,0:T(8,128)(2,1)}), bf16[2048,1280]{1,0:T(8,128)(2,1)}) %all-gather.34.cloned.1.call-update) | async-done | bytes 5242896 | tf_op jit(solution)/shard_map/all_gather | solution.py:190
  655.4 54.1 %all-gather.32.cloned.1.call-done = bf16[1024,2048]{1,0:T(8,128)(2,1)} async-done(((bf16[256,2048]{1,0:T(8,128)(2,1)}), bf16[1024,2048]{1,0:T(8,128)(2,1)}) %all-gather.32.cloned.1.call-update) | async-done | bytes 4194320 | tf_op jit(solution)/shard_map/all_gather | solution.py:197
  720.0 47.9 %all-gather.36.cloned.1.call-done = bf16[2048,1280]{1,0:T(8,128)(2,1)} async-done(((bf16[256,1280]{1,0:T(8,128)(2,1)}), bf16[2048,1280]{1,0:T(8,128)(2,1)}) %all-gather.36.cloned.1.call-update) | async-done | bytes 5242896 | tf_op jit(solution)/shard_map/all_gather | solution.py:191
  778.3 43.0 %all-gather.56.cloned.1.call-done = bf16[1,1024,2048]{2,1,0:T(8,128)(2,1)} async-done(((bf16[1,256,2048]{2,1,0:T(8,128)(2,1)}), bf16[1,1024,2048]{2,1,0:T(8,128)(2,1)}) %all-gather.56.cloned.1.call-update) | async-done | bytes 4194320 | tf_op jit(solution)/shard_map/all_gather | solution.py:197
  821.2 58.4 %all-gather.38.cloned.1.call-done = bf16[2048,1280]{1,0:T(8,128)(2,1)} async-done(((bf16[256,1280]{1,0:T(8,128)(2,1)}), bf16[2048,1280]{1,0:T(8,128)(2,1)}) %all-gather.38.cloned.1.call-update) | async-done | bytes 5242896 | tf_op jit(solution)/shard_map/all_gather | solution.py:192
  925.1 66.1 %reduce-scatter.8.cloned.1.call-done = f32[256,2048]{1,0:T(8,128)} async-done(((f32[1024,2048]{1,0:T(8,128)}), f32[256,2048]{1,0:T(8,128)}) %reduce-scatter.8.cloned.1.call-update) | async-done | bytes 2097168 | tf_op jit(solution)/shard_map/reduce_scatter | solution.py:200
  991.2 89.5 %reduce-scatter.10.cloned.1.call-done = f32[256,2048]{1,0:T(8,128)} async-done(((f32[1024,2048]{1,0:T(8,128)}), f32[256,2048]{1,0:T(8,128)}) %reduce-scatter.10.cloned.1.call-update) | async-done | bytes 2097168 | tf_op jit(solution)/shard_map/reduce_scatter | solution.py:200
  1088.5 52.8 %all-gather.40.cloned.1.call-done = bf16[1024,2048]{1,0:T(8,128)(2,1)} async-done(((bf16[256,2048]{1,0:T(8,128)(2,1)}), bf16[1024,2048]{1,0:T(8,128)(2,1)}) %all-gather.40.cloned.1.call-update) | async-done | bytes 4194320 | tf_op jit(solution)/shard_map/all_gather | solution.py:197
  1148.1 707.5 %while.38 = (s32[]{:T(128)}, f32[1024,8,64]{0,2,1:T(8,128)}, f32[1024,8,64]{0,2,1:T(8,128)}, f32[8,2047]{1,0:T(8,128)}, bf16[2,512,8,64]{1,3,2,0:T(8,128)(2,1)},...) while((s32[]{:T(128)}, f32[1024,8,64]{0,2,1:T(8,128)}, ...), condition=%wide.region_13.14_spmd.clone, body=%wide.region_10.13_spmd.clone.sunk | while | flops 2735226880 | bytes 843474880 | solution.py:127
  1170.5 38.3 %reshape.278 = f32[6287360]{0:T(1024)} reshape(f32[8,512,1535]{2,1,0:T(8,128)} %tile.38) | data formatting | bytes 50298880 | tf_op jit(solution)/shard_map/while
  1438.0 39.4 %reshape.284 = f32[8,512,1535]{2,1,0:T(8,128)} reshape(f32[6287360]{0:T(1024)} %reshape.283) | data formatting | bytes 50298880 | tf_op jit(solution)/shard_map/while/body/eval_jaxpr/reshape | solution.py:48
  1519.5 38.0 %reshape.278 = f32[6287360]{0:T(1024)} reshape(f32[8,512,1535]{2,1,0:T(8,128)} %tile.38) | data formatting | bytes 50298880 | tf_op jit(solution)/shard_map/while
  1788.1 39.6 %reshape.284 = f32[8,512,1535]{2,1,0:T(8,128)} reshape(f32[6287360]{0:T(1024)} %reshape.283) | data formatting | bytes 50298880 | tf_op jit(solution)/shard_map/while/body/eval_jaxpr/reshape | solution.py:48
  1912.5 224.6 %reduce-scatter.14.cloned.1.call-done = bf16[256,5888]{0,1:T(8,128)(2,1)} async-done(((bf16[2048,5888]{0,1:T(8,128)(2,1)}), bf16[256,5888]{0,1:T(8,128)(2,1)}) %reduce-scatter.14.cloned.1.call-update) | async-done | bytes 3014672 | tf_op jit(solution)/shard_map/reduce_scatter | solution.py:293
  2149.7 75.5 %reduce-scatter.12.cloned.1.call-done = f32[256,2048]{1,0:T(8,128)} async-done(((f32[1024,2048]{1,0:T(8,128)}), f32[256,2048]{1,0:T(8,128)}) %reduce-scatter.12.cloned.1.call-update) | async-done | bytes 2097168 | tf_op jit(solution)/shard_map/reduce_scatter | solution.py:200
  2227.7 40.2 %all-reduce.2 = (f32[2048]{0:T(1024)S(1)}, f32[32,32]{1,0:T(8,128)S(1)}, f32[2048]{0:T(1024)S(1)}, f32[4]{0:T(128)S(1)}) all-reduce(f32[2048]{0:T(1024)S(1)} %get-tuple-element.582, f32[32,32]{1,0:T(8,128)S(1)} %convolution_dynamic-update-slice_fusion, f32[2048]{0:T(1024)S(1)} %copy-done.32, ...), channel_id=1, replica_groups=mesh['fsdp'=8,'seq'=4] {'fsdp','seq'}, use_global_device_ids=true, to_apply=%region_18.19 | all-reduce | flops 5124 | bytes 40992 | tf_op jit(solution)/shard_map/psum | solution.py:353
  2343.3 39.5 %all-gather.50.cloned.1.call-done = bf16[256,5120]{0,1:T(8,128)(2,1)} async-done(((bf16[256,1280]{0,1:T(8,128)(2,1)}), bf16[256,5120]{0,1:T(8,128)(2,1)}) %all-gather.50.cloned.1.call-update) | async-done | bytes 2621456 | tf_op jit(solution)/shard_map/all_gather | solution.py:328
  2387.7 37.2 %all-gather.52.cloned.1.call-done = bf16[256,5120]{0,1:T(8,128)(2,1)} async-done(((bf16[256,1280]{0,1:T(8,128)(2,1)}), bf16[256,5120]{0,1:T(8,128)(2,1)}) %all-gather.52.cloned.1.call-update) | async-done | bytes 2621456 | tf_op jit(solution)/shard_map/all_gather | solution.py:331
  2430.0 37.1 %all-gather.54.cloned.1.call-done = bf16[256,5120]{0,1:T(8,128)(2,1)} async-done(((bf16[256,1280]{0,1:T(8,128)(2,1)}), bf16[256,5120]{0,1:T(8,128)(2,1)}) %all-gather.54.cloned.1.call-update) | async-done | bytes 2621456 | tf_op jit(solution)/shard_map/all_gather | solution.py:334
  (384 shorter events, 1175.1 us)
Async XLA Ops:
  7.2 34.8 %all-gather.24.cloned.1.call-start = ((), (), s32[]{:S(2)}) async-start(), calls=%async_computation.6 | async-start | bytes 2359296 | tf_op jit(solution)/shard_map/all_gather | solution.py:186
  9.1 87.6 %all-gather.22.cloned.1.call-start = ((), (), s32[]{:S(2)}) async-start(), calls=%async_computation.5 | async-start | bytes 5242880 | tf_op jit(solution)/shard_map/all_gather | solution.py:197
  27.9 100.1 %all-gather.26.cloned.1.call-start = ((), (), s32[]{:S(2)}) async-start(), calls=%async_computation.7 | async-start | bytes 2359296 | tf_op jit(solution)/shard_map/all_gather | solution.py:187
  29.7 129.0 %all-gather.28.cloned.1.call-start = ((), (), s32[]{:S(2)}) async-start(), calls=%async_computation.8 | async-start | bytes 2359296 | tf_op jit(solution)/shard_map/all_gather | solution.py:188
  31.4 471.9 %all-gather.30.cloned.1.call-start = ((), (), s32[]{:S(2)}) async-start(), calls=%async_computation.9 | async-start | bytes 2359296 | tf_op jit(solution)/shard_map/all_gather | solution.py:189
  33.2 563.9 %reduce-scatter.6.cloned.1.call-start = ((), (), s32[]{:S(2)}) async-start(), calls=%async_computation.10 | async-start | bytes 10485760 | tf_op jit(solution)/shard_map/reduce_scatter | solution.py:200
  510.9 144.5 %all-gather.34.cloned.1.call-start = ((), (), s32[]{:S(2)}) async-start(), calls=%async_computation.12 | async-start | bytes 5898240 | tf_op jit(solution)/shard_map/all_gather | solution.py:190
  511.9 197.6 %all-gather.32.cloned.1.call-start = ((), (), s32[]{:S(2)}) async-start(), calls=%async_computation.11 | async-start | bytes 5242880 | tf_op jit(solution)/shard_map/all_gather | solution.py:197
  522.4 563.1 %copy-start.28 = (f32[8,1,256]{2,1,0:T(1,128)}, f32[8,1,256]{2,1,0:T(1,128)S(1)}, u32[]{:S(2)}) copy-start(f32[8,1,256]{2,1,0:T(1,128)S(1)} %convert_element_type.185) | copy-start | bytes 24580
  601.5 166.4 %all-gather.36.cloned.1.call-start = ((), (), s32[]{:S(2)}) async-start(), calls=%async_computation.13 | async-start | bytes 5898240 | tf_op jit(solution)/shard_map/all_gather | solution.py:191
  603.5 217.7 %all-gather.56.cloned.1.call-start = ((), (), s32[]{:S(2)}) async-start(), calls=%async_computation.27 | async-start | bytes 5242880 | tf_op jit(solution)/shard_map/all_gather | solution.py:197
  604.1 275.5 %all-gather.38.cloned.1.call-start = ((), (), s32[]{:S(2)}) async-start(), calls=%async_computation.14 | async-start | bytes 5898240 | tf_op jit(solution)/shard_map/all_gather | solution.py:192
  606.1 385.1 %reduce-scatter.8.cloned.1.call-start = ((), (), s32[]{:S(2)}) async-start(), calls=%async_computation.15 | async-start | bytes 10485760 | tf_op jit(solution)/shard_map/reduce_scatter | solution.py:200
  905.9 174.8 %reduce-scatter.10.cloned.1.call-start = ((), (), s32[]{:S(2)}) async-start(), calls=%async_computation.16 | async-start | bytes 10485760 | tf_op jit(solution)/shard_map/reduce_scatter | solution.py:200
  925.0 216.2 %all-gather.40.cloned.1.call-start = ((), (), s32[]{:S(2)}) async-start(), calls=%async_computation.17 | async-start | bytes 5242880 | tf_op jit(solution)/shard_map/all_gather | solution.py:197
  1088.4 1048.7 %reduce-scatter.14.cloned.1.call-start = ((), (), s32[]{:S(2)}) async-start(), calls=%async_computation.19 | async-start | bytes 27131904 | tf_op jit(solution)/shard_map/reduce_scatter | solution.py:293
  1899.6 325.5 %reduce-scatter.12.cloned.1.call-start = ((), (), s32[]{:S(2)}) async-start(), calls=%async_computation.18 | async-start | bytes 10485760 | tf_op jit(solution)/shard_map/reduce_scatter | solution.py:200
  1912.4 364.0 %all-gather.42.cloned.1.call-start = ((), (), s32[]{:S(2)}) async-start(), calls=%async_computation.20 | async-start | bytes 1310720 | tf_op jit(solution)/shard_map/all_gather | solution.py:316
  2139.3 143.5 %all-gather.44.cloned.1.call-start = ((), (), s32[]{:S(2)}) async-start(), calls=%async_computation.21 | async-start | bytes 1310720 | tf_op jit(solution)/shard_map/all_gather | solution.py:319
  2139.9 172.0 %all-gather.46.cloned.1.call-start = ((), (), s32[]{:S(2)}) async-start(), calls=%async_computation.22 | async-start | bytes 1310720 | tf_op jit(solution)/shard_map/all_gather | solution.py:322
  2140.6 200.1 %all-gather.48.cloned.1.call-start = ((), (), s32[]{:S(2)}) async-start(), calls=%async_computation.23 | async-start | bytes 1310720 | tf_op jit(solution)/shard_map/all_gather | solution.py:325
  2141.2 241.6 %all-gather.50.cloned.1.call-start = ((), (), s32[]{:S(2)}) async-start(), calls=%async_computation.24 | async-start | bytes 3276800 | tf_op jit(solution)/shard_map/all_gather | solution.py:328
  2144.2 280.7 %all-gather.52.cloned.1.call-start = ((), (), s32[]{:S(2)}) async-start(), calls=%async_computation.25 | async-start | bytes 3276800 | tf_op jit(solution)/shard_map/all_gather | solution.py:331
  2145.0 322.0 %all-gather.54.cloned.1.call-start = ((), (), s32[]{:S(2)}) async-start(), calls=%async_computation.26 | async-start | bytes 3276800 | tf_op jit(solution)/shard_map/all_gather | solution.py:334
  (80 other events, 4287.9 us)
Sparse Core Ops, SparseCore 0:
  10.2 31.7 all-gather.23
  44.5 52.1 all-gather.21
  98.9 29.0 all-gather.25
  130.0 28.5 all-gather.27
  160.7 28.5 all-gather.29
  511.1 85.9 reduce-scatter.5
  599.4 56.0 all-gather.33
  658.0 51.4 all-gather.31
  711.8 56.0 all-gather.35
  769.7 51.4 all-gather.55
  823.5 56.0 all-gather.37
  906.0 85.1 reduce-scatter.7
  994.3 86.3 reduce-scatter.9
  1088.5 52.6 all-gather.39
  1899.7 237.2 reduce-scatter.13
  2140.3 84.7 reduce-scatter.11
  2227.4 26.7 all-gather.41
  2255.8 26.8 all-gather.43
  2285.2 26.6 all-gather.45
  2314.1 26.6 all-gather.47
  2343.2 39.6 all-gather.49
  2385.3 39.6 all-gather.51
  2427.3 39.6 all-gather.53
where the time goes:
time: 2490 us; the launch traced here: 2480 us
  waiting for transfers between devices  1120 us (45%)
  local copies, waits for them, and re-layouts  862 us (35%)
  matrix products  299 us (12%)
  other arithmetic  103 us (4%)
  blocking collectives  64 us (3%)
    while x88, local copies, waits for them, and re-layouts  323 us
    reduce_scatter x4, waiting for transfers between devices, token_sum(): lax.psum_scatter(term(jnp.int32(0), lax.axis_size('seq') * token_rows), '...  306 us
    reduce_scatter x1, waiting for transfers between devices, on_device(): lax.psum_scatter(jnp.concatenate([rows_dot(attn_rows, query_back), rows_d...  225 us
    all_gather x4, waiting for transfers between devices, whole_row(): return lax.all_gather(piece, 'seq', axis=0, tiled=True)  204 us
    another operation x8, local copies, waits for them, and re-layouts, toeplitz_bias(): tiled = jnp.tile(turned, (1, block_rows))[:, :block_rows * (width - 1)]  142 us
    reshape x4, local copies, waits for them, and re-layouts, toeplitz_bias(): tiled.reshape(relative.shape[0], block_rows, width - 1)[:, :, :row_length]  96.8 us
    reshape x2, local copies, waits for them, and re-layouts, offset_sums(): folded = jnp.sum(flat.reshape(head_count, block_rows, width), axis=1)  79 us
    slice x4, local copies, waits for them, and re-layouts, toeplitz_bias(): tiled = jnp.tile(turned, (1, block_rows))[:, :block_rows * (width - 1)]  68.4 us
  transfers between devices with their start and end apart: 23, of which 21 were waited for; matrix products, arithmetic and copies ran while one was open for 19% of the time, Pallas kernels for 0%

commit v1 on v0

--- a/solution.py
+++ b/solution.py
@@ -1,6 +1,10 @@
+import functools
+
 import jax
 import jax.numpy as jnp
 from jax import lax
+from jax.experimental import pallas as pl
+from jax.experimental.pallas import tpu as pltpu
 from jax.sharding import PartitionSpec as P
 
 DH = 64
@@ -9,6 +13,9 @@
 EPSILON = 1e-06
 PRECISE = lax.Precision.HIGHEST
 MASKED_SCORE = -1e30
+TILE = 128
+PAIR = 2 * DH
+VMEM_BYTES = 56 * 1024 * 1024
 
 
 def rows_dot(left, right):
@@ -31,109 +38,134 @@
     return jax.nn.gelu(gate, approximate=True) * up_proj
 
 
-def toeplitz_bias(relative, first_row, block_rows, row_length):
-    width = row_length + block_rows - 1
-    begin = row_length - first_row - block_rows
-    window = lax.dynamic_slice_in_dim(relative, begin, width, 1)
-    turned = jnp.concatenate([window[:, block_rows - 1 :], window[:, : block_rows - 1]], axis=1)
-    tiled = jnp.tile(turned, (1, block_rows))[:, : block_rows * (width - 1)]
-    return tiled.reshape(relative.shape[0], block_rows, width - 1)[:, :, :row_length]
-
-
-def offset_sums(score_grad, block_rows, row_length):
-    head_count = score_grad.shape[0]
-    width = row_length + block_rows - 1
-    padded = jnp.pad(score_grad, ((0, 0), (0, 0), (0, width - 1 - row_length)))
-    flat = jnp.pad(padded.reshape(head_count, block_rows * (width - 1)), ((0, 0), (0, block_rows)))
-    folded = jnp.sum(flat.reshape(head_count, block_rows, width), axis=1)
-    return jnp.concatenate([folded[:, row_length:], folded[:, :row_length]], axis=1)
-
-
-def block_scores(query_block, key_rows, segment_block, segment_row, first_row, relative):
-    row_length = segment_row.shape[0]
-    block_rows = query_block.shape[0]
-    scores = jnp.einsum(
-        "qhd,khd->hqk", query_block, key_rows, preferred_element_type=jnp.float32
-    ) + toeplitz_bias(relative, first_row, block_rows, row_length)
-    allowed = segment_block[:, None] == segment_row[None, :]
-    return jnp.where(allowed[None, :, :], scores, MASKED_SCORE)
-
-
-def attention_forward(query_rows, key_rows, value_rows, segment_row, relative, block_rows):
-    blocks = query_rows.shape[0] // block_rows
-
-    def one_block(block_index):
-        first_row = block_index * block_rows
-        query_block = lax.dynamic_slice_in_dim(query_rows, first_row, block_rows, 0)
-        segment_block = lax.dynamic_slice_in_dim(segment_row, first_row, block_rows, 0)
-        scores = block_scores(
-            query_block, key_rows, segment_block, segment_row, first_row, relative
-        )
-        highest = jnp.max(scores, axis=-1, keepdims=True)
-        exponent = jnp.exp(scores - highest)
-        totals = jnp.sum(exponent, axis=-1, keepdims=True)
-        attention = (exponent / totals).astype(jnp.bfloat16)
-        context = jnp.einsum(
-            "hqk,khd->qhd", attention, value_rows, preferred_element_type=jnp.float32
-        )
-        return (context.astype(jnp.bfloat16), (highest + jnp.log(totals))[:, :, 0])
-
-    return lax.map(one_block, jnp.arange(blocks, dtype=jnp.int32))
-
-
-def attention_backward(
-    query_rows, key_rows, value_rows, segment_row, relative, log_total, context_grad, block_rows
-):
-    row_length, head_count, head_size = query_rows.shape
-    blocks = row_length // block_rows
-    width = row_length + block_rows - 1
-
-    def one_block(carry, pieces):
-        key_grad, value_grad, relative_grad = carry
-        block_index, block_total = pieces
-        first_row = block_index * block_rows
-        query_block = lax.dynamic_slice_in_dim(query_rows, first_row, block_rows, 0)
-        segment_block = lax.dynamic_slice_in_dim(segment_row, first_row, block_rows, 0)
-        grad_block = lax.dynamic_slice_in_dim(context_grad, first_row, block_rows, 0)
-        scores = block_scores(
-            query_block, key_rows, segment_block, segment_row, first_row, relative
-        )
-        attention = jnp.exp(scores - block_total[:, :, None])
-        attention_grad = jnp.einsum(
-            "qhd,khd->hqk", grad_block, value_rows, preferred_element_type=jnp.float32
-        )
-        centre = jnp.sum(attention * attention_grad, axis=-1, keepdims=True)
-        score_grad = attention * (attention_grad - centre)
-        begin = row_length - first_row - block_rows
-        current = lax.dynamic_slice_in_dim(relative_grad, begin, width, 1)
-        relative_grad = lax.dynamic_update_slice_in_dim(
-            relative_grad, current + offset_sums(score_grad, block_rows, row_length), begin, 1
-        )
-        score_low = score_grad.astype(jnp.bfloat16)
-        attention_low = attention.astype(jnp.bfloat16)
-        query_grad = jnp.einsum(
-            "hqk,khd->qhd", score_low, key_rows, preferred_element_type=jnp.float32
-        )
-        key_grad = key_grad + jnp.einsum(
-            "hqk,qhd->khd", score_low, query_block, preferred_element_type=jnp.float32
-        )
-        value_grad = value_grad + jnp.einsum(
-            "hqk,qhd->khd", attention_low, grad_block, preferred_element_type=jnp.float32
-        )
-        return ((key_grad, value_grad, relative_grad), query_grad)
-
-    zero_rows = jnp.zeros((row_length, head_count, head_size), jnp.float32)
-    start_carry = (zero_rows, zero_rows, jnp.zeros((head_count, 2 * row_length - 1), jnp.float32))
-    carried, query_grad = lax.scan(
-        one_block, start_carry, (jnp.arange(blocks, dtype=jnp.int32), log_total)
-    )
-    key_grad, value_grad, relative_grad = carried
-    return (
-        query_grad.reshape(row_length, -1),
-        key_grad.reshape(row_length, -1),
-        value_grad.reshape(row_length, -1),
-        relative_grad,
-    )
+def half_lanes(shape, which):
+    lane = lax.broadcasted_iota(jnp.int32, shape, 1)
+    return (lane < DH) if which == 0 else (lane >= DH)
+
+def fold_rows(tile):
+    return jnp.sum(tile.reshape(tile.shape[0] // 8, 8, tile.shape[1]), axis=0)
+
+def forward_kernel(block, q_ref, k_ref, v_ref, row_ref, col_ref, bias_ref, ctx_ref, e_ref, inv_ref, strip_ref, score_ref):
+    length = q_ref.shape[0]
+    tiles = length // TILE
+    width = 2 * length
+    reach = length - TILE
+    values_t = jnp.transpose(v_ref[...])
+    for head in range(2):
+        wide = jnp.broadcast_to(bias_ref[0, head : head + 1, :], (TILE, width))
+        strip_ref[head] = pltpu.roll(wide, width - (TILE - 1), 1, stride=1, stride_axis=0)
+    def one_block(index, carry):
+        first = pl.multiple_of(index * block, block)
+        q_block = q_ref[pl.ds(first, block), :]
+        segment_q = row_ref[:, pl.ds(first, block)]
+        outs = []
+        for head in range(2):
+            q_head = jnp.where(half_lanes(q_block.shape, head), q_block, jnp.zeros_like(q_block))
+            raw = cols_dot(k_ref[...], q_head)
+            highest = jnp.full((8, block), -jnp.inf, jnp.float32)
+            for tile in range(tiles):
+                bias = strip_ref[head, :, pl.ds(pl.multiple_of(first + (reach - TILE * tile), TILE), block)]
+                segment_k = jnp.concatenate([col_ref[tile * TILE : (tile + 1) * TILE, :]] * (block // TILE), axis=1)
+                score = jnp.where(segment_k == segment_q, raw[tile * TILE : (tile + 1) * TILE, :] + bias, MASKED_SCORE)
+                score_ref[tile * TILE : (tile + 1) * TILE, :] = score
+                highest = jnp.maximum(highest, jnp.max(score.reshape(TILE // 8, 8, block), axis=0))
+            top = jnp.max(highest, axis=0, keepdims=True)
+            total = jnp.zeros((8, block), jnp.float32)
+            for tile in range(tiles):
+                exponent = jnp.exp(score_ref[tile * TILE : (tile + 1) * TILE, :] - top)
+                total = total + fold_rows(exponent)
+                e_ref[head, tile * TILE : (tile + 1) * TILE, pl.ds(first, block)] = exponent.astype(jnp.bfloat16)
+            inverse = 1.0 / jnp.sum(total, axis=0, keepdims=True)
+            inv_ref[head, :, pl.ds(first, block)] = inverse
+            context = jnp.dot(values_t[head * DH : (head + 1) * DH, :], e_ref[head, :, pl.ds(first, block)], preferred_element_type=jnp.float32)
+            outs.append(context * inverse)
+        ctx_ref[pl.ds(first, block), :] = jnp.transpose(jnp.concatenate(outs, axis=0)).astype(jnp.bfloat16)
+        return carry
+    lax.fori_loop(0, length // block, one_block, 0)
+
+def attention_forward(q, k, v, segment_row, segment_wide, bias_line, heads, block):
+    length = q.shape[0]
+    pair = pl.BlockSpec((length, PAIR), lambda i: (0, i))
+    return pl.pallas_call(
+        functools.partial(forward_kernel, block),
+        grid=(heads // 2,),
+        in_specs=[pair, pair, pair,
+                  pl.BlockSpec((1, length), lambda i: (0, 0)),
+                  pl.BlockSpec((length, TILE), lambda i: (0, 0)),
+                  pl.BlockSpec((1, 2, 2 * length), lambda i: (i, 0, 0))],
+        out_specs=[pair,
+                   pl.BlockSpec((2, length, length), lambda i: (i, 0, 0)),
+                   pl.BlockSpec((2, 1, length), lambda i: (i, 0, 0))],
+        out_shape=[jax.ShapeDtypeStruct((length, heads * DH), jnp.bfloat16),
+                   jax.ShapeDtypeStruct((heads, length, length), jnp.bfloat16),
+                   jax.ShapeDtypeStruct((heads, 1, length), jnp.float32)],
+        scratch_shapes=[pltpu.VMEM((2, TILE, 2 * length), jnp.float32), pltpu.VMEM((length, block), jnp.float32)],
+        compiler_params=pltpu.CompilerParams(vmem_limit_bytes=VMEM_BYTES),
+        name="attention_forward",
+    )(q, k, v, segment_row, segment_wide, bias_line)
+
+def backward_kernel(block, q_ref, k_ref, v_ref, d_ref, e_ref, inv_ref, dq_ref, dk_ref, dv_ref, line_ref, strip_ref, prob_ref, low_ref, dk_sum, dv_sum):
+    length = q_ref.shape[0]
+    tiles = length // TILE
+    width = 2 * length
+    reach = length - TILE
+    keys_t = jnp.transpose(k_ref[...])
+    strip_ref[...] = jnp.zeros_like(strip_ref)
+    dk_sum[...] = jnp.zeros_like(dk_sum)
+    dv_sum[...] = jnp.zeros_like(dv_sum)
+    def one_block(index, carry):
+        first = pl.multiple_of(index * block, block)
+        q_block = q_ref[pl.ds(first, block), :]
+        d_block = d_ref[pl.ds(first, block), :]
+        outs = []
+        for head in range(2):
+            mask = half_lanes(q_block.shape, head)
+            q_head = jnp.where(mask, q_block, jnp.zeros_like(q_block))
+            d_head = jnp.where(mask, d_block, jnp.zeros_like(d_block))
+            prob_ref[...] = cols_dot(v_ref[...], d_head)
+            total = jnp.zeros((8, block), jnp.float32)
+            for tile in range(tiles):
+                rows = slice(tile * TILE, (tile + 1) * TILE)
+                total = total + fold_rows(e_ref[head, rows, pl.ds(first, block)].astype(jnp.float32) * prob_ref[rows, :])
+            centre = jnp.sum(total, axis=0, keepdims=True) * inv_ref[head, :, pl.ds(first, block)]
+            for tile in range(tiles):
+                rows = slice(tile * TILE, (tile + 1) * TILE)
+                grad = e_ref[head, rows, pl.ds(first, block)].astype(jnp.float32) * (prob_ref[rows, :] - centre)
+                place = pl.ds(pl.multiple_of(first + (reach - TILE * tile), TILE), block)
+                strip_ref[head, :, place] = strip_ref[head, :, place] + grad
+                low_ref[rows, :] = grad.astype(jnp.bfloat16)
+            dk_sum[...] += jnp.dot(low_ref[...], q_head, preferred_element_type=jnp.float32)
+            dv_sum[...] += jnp.dot(e_ref[head, :, pl.ds(first, block)], d_head, preferred_element_type=jnp.float32)
+            outs.append(jnp.dot(keys_t[head * DH : (head + 1) * DH, :], low_ref[...], preferred_element_type=jnp.float32))
+        dq_ref[pl.ds(first, block), :] = jnp.transpose(jnp.concatenate(outs, axis=0)).astype(jnp.bfloat16)
+        return carry
+    lax.fori_loop(0, length // block, one_block, 0)
+    dk_ref[...] = dk_sum[...].astype(jnp.bfloat16)
+    dv_ref[...] = dv_sum[...].astype(jnp.bfloat16)
+    for head in range(2):
+        turned = strip_ref[head]
+        while turned.shape[0] > 1:
+            half = turned.shape[0] // 2
+            turned = pltpu.roll(turned[:half], half, 1) + turned[half:]
+        line_ref[0, head : head + 1, :] = turned
+
+def attention_backward(q, k, v, d, e, inv, heads, block):
+    length = q.shape[0]
+    pair = pl.BlockSpec((length, PAIR), lambda i: (0, i))
+    rows = jax.ShapeDtypeStruct((length, heads * DH), jnp.bfloat16)
+    return pl.pallas_call(
+        functools.partial(backward_kernel, block),
+        grid=(heads // 2,),
+        in_specs=[pair, pair, pair, pair,
+                  pl.BlockSpec((2, length, length), lambda i: (i, 0, 0)),
+                  pl.BlockSpec((2, 1, length), lambda i: (i, 0, 0))],
+        out_specs=[pair, pair, pair, pl.BlockSpec((1, 2, 2 * length), lambda i: (i, 0, 0))],
+        out_shape=[rows, rows, rows, jax.ShapeDtypeStruct((heads // 2, 2, 2 * length), jnp.float32)],
+        scratch_shapes=[pltpu.VMEM((2, TILE, 2 * length), jnp.float32), pltpu.VMEM((length, block), jnp.float32),
+                        pltpu.VMEM((length, block), jnp.bfloat16), pltpu.VMEM((length, PAIR), jnp.float32), pltpu.VMEM((length, PAIR), jnp.float32)],
+        compiler_params=pltpu.CompilerParams(vmem_limit_bytes=VMEM_BYTES),
+        name="attention_backward",
+    )(q, k, v, d, e, inv)
 
 
 def on_device(
@@ -157,18 +189,20 @@
     ffn_width = w_gate.shape[1]
     segment_row = segments[0]
     row_length = segment_row.shape[0]
-    block_rows = min(512, row_length)
+    block = min(256, row_length)
     seq_count = lax.axis_size("seq")
     fsdp_count = lax.axis_size("fsdp")
     seq_place = lax.axis_index("seq")
     fsdp_place = lax.axis_index("fsdp")
     head_count = model_width // seq_count // DH
-    head_shape = (row_length, head_count, DH)
+    table_rows = jnp.pad(buckets[::-1], (0, 1), constant_values=-1)
     bucket_table = (
-        buckets[:, None] == jnp.arange(rel_table.shape[1], dtype=jnp.int32)[None, :]
+        table_rows[:, None] == jnp.arange(rel_table.shape[1], dtype=jnp.int32)[None, :]
     ).astype(jnp.float32)
     local_table = lax.dynamic_slice_in_dim(rel_table, seq_place * head_count, head_count, 0)
-    relative = jnp.dot(local_table, jnp.transpose(bucket_table), precision=PRECISE)
+    bias_line = jnp.dot(local_table, jnp.transpose(bucket_table), precision=PRECISE)
+    bias_line = bias_line.reshape(head_count // 2, 2, 2 * row_length)
+    segment_wide = jnp.broadcast_to(segment_row[:, None], (row_length, TILE))
     stream = tokens[0].astype(jnp.float32)
     scale_attn = lax.rsqrt(jnp.mean(stream * stream, axis=-1, keepdims=True) + EPSILON)
     normed_attn = stream * scale_attn
@@ -209,22 +243,18 @@
     query_rows = (
         jnp.dot(attn_rows, query_w, preferred_element_type=jnp.float32)
         .astype(jnp.bfloat16)
-        .reshape(head_shape)
     )
     key_rows = (
         jnp.dot(attn_rows, key_w, preferred_element_type=jnp.float32)
         .astype(jnp.bfloat16)
-        .reshape(head_shape)
     )
     value_rows = (
         jnp.dot(attn_rows, value_w, preferred_element_type=jnp.float32)
         .astype(jnp.bfloat16)
-        .reshape(head_shape)
-    )
-    context_heads, log_total = attention_forward(
-        query_rows, key_rows, value_rows, segment_row, relative, block_rows
-    )
-    context = context_heads.reshape(row_length, -1)
+    )
+    context, exponents, inverse = attention_forward(
+        query_rows, key_rows, value_rows, segments, segment_wide, bias_line, head_count, block
+    )
 
     def attn_term(first_row, row_count):
         return cols_dot(context, output_w)
@@ -261,22 +291,13 @@
     )
     attn_grad = resid_grad.astype(jnp.bfloat16)
     attn_grad_rows = whole_row(attn_grad)
-    context_grad = jnp.dot(attn_grad_rows, output_w, preferred_element_type=jnp.float32).astype(
-        jnp.bfloat16
-    )
-    query_grad, key_grad, value_grad, relative_grad = attention_backward(
-        query_rows,
-        key_rows,
-        value_rows,
-        segment_row,
-        relative,
-        log_total,
-        context_grad.reshape(head_shape),
-        block_rows,
-    )
-    query_back = query_grad.astype(jnp.bfloat16)
-    key_back = key_grad.astype(jnp.bfloat16)
-    value_back = value_grad.astype(jnp.bfloat16)
+    inverse_rows = jnp.repeat(jnp.transpose(inverse[:, 0, :]), DH, axis=1)
+    context_grad = (
+        jnp.dot(attn_grad_rows, output_w, preferred_element_type=jnp.float32) * inverse_rows
+    ).astype(jnp.bfloat16)
+    query_back, key_back, value_back, line_grad = attention_backward(
+        query_rows, key_rows, value_rows, context_grad, exponents, inverse, head_count, block
+    )
 
     def triple_term(first_row, row_count):
         return (
@@ -346,7 +367,9 @@
             jnp.sum(valid),
         ]
     )
-    table_part = jnp.dot(relative_grad, bucket_table, precision=PRECISE)
+    table_part = jnp.dot(
+        line_grad.reshape(head_count, 2 * row_length), bucket_table, precision=PRECISE
+    )
     full_table = lax.dynamic_update_slice_in_dim(
         jnp.zeros(rel_table.shape, jnp.float32), table_part, seq_place * head_count, 0
     )

time: 2490 us -> 1510 us (0.61)
  local copies, waits for them, and re-layouts: 862 us -> 53.4 us
  matrix products: 299 us -> 151 us
  other arithmetic: 103 us -> 26.5 us
  Pallas kernels: 0 us -> 75.7 us
    while x89 -> x0, local copies, waits for them, and re-layouts: 325 us -> none
    reshape x8 -> x3, local copies, waits for them, and re-layouts: 216 us -> 3.61 us  [the longest x1 2.88 us: on_device(): inverse_rows = jnp.repeat(jnp.transpose(inverse[:, 0, :]), DH, axis=1)]
    dot_general x15 -> x1, matrix products: 150 us -> 0.58 us  [on_device(): jnp.dot(line_grad.reshape(head_count, 2 * row_length), bucket_table, prec...]
    another operation x8 -> x0, local copies, waits for them, and re-layouts: 142 us -> none  [toeplitz_bias(): tiled = jnp.tile(turned, (1, block_rows))[:, :block_rows * (width - 1)]]
    pallas_call x0 -> x2, Pallas kernels: none -> 75.7 us  [the longest x1 40.6 us: attention_backward(): pl.pallas_call(functools.partial(backward_kernel, block), grid=(heads //...]
    slice x16 -> x0, local copies, waits for them, and re-layouts: 69 us -> none  [the longest x4 68.4 us: toeplitz_bias(): tiled = jnp.tile(turned, (1, block_rows))[:, :block_rows * (width - 1)]]
    pad x4 -> x1, local copies, waits for them, and re-layouts: 54.8 us -> 0.01 us  [on_device(): table_rows = jnp.pad(buckets[::-1], (0, 1), constant_values=-1)]
    mul x2 -> x0, other arithmetic: 36.1 us -> none  [one_block(): score_grad = attention * (attention_grad - centre)]
  transfers between devices with their start and end apart: 23 -> 23, of which waited for: 21 -> 21; matrix products, arithmetic and copies ran while one was open for 19% -> 9% of each run, Pallas kernels for 0% -> 2%
where the time goes in v1:
time: 1510 us; the launch traced here: 1500 us
  waiting for transfers between devices  1120 us (74%)
  matrix products  151 us (10%)
  Pallas kernels  75.7 us (5%)
  blocking collectives  63.6 us (4%)
  local copies, waits for them, and re-layouts  53.4 us (4%)
  other arithmetic  26.5 us (2%)
  between operations  15.5 us (1%)
    reduce_scatter x4, waiting for transfers between devices, token_sum(): lax.psum_scatter(term(jnp.int32(0), lax.axis_size('seq') * token_rows), '...  305 us
    reduce_scatter x1, waiting for transfers between devices, on_device(): lax.psum_scatter(jnp.concatenate([rows_dot(attn_rows, query_back), rows_d...  225 us
    all_gather x4, waiting for transfers between devices, whole_row(): return lax.all_gather(piece, 'seq', axis=0, tiled=True)  200 us
    all_gather x1, waiting for transfers between devices, on_device(): lax.all_gather(columns(w_down, unit_count), 'fsdp', axis=0, tiled=True)  58.4 us
    all_gather x1, waiting for transfers between devices, on_device(): lax.all_gather(columns(w_gate, unit_count), 'fsdp', axis=0, tiled=True)  49.3 us
    all_gather x1, waiting for transfers between devices, on_device(): lax.all_gather(columns(w_up, unit_count), 'fsdp', axis=0, tiled=True)  48 us
    dot_general x7, matrix products, cols_dot(): lax.dot_general(left, right, (((1,), (1,)), ((), ())), preferred_element_...  46.7 us
    pallas_call x1, Pallas kernels, attention_backward(): pl.pallas_call(functools.partial(backward_kernel, block), grid=(heads //...  40.6 us
  transfers between devices with their start and end apart: 23, of which 21 were waited for; matrix products, arithmetic and copies ran while one was open for 9% of the time, Pallas kernels for 2%

profile of v1, /device:TPU:0, one launch (start us, length us, event | category | flops | bytes accessed | tf_op | source)
XLA Modules:
  0.0 1504.5 jit_solution(9706766134992732266)
XLA Ops:
  9.8 13.4 all-gather.1
  42.0 54.6 %all-gather.22.cloned.1.call-done = bf16[1024,2048]{1,0:T(8,128)(2,1)} async-done(((bf16[256,2048]{1,0:T(8,128)(2,1)}), bf16[1024,2048]{1,0:T(8,128)(2,1)}) %all-gather.22.cloned.1.call-update) | async-done | bytes 4194320 | tf_op jit(solution)/shard_map/all_gather | solution.py:231
  102.9 25.1 %all-gather.26.cloned.1.call-done = bf16[2048,512]{1,0:T(8,128)(2,1)} async-done(((bf16[256,512]{1,0:T(8,128)(2,1)}), bf16[2048,512]{1,0:T(8,128)(2,1)}) %all-gather.26.cloned.1.call-update) | async-done | bytes 2097168 | tf_op jit(solution)/shard_map/all_gather | solution.py:221
  134.2 24.5 %all-gather.28.cloned.1.call-done = bf16[2048,512]{1,0:T(8,128)(2,1)} async-done(((bf16[256,512]{1,0:T(8,128)(2,1)}), bf16[2048,512]{1,0:T(8,128)(2,1)}) %all-gather.28.cloned.1.call-update) | async-done | bytes 2097168 | tf_op jit(solution)/shard_map/all_gather | solution.py:222
  165.8 35.2 %attention_forward.1 = (bf16[1024,512]{1,0:T(8,128)(2,1)}, bf16[8,1024,1024]{2,1,0:T(8,128)(2,1)}, f32[8,1,1024]{2,1,0:T(1,128)}) custom-call(bf16[1024,512]{1,0:T(8,128)(2,1)} %convolution_convert_fusion.9.q_ref, bf16[1024,512]{1,0:T(8,128)(2,1)} %convolution_convert_fusion.8.k_ref, bf16[1024,512]{1,0:T(8,128)(2,1)} %convolution_convert_fusion.7.v_ref, ...), custom_call_target="tpu_custom_call" | custom-call | tf_op jit(solution)/shard_map/attention_forward/pallas_call | solution.py:89
  220.0 74.7 %reduce-scatter.6.cloned.1.call-done = f32[256,2048]{1,0:T(8,128)} async-done(((f32[1024,2048]{1,0:T(8,128)}), f32[256,2048]{1,0:T(8,128)}) %reduce-scatter.6.cloned.1.call-update) | async-done | bytes 2097168 | tf_op jit(solution)/shard_map/reduce_scatter | solution.py:234
  303.7 49.3 %all-gather.34.cloned.1.call-done = bf16[2048,1280]{1,0:T(8,128)(2,1)} async-done(((bf16[256,1280]{1,0:T(8,128)(2,1)}), bf16[2048,1280]{1,0:T(8,128)(2,1)}) %all-gather.34.cloned.1.call-update) | async-done | bytes 5242896 | tf_op jit(solution)/shard_map/all_gather | solution.py:224
  353.0 54.1 %all-gather.32.cloned.1.call-done = bf16[1024,2048]{1,0:T(8,128)(2,1)} async-done(((bf16[256,2048]{1,0:T(8,128)(2,1)}), bf16[1024,2048]{1,0:T(8,128)(2,1)}) %all-gather.32.cloned.1.call-update) | async-done | bytes 4194320 | tf_op jit(solution)/shard_map/all_gather | solution.py:231
  417.5 48.0 %all-gather.36.cloned.1.call-done = bf16[2048,1280]{1,0:T(8,128)(2,1)} async-done(((bf16[256,1280]{1,0:T(8,128)(2,1)}), bf16[2048,1280]{1,0:T(8,128)(2,1)}) %all-gather.36.cloned.1.call-update) | async-done | bytes 5242896 | tf_op jit(solution)/shard_map/all_gather | solution.py:225
  475.9 43.0 %all-gather.56.cloned.1.call-done = bf16[1,1024,2048]{2,1,0:T(8,128)(2,1)} async-done(((bf16[1,256,2048]{2,1,0:T(8,128)(2,1)}), bf16[1,1024,2048]{2,1,0:T(8,128)(2,1)}) %all-gather.56.cloned.1.call-update) | async-done | bytes 4194320 | tf_op jit(solution)/shard_map/all_gather | solution.py:231
  518.8 58.4 %all-gather.38.cloned.1.call-done = bf16[2048,1280]{1,0:T(8,128)(2,1)} async-done(((bf16[256,1280]{1,0:T(8,128)(2,1)}), bf16[2048,1280]{1,0:T(8,128)(2,1)}) %all-gather.38.cloned.1.call-update) | async-done | bytes 5242896 | tf_op jit(solution)/shard_map/all_gather | solution.py:226
  577.2 16.9 %fusion.11 = (bf16[1024,1280]{1,0:T(8,128)(2,1)}, bf16[1024,1280]{1,0:T(8,128)(2,1)}, bf16[1024,1280]{1,0:T(8,128)(2,1)S(1)}) fusion(f32[1024,1280]{1,0:T(8,128)} %fusion.41, f32[1024,1280]{1,0:T(8,128)} %fusion.42, bf16[2048,1280]{1,0:T(8,128)(2,1)} %all-gather.38.cloned.1.call-done, bf16[1,1024,2048]{2,1,0:T(8,128)(2,1)} %all-gather.56.cloned.1.call-done), kind=kOutput, calls=%fused_computation.19 | convolution fusion | flops 5402787840 | bytes 27787264 | tf_op jit(solution)/shard_map/dot_general | solution.py:278
  622.9 65.9 %reduce-scatter.8.cloned.1.call-done = f32[256,2048]{1,0:T(8,128)} async-done(((f32[1024,2048]{1,0:T(8,128)}), f32[256,2048]{1,0:T(8,128)}) %reduce-scatter.8.cloned.1.call-update) | async-done | bytes 2097168 | tf_op jit(solution)/shard_map/reduce_scatter | solution.py:234
  688.8 89.5 %reduce-scatter.10.cloned.1.call-done = f32[256,2048]{1,0:T(8,128)} async-done(((f32[1024,2048]{1,0:T(8,128)}), f32[256,2048]{1,0:T(8,128)}) %reduce-scatter.10.cloned.1.call-update) | async-done | bytes 2097168 | tf_op jit(solution)/shard_map/reduce_scatter | solution.py:234
  789.3 48.3 %all-gather.40.cloned.1.call-done = bf16[1024,2048]{1,0:T(8,128)(2,1)} async-done(((bf16[256,2048]{1,0:T(8,128)(2,1)}), bf16[1024,2048]{1,0:T(8,128)(2,1)}) %all-gather.40.cloned.1.call-update) | async-done | bytes 4194320 | tf_op jit(solution)/shard_map/all_gather | solution.py:231
  844.3 40.6 %attention_backward.1 = (bf16[1024,512]{1,0:T(8,128)(2,1)}, bf16[1024,512]{1,0:T(8,128)(2,1)}, bf16[1024,512]{1,0:T(8,128)(2,1)}, f32[4,2,2048]{2,1,0:T(2,128)}) custom-call(bf16[1024,512]{1,0:T(8,128)(2,1)} %convolution_convert_fusion.9.q_ref, bf16[1024,512]{1,0:T(8,128)(2,1)} %convolution_convert_fusion.8.k_ref, ...), custom_call_target="tpu_custom_call" | custom-call | tf_op jit(solution)/shard_map/attention_backward/pallas_call | solution.py:156
  937.6 224.5 %reduce-scatter.14.cloned.1.call-done = bf16[256,5888]{0,1:T(8,128)(2,1)} async-done(((bf16[2048,5888]{0,1:T(8,128)(2,1)}), bf16[256,5888]{0,1:T(8,128)(2,1)}) %reduce-scatter.14.cloned.1.call-update) | async-done | bytes 3014672 | tf_op jit(solution)/shard_map/reduce_scatter | solution.py:314
  1175.3 74.9 %reduce-scatter.12.cloned.1.call-done = f32[256,2048]{1,0:T(8,128)} async-done(((f32[1024,2048]{1,0:T(8,128)}), f32[256,2048]{1,0:T(8,128)}) %reduce-scatter.12.cloned.1.call-update) | async-done | bytes 2097168 | tf_op jit(solution)/shard_map/reduce_scatter | solution.py:234
  1252.7 39.9 %all-reduce.1 = (f32[2048]{0:T(1024)S(1)}, f32[32,32]{1,0:T(8,128)S(1)}, f32[2048]{0:T(1024)S(1)}, f32[4]{0:T(128)S(1)}) all-reduce(f32[2048]{0:T(1024)S(1)} %get-tuple-element.68, f32[32,32]{1,0:T(8,128)S(1)} %convolution_dynamic-update-slice_fusion, ...), channel_id=1, replica_groups=mesh['fsdp'=8,'seq'=4] {'fsdp','seq'}, use_global_device_ids=true, to_apply=%region_10.11 | all-reduce | flops 5124 | bytes 40992 | tf_op jit(solution)/shard_map/psum | solution.py:376
  1310.9 26.5 %all-gather.46.cloned.1.call-done = bf16[256,2048]{0,1:T(8,128)(2,1)} async-done(((bf16[256,512]{0,1:T(8,128)(2,1)}), bf16[256,2048]{0,1:T(8,128)(2,1)}) %all-gather.46.cloned.1.call-update) | async-done | bytes 1048592 | tf_op jit(solution)/shard_map/all_gather | solution.py:343
  1340.0 26.4 %all-gather.48.cloned.1.call-done = bf16[256,2048]{0,1:T(8,128)(2,1)} async-done(((bf16[256,512]{0,1:T(8,128)(2,1)}), bf16[256,2048]{0,1:T(8,128)(2,1)}) %all-gather.48.cloned.1.call-update) | async-done | bytes 1048592 | tf_op jit(solution)/shard_map/all_gather | solution.py:346
  1368.9 39.5 %all-gather.50.cloned.1.call-done = bf16[256,5120]{0,1:T(8,128)(2,1)} async-done(((bf16[256,1280]{0,1:T(8,128)(2,1)}), bf16[256,5120]{0,1:T(8,128)(2,1)}) %all-gather.50.cloned.1.call-update) | async-done | bytes 2621456 | tf_op jit(solution)/shard_map/all_gather | solution.py:349
  1413.3 37.2 %all-gather.52.cloned.1.call-done = bf16[256,5120]{0,1:T(8,128)(2,1)} async-done(((bf16[256,1280]{0,1:T(8,128)(2,1)}), bf16[256,5120]{0,1:T(8,128)(2,1)}) %all-gather.52.cloned.1.call-update) | async-done | bytes 2621456 | tf_op jit(solution)/shard_map/all_gather | solution.py:352
  1455.6 37.1 %all-gather.54.cloned.1.call-done = bf16[256,5120]{0,1:T(8,128)(2,1)} async-done(((bf16[256,1280]{0,1:T(8,128)(2,1)}), bf16[256,5120]{0,1:T(8,128)(2,1)}) %all-gather.54.cloned.1.call-update) | async-done | bytes 2621456 | tf_op jit(solution)/shard_map/all_gather | solution.py:355
  (187 shorter events, 241.5 us)
Async XLA Ops:
  7.2 34.8 %all-gather.24.cloned.1.call-start = ((), (), s32[]{:S(2)}) async-start(), calls=%async_computation.6 | async-start | bytes 2359296 | tf_op jit(solution)/shard_map/all_gather | solution.py:220
  9.1 87.6 %all-gather.22.cloned.1.call-start = ((), (), s32[]{:S(2)}) async-start(), calls=%async_computation.5 | async-start | bytes 5242880 | tf_op jit(solution)/shard_map/all_gather | solution.py:231
  27.9 100.1 %all-gather.26.cloned.1.call-start = ((), (), s32[]{:S(2)}) async-start(), calls=%async_computation.7 | async-start | bytes 2359296 | tf_op jit(solution)/shard_map/all_gather | solution.py:221
  29.6 129.0 %all-gather.28.cloned.1.call-start = ((), (), s32[]{:S(2)}) async-start(), calls=%async_computation.8 | async-start | bytes 2359296 | tf_op jit(solution)/shard_map/all_gather | solution.py:222
  31.4 169.6 %all-gather.30.cloned.1.call-start = ((), (), s32[]{:S(2)}) async-start(), calls=%async_computation.9 | async-start | bytes 2359296 | tf_op jit(solution)/shard_map/all_gather | solution.py:223
  33.1 261.5 %reduce-scatter.6.cloned.1.call-start = ((), (), s32[]{:S(2)}) async-start(), calls=%async_computation.10 | async-start | bytes 10485760 | tf_op jit(solution)/shard_map/reduce_scatter | solution.py:234
  208.6 144.4 %all-gather.34.cloned.1.call-start = ((), (), s32[]{:S(2)}) async-start(), calls=%async_computation.12 | async-start | bytes 5898240 | tf_op jit(solution)/shard_map/all_gather | solution.py:224
  209.6 197.5 %all-gather.32.cloned.1.call-start = ((), (), s32[]{:S(2)}) async-start(), calls=%async_computation.11 | async-start | bytes 5242880 | tf_op jit(solution)/shard_map/all_gather | solution.py:231
  298.8 166.7 %all-gather.36.cloned.1.call-start = ((), (), s32[]{:S(2)}) async-start(), calls=%async_computation.13 | async-start | bytes 5898240 | tf_op jit(solution)/shard_map/all_gather | solution.py:225
  300.8 218.0 %all-gather.56.cloned.1.call-start = ((), (), s32[]{:S(2)}) async-start(), calls=%async_computation.27 | async-start | bytes 5242880 | tf_op jit(solution)/shard_map/all_gather | solution.py:231
  301.4 275.8 %all-gather.38.cloned.1.call-start = ((), (), s32[]{:S(2)}) async-start(), calls=%async_computation.14 | async-start | bytes 5898240 | tf_op jit(solution)/shard_map/all_gather | solution.py:226
  303.5 385.3 %reduce-scatter.8.cloned.1.call-start = ((), (), s32[]{:S(2)}) async-start(), calls=%async_computation.15 | async-start | bytes 10485760 | tf_op jit(solution)/shard_map/reduce_scatter | solution.py:234
  603.5 174.8 %reduce-scatter.10.cloned.1.call-start = ((), (), s32[]{:S(2)}) async-start(), calls=%async_computation.16 | async-start | bytes 10485760 | tf_op jit(solution)/shard_map/reduce_scatter | solution.py:234
  622.9 214.7 %all-gather.40.cloned.1.call-start = ((), (), s32[]{:S(2)}) async-start(), calls=%async_computation.17 | async-start | bytes 5242880 | tf_op jit(solution)/shard_map/all_gather | solution.py:231
  784.7 377.4 %reduce-scatter.14.cloned.1.call-start = ((), (), s32[]{:S(2)}) async-start(), calls=%async_computation.19 | async-start | bytes 27131904 | tf_op jit(solution)/shard_map/reduce_scatter | solution.py:314
  924.7 325.5 %reduce-scatter.12.cloned.1.call-start = ((), (), s32[]{:S(2)}) async-start(), calls=%async_computation.18 | async-start | bytes 10485760 | tf_op jit(solution)/shard_map/reduce_scatter | solution.py:234
  937.6 237.1 %copy-start.15 = (s32[2048]{0:T(1024)S(1)}, s32[2048]{0:T(1024)}, u32[]{:S(2)}) copy-start(s32[2048]{0:T(1024)} %copy-done.14) | copy-start | bytes 24580
  937.6 363.6 %all-gather.42.cloned.1.call-start = ((), (), s32[]{:S(2)}) async-start(), calls=%async_computation.20 | async-start | bytes 1310720 | tf_op jit(solution)/shard_map/all_gather | solution.py:337
  1164.3 144.0 %all-gather.44.cloned.1.call-start = ((), (), s32[]{:S(2)}) async-start(), calls=%async_computation.21 | async-start | bytes 1310720 | tf_op jit(solution)/shard_map/all_gather | solution.py:340
  1164.9 172.5 %all-gather.46.cloned.1.call-start = ((), (), s32[]{:S(2)}) async-start(), calls=%async_computation.22 | async-start | bytes 1310720 | tf_op jit(solution)/shard_map/all_gather | solution.py:343
  1165.7 200.7 %all-gather.48.cloned.1.call-start = ((), (), s32[]{:S(2)}) async-start(), calls=%async_computation.23 | async-start | bytes 1310720 | tf_op jit(solution)/shard_map/all_gather | solution.py:346
  1166.3 242.2 %all-gather.50.cloned.1.call-start = ((), (), s32[]{:S(2)}) async-start(), calls=%async_computation.24 | async-start | bytes 3276800 | tf_op jit(solution)/shard_map/all_gather | solution.py:349
  1169.1 281.4 %all-gather.52.cloned.1.call-start = ((), (), s32[]{:S(2)}) async-start(), calls=%async_computation.25 | async-start | bytes 3276800 | tf_op jit(solution)/shard_map/all_gather | solution.py:352
  1169.9 322.8 %all-gather.54.cloned.1.call-start = ((), (), s32[]{:S(2)}) async-start(), calls=%async_computation.26 | async-start | bytes 3276800 | tf_op jit(solution)/shard_map/all_gather | solution.py:355
  (31 other events, 1157.3 us)
Sparse Core Ops, SparseCore 0:
  10.2 31.7 all-gather.23
  44.5 52.1 all-gather.21
  98.9 29.0 all-gather.25
  130.0 28.5 all-gather.27
  160.7 28.5 all-gather.29
  208.8 85.8 reduce-scatter.5
  297.0 56.0 all-gather.33
  355.6 51.4 all-gather.31
  409.4 56.0 all-gather.35
  467.3 51.4 all-gather.55
  521.2 56.0 all-gather.37
  603.6 85.1 reduce-scatter.7
  691.9 86.3 reduce-scatter.9
  784.9 52.6 all-gather.39
  924.8 237.2 reduce-scatter.13
  1165.4 84.7 reduce-scatter.11
  1252.4 26.7 all-gather.41
  1281.5 26.8 all-gather.43
  1310.8 26.6 all-gather.45
  1339.7 26.6 all-gather.47
  1368.8 39.6 all-gather.49
  1410.9 39.6 all-gather.51
  1453.0 39.6 all-gather.53

commit v2 on v1

v2 whole, which is shorter than its diff:
```python
import functools

import jax
import jax.numpy as jnp
from jax import lax
from jax.experimental import pallas as pl
from jax.experimental.pallas import tpu as pltpu
from jax.sharding import PartitionSpec as P

DH = 64


EPSILON = 1e-06
PRECISE = lax.Precision.HIGHEST
MASKED_SCORE = -1e30
TILE = 128
PAIR = 2 * DH
GELU_SCALE = 0.7978845608
GELU_CUBE = 0.044715
VMEM_BYTES = 56 * 1024 * 1024


def rows_dot(left, right):
    return lax.dot_general(
        left, right, (((0,), (0,)), ((), ())), preferred_element_type=jnp.float32
    )


def cols_dot(left, right):
    return lax.dot_general(
        left, right, (((1,), (1,)), ((), ())), preferred_element_type=jnp.float32
    )


def norm_back(grad_hat, normed, scale):
    return scale * (grad_hat - normed * jnp.mean(grad_hat * normed, axis=-1, keepdims=True))


def half_lanes(shape, which):
    lane = lax.broadcasted_iota(jnp.int32, shape, 1)
    return (lane < DH) if which == 0 else (lane >= DH)


def fold_rows(tile):
    return jnp.sum(tile.reshape(tile.shape[0] // 8, 8, tile.shape[1]), axis=0)


def whole_place(row, token_rows, place):
    return jnp.bitwise_xor(row // token_rows, place) * token_rows + row % token_rows


def forward_kernel(
    block,
    token_rows,
    place_ref,
    qkv_ref,
    row_ref,
    col_ref,
    bias_ref,
    ctx_ref,
    e_ref,
    inv_ref,
    strip_ref,
    score_ref,
):
    length = qkv_ref.shape[0]
    q_ref = qkv_ref.at[:, :PAIR]
    k_ref = qkv_ref.at[:, PAIR : 2 * PAIR]
    v_ref = qkv_ref.at[:, 2 * PAIR :]
    tiles = length // TILE
    width = 2 * length
    reach = length - TILE
    place = place_ref[0]
    key_places = [
        pl.multiple_of(whole_place(tile * TILE, token_rows, place), TILE) for tile in range(tiles)
    ]
    values_t = jnp.transpose(v_ref[...])
    for head in range(2):
        wide = jnp.broadcast_to(bias_ref[0, head : head + 1, :], (TILE, width))
        strip_ref[head] = pltpu.roll(wide, width - (TILE - 1), 1, stride=1, stride_axis=0)

    def one_block(index, carry):
        first = pl.multiple_of(index * block, block)
        query_place = pl.multiple_of(whole_place(first, token_rows, place), block)
        q_block = q_ref[pl.ds(first, block), :]
        segment_q = row_ref[:, pl.ds(query_place, block)]
        outs = []
        for head in range(2):
            q_head = jnp.where(half_lanes(q_block.shape, head), q_block, jnp.zeros_like(q_block))
            raw = cols_dot(k_ref[...], q_head)
            highest = jnp.full((8, block), -jnp.inf, jnp.float32)
            for tile in range(tiles):
                rows = slice(tile * TILE, (tile + 1) * TILE)
                offset = pl.multiple_of(query_place + (reach - key_places[tile]), TILE)
                bias = strip_ref[head, :, pl.ds(offset, block)]
                segment_k = col_ref[pl.ds(key_places[tile], TILE), :]
                segment_k = jnp.concatenate([segment_k] * (block // TILE), axis=1)
                score = jnp.where(segment_k == segment_q, raw[rows, :] + bias, MASKED_SCORE)
                score_ref[rows, :] = score
                highest = jnp.maximum(
                    highest, jnp.max(score.reshape(TILE // 8, 8, block), axis=0)
                )
            top = jnp.max(highest, axis=0, keepdims=True)
            total = jnp.zeros((8, block), jnp.float32)
            for tile in range(tiles):
                rows = slice(tile * TILE, (tile + 1) * TILE)
                exponent = jnp.exp(score_ref[rows, :] - top)
                total = total + fold_rows(exponent)
                e_ref[head, rows, pl.ds(first, block)] = exponent.astype(jnp.bfloat16)
            inverse = 1.0 / jnp.sum(total, axis=0, keepdims=True)
            inv_ref[head, :, pl.ds(first, block)] = inverse
            context = jnp.dot(
                values_t[head * DH : (head + 1) * DH, :],
                e_ref[head, :, pl.ds(first, block)],
                preferred_element_type=jnp.float32,
            )
            outs.append(context * inverse)
        ctx_ref[pl.ds(first, block), :] = jnp.transpose(jnp.concatenate(outs, axis=0)).astype(
            jnp.bfloat16
        )
        return carry

    lax.fori_loop(0, length // block, one_block, 0)


def attention_forward(qkv, place, segment_row, segment_wide, bias_line, heads, token_rows):
    length = qkv.shape[0]
    block = min(256, token_rows)
    pairs = heads // 2
    return pl.pallas_call(
        functools.partial(forward_kernel, block, token_rows),
        grid=(pairs,),
        in_specs=[
            pl.BlockSpec(memory_space=pltpu.SMEM),
            pl.BlockSpec((length, 3 * PAIR), lambda i: (0, i)),
            pl.BlockSpec((1, length), lambda i: (0, 0)),
            pl.BlockSpec((length, TILE), lambda i: (0, 0)),
            pl.BlockSpec((1, 2, 2 * length), lambda i: (i, 0, 0)),
        ],
        out_specs=[
            pl.BlockSpec((length, PAIR), lambda i: (0, i)),
            pl.BlockSpec((2, length, length), lambda i: (i, 0, 0)),
            pl.BlockSpec((2, 1, length), lambda i: (i, 0, 0)),
        ],
        out_shape=[
            jax.ShapeDtypeStruct((length, heads * DH), jnp.bfloat16),
            jax.ShapeDtypeStruct((heads, length, length), jnp.bfloat16),
            jax.ShapeDtypeStruct((heads, 1, length), jnp.float32),
        ],
        scratch_shapes=[
            pltpu.VMEM((2, TILE, 2 * length), jnp.float32),
            pltpu.VMEM((length, block), jnp.float32),
        ],
        compiler_params=pltpu.CompilerParams(vmem_limit_bytes=VMEM_BYTES),
        cost_estimate=pl.CostEstimate(
            flops=16 * heads * length * length * DH,
            bytes_accessed=2 * heads * length * length,
            transcendentals=heads * length * length,
        ),
        name="attention_forward",
    )(place, qkv, segment_row, segment_wide, bias_line)


def backward_kernel(
    block,
    token_rows,
    place_ref,
    qkv_ref,
    d_ref,
    e_ref,
    inv_ref,
    grad_ref,
    line_ref,
    strip_ref,
    prob_ref,
    low_ref,
    dk_sum,
    dv_sum,
):
    length = qkv_ref.shape[0]
    q_ref = qkv_ref.at[:, :PAIR]
    k_ref = qkv_ref.at[:, PAIR : 2 * PAIR]
    v_ref = qkv_ref.at[:, 2 * PAIR :]
    tiles = length // TILE
    reach = length - TILE
    place = place_ref[0]
    key_places = [whole_place(tile * TILE, token_rows, place) for tile in range(tiles)]
    keys_t = jnp.transpose(k_ref[...])
    strip_ref[...] = jnp.zeros_like(strip_ref)
    dk_sum[...] = jnp.zeros_like(dk_sum)
    dv_sum[...] = jnp.zeros_like(dv_sum)

    def one_block(index, carry):
        first = pl.multiple_of(index * block, block)
        query_place = whole_place(first, token_rows, place)
        q_block = q_ref[pl.ds(first, block), :]
        d_block = d_ref[pl.ds(first, block), :]
        outs = []
        for head in range(2):
            mask = half_lanes(q_block.shape, head)
            q_head = jnp.where(mask, q_block, jnp.zeros_like(q_block))
            inverse = inv_ref[head, :, pl.ds(first, block)]
            scale = jnp.transpose(jnp.broadcast_to(inverse, (PAIR, block)))
            d_head = jnp.where(mask, d_block.astype(jnp.float32) * scale, 0.0)
            d_head = d_head.astype(jnp.bfloat16)
            prob_ref[...] = cols_dot(v_ref[...], d_head)
            total = jnp.zeros((8, block), jnp.float32)
            for tile in range(tiles):
                rows = slice(tile * TILE, (tile + 1) * TILE)
                exponent = e_ref[head, rows, pl.ds(first, block)].astype(jnp.float32)
                total = total + fold_rows(exponent * prob_ref[rows, :])
            centre = jnp.sum(total, axis=0, keepdims=True) * inverse
            for tile in range(tiles):
                rows = slice(tile * TILE, (tile + 1) * TILE)
                exponent = e_ref[head, rows, pl.ds(first, block)].astype(jnp.float32)
                grad = exponent * (prob_ref[rows, :] - centre)
                offset = pl.multiple_of(query_place + (reach - key_places[tile]), TILE)
                at = pl.ds(offset, block)
                strip_ref[head, :, at] = strip_ref[head, :, at] + grad
                low_ref[rows, :] = grad.astype(jnp.bfloat16)
            dk_sum[...] += jnp.dot(low_ref[...], q_head, preferred_element_type=jnp.float32)
            dv_sum[...] += jnp.dot(
                e_ref[head, :, pl.ds(first, block)], d_head, preferred_element_type=jnp.float32
            )
            outs.append(
                jnp.dot(
                    keys_t[head * DH : (head + 1) * DH, :],
                    low_ref[...],
                    preferred_element_type=jnp.float32,
                )
            )
        grad_ref[pl.ds(first, block), :PAIR] = jnp.transpose(jnp.concatenate(outs, axis=0)).astype(
            jnp.bfloat16
        )
        return carry

    lax.fori_loop(0, length // block, one_block, 0)
    grad_ref[:, PAIR : 2 * PAIR] = dk_sum[...].astype(jnp.bfloat16)
    grad_ref[:, 2 * PAIR :] = dv_sum[...].astype(jnp.bfloat16)
    for head in range(2):
        turned = strip_ref[head]
        while turned.shape[0] > 1:
            half = turned.shape[0] // 2
            turned = pltpu.roll(turned[:half], half, 1) + turned[half:]
        line_ref[0, head : head + 1, :] = turned


def attention_backward(qkv, place, d, e, inv, heads, token_rows):
    length = qkv.shape[0]
    block = min(256, token_rows)
    pairs = heads // 2
    triple = pl.BlockSpec((length, 3 * PAIR), lambda i: (0, i))
    return pl.pallas_call(
        functools.partial(backward_kernel, block, token_rows),
        grid=(pairs,),
        in_specs=[
            pl.BlockSpec(memory_space=pltpu.SMEM),
            triple,
            pl.BlockSpec((length, PAIR), lambda i: (0, i)),
            pl.BlockSpec((2, length, length), lambda i: (i, 0, 0)),
            pl.BlockSpec((2, 1, length), lambda i: (i, 0, 0)),
        ],
        out_specs=[triple, pl.BlockSpec((1, 2, 2 * length), lambda i: (i, 0, 0))],
        out_shape=[
            jax.ShapeDtypeStruct((length, 3 * heads * DH), jnp.bfloat16),
            jax.ShapeDtypeStruct((pairs, 2, 2 * length), jnp.float32),
        ],
        scratch_shapes=[
            pltpu.VMEM((2, TILE, 2 * length), jnp.float32),
            pltpu.VMEM((length, block), jnp.float32),
            pltpu.VMEM((length, block), jnp.bfloat16),
            pltpu.VMEM((length, PAIR), jnp.float32),
            pltpu.VMEM((length, PAIR), jnp.float32),
        ],
        compiler_params=pltpu.CompilerParams(vmem_limit_bytes=VMEM_BYTES),
        cost_estimate=pl.CostEstimate(
            flops=40 * heads * length * length * DH,
            bytes_accessed=2 * heads * length * length,
            transcendentals=0,
        ),
        name="attention_backward",
    )(place, qkv, d, e, inv)


def swap(piece, axis, step):
    return lax.ppermute(piece, axis, [(i, i ^ step) for i in range(lax.axis_size(axis))])


def gather_pieces(piece, relay=True):
    count = lax.axis_size("seq")
    if count != 4 or not relay:
        return [[piece]] + [[swap(piece, "seq", step)] for step in range(1, count)]
    half = piece.shape[0] // 2
    first = swap(piece, "seq", 1)
    second = swap(piece, "seq", 2)
    third_upper = swap(second[:half], "seq", 1)
    third_lower = swap(first[half:], "seq", 2)
    return [[piece], [first], [second], [third_upper, third_lower]]


def gather_rows(piece):
    return jnp.concatenate([part for parts in gather_pieces(piece) for part in parts], axis=0)


def scatter_terms(rows, weights):
    size = rows.shape[0] // lax.axis_size("seq")
    return cols_dot(rows[size:], weights).astype(jnp.bfloat16)


def scatter_begin(terms):
    count = lax.axis_size("seq")
    size = terms.shape[0] // (count - 1)
    if count != 4:
        return tuple(
            swap(terms[k * size : (k + 1) * size], "seq", k + 1) for k in range(count - 1)
        )
    upper = swap(terms[2 * size : 2 * size + size // 2], "seq", 1)
    lower = swap(terms[2 * size + size // 2 :], "seq", 2)
    return upper, lower


def scatter_add(terms, received):
    if lax.axis_size("seq") != 4:
        return received
    size = terms.shape[0] // 3
    upper, lower = (part.astype(jnp.float32) for part in received)
    first = terms[:size].astype(jnp.float32) + jnp.pad(lower, ((size // 2, 0), (0, 0)))
    second = terms[size : 2 * size].astype(jnp.float32) + jnp.pad(upper, ((0, size // 2), (0, 0)))
    return first.astype(jnp.bfloat16), second.astype(jnp.bfloat16)


def scatter_end(sums):
    if lax.axis_size("seq") != 4:
        return sums
    return swap(sums[0], "seq", 1), swap(sums[1], "seq", 2)


def scatter_own(rows, weights, received):
    own = cols_dot(rows[: rows.shape[0] // lax.axis_size("seq")], weights)
    return own + sum(part.astype(jnp.float32) for part in received)


def scatter_sum(rows, weights):
    terms = scatter_terms(rows, weights)
    return scatter_own(rows, weights, scatter_end(scatter_add(terms, scatter_begin(terms))))


def total_sum(values, axis):
    count = lax.axis_size(axis)
    level = [values] + [swap(values, axis, step) for step in range(1, count)]
    while len(level) > 1:
        level = [level[i] + level[i + 1] for i in range(0, len(level), 2)]
    return level[0]


def feed_forward_kernel(tile, x_ref, w_ref, act_ref, gelu_ref, slope_ref):
    rows = x_ref.shape[0]
    chunk = min(512, rows)
    for start in range(0, rows, chunk):
        at = slice(start, start + chunk)
        both = jnp.dot(x_ref[at, :], w_ref[...], preferred_element_type=jnp.float32)
        gate, up = both[:, :tile], both[:, tile:]
        square = gate * gate
        tanh = jnp.tanh(GELU_SCALE * gate * (1.0 + GELU_CUBE * square))
        half_up = 0.5 * (1.0 + tanh)
        gelu = gate * half_up
        bend = 0.5 * GELU_SCALE * gate * (1.0 - tanh * tanh) * (1.0 + 3.0 * GELU_CUBE * square)
        act_ref[at, :] = (gelu * up).astype(jnp.bfloat16)
        gelu_ref[at, :] = gelu.astype(jnp.bfloat16)
        slope_ref[at, :] = (up * (half_up + bend)).astype(jnp.bfloat16)


def feed_forward(rows, weights, tile):
    length, model_width = rows.shape
    units = weights.shape[1] // 2
    block = pl.BlockSpec((length, tile), lambda j: (0, j))
    return pl.pallas_call(
        functools.partial(feed_forward_kernel, tile),
        grid=(units // tile,),
        in_specs=[
            pl.BlockSpec((length, model_width), lambda j: (0, 0)),
            pl.BlockSpec((model_width, 2 * tile), lambda j: (0, j)),
        ],
        out_specs=[block, block, block],
        out_shape=[
            jax.ShapeDtypeStruct((length, units), jnp.bfloat16),
            jax.ShapeDtypeStruct((length, units), jnp.bfloat16),
            jax.ShapeDtypeStruct((length, units), jnp.bfloat16),
        ],
        compiler_params=pltpu.CompilerParams(vmem_limit_bytes=VMEM_BYTES),
        cost_estimate=pl.CostEstimate(
            flops=4 * length * model_width * units,
            bytes_accessed=4 * model_width * units + 10 * length * units,
            transcendentals=length * units,
        ),
        name="feed_forward",
    )(rows, weights)


def feed_forward_back_kernel(tile, d_ref, w_ref, gelu_ref, slope_ref, grad_ref):
    rows = d_ref.shape[0]
    chunk = min(512, rows)
    for start in range(0, rows, chunk):
        at = slice(start, start + chunk)
        grad = jnp.dot(d_ref[at, :], w_ref[...], preferred_element_type=jnp.float32)
        grad_ref[at, :tile] = (grad * slope_ref[at, :].astype(jnp.float32)).astype(jnp.bfloat16)
        grad_ref[at, tile:] = (grad * gelu_ref[at, :].astype(jnp.float32)).astype(jnp.bfloat16)


def feed_forward_back(grad_rows, weights, gelu, slope, tile):
    length, model_width = grad_rows.shape
    units = weights.shape[1]
    block = pl.BlockSpec((length, tile), lambda j: (0, j))
    return pl.pallas_call(
        functools.partial(feed_forward_back_kernel, tile),
        grid=(units // tile,),
        in_specs=[
            pl.BlockSpec((length, model_width), lambda j: (0, 0)),
            pl.BlockSpec((model_width, tile), lambda j: (0, j)),
            block,
            block,
        ],
        out_specs=pl.BlockSpec((length, 2 * tile), lambda j: (0, j)),
        out_shape=jax.ShapeDtypeStruct((length, 2 * units), jnp.bfloat16),
        compiler_params=pltpu.CompilerParams(vmem_limit_bytes=VMEM_BYTES),
        cost_estimate=pl.CostEstimate(
            flops=2 * length * model_width * units,
            bytes_accessed=2 * model_width * units + 12 * length * units,
            transcendentals=0,
        ),
        name="feed_forward_back",
    )(grad_rows, weights, gelu, slope)


def place_kernel(moves, count, widths, place_ref, *refs):
    pieces, outs = refs[:count], refs[count:]
    for step in range(count):
        owner = jnp.bitwise_xor(place_ref[0], step)
        for out, source, target, size in moves:
            at = pl.multiple_of(owner * widths[out] + target, TILE)
            block = pieces[step][:, source : source + size]
            outs[out][:, pl.ds(at, size)] = block.astype(jnp.float32)


def place_columns(parts, place, moves, widths):
    pieces = [part[0] if len(part) == 1 else jnp.concatenate(part, axis=0) for part in parts]
    count = len(pieces)
    rows, width = pieces[0].shape
    block = min(64, rows)
    return pl.pallas_call(
        functools.partial(place_kernel, moves, count, widths),
        grid=(rows // block,),
        in_specs=[pl.BlockSpec(memory_space=pltpu.SMEM)]
        + [pl.BlockSpec((block, width), lambda i: (i, 0))] * count,
        out_specs=[pl.BlockSpec((block, count * size), lambda i: (i, 0)) for size in widths],
        out_shape=[jax.ShapeDtypeStruct((rows, count * size), jnp.float32) for size in widths],
        compiler_params=pltpu.CompilerParams(vmem_limit_bytes=VMEM_BYTES),
        cost_estimate=pl.CostEstimate(
            flops=0, bytes_accessed=6 * rows * count * width, transcendentals=0
        ),
        name="place_columns",
    )(place, *pieces)


def take_kernel(moves, count, place_ref, *refs):
    out_ref = refs[count]
    for which, source, target, size in moves:
        out_ref[:, source : source + size] = refs[which][:, target : target + size]


def take_columns(place, weights, moves, counts):
    rows = weights[0].shape[0]
    block = min(64, rows)
    width = sum(counts)

    def chosen(count):
        return pl.BlockSpec((block, count), lambda i, place_ref: (i, place_ref[0]))

    return pl.pallas_call(
        functools.partial(take_kernel, moves, len(weights)),
        grid_spec=pltpu.PrefetchScalarGridSpec(
            num_scalar_prefetch=1,
            grid=(rows // block,),
            in_specs=[chosen(count) for count in counts],
            out_specs=pl.BlockSpec((block, width), lambda i, place_ref: (i, 0)),
        ),
        out_shape=jax.ShapeDtypeStruct((rows, width), weights[0].dtype),
        compiler_params=pltpu.CompilerParams(vmem_limit_bytes=VMEM_BYTES),
        cost_estimate=pl.CostEstimate(flops=0, bytes_accessed=4 * rows * width, transcendentals=0),
        name="take_columns",
    )(place, *weights)


def split_kernel(core_ref, own_in, other_in, own_ref, other_ref):
    own_ref[...] = own_in[...]
    other_ref[...] = other_in[...]


def split_columns(rows, core, groups):
    length, width = rows.shape
    size = width // groups

    def chosen(side):
        return pl.BlockSpec(
            (length, size), lambda i, core_ref: (0, 2 * i + jnp.bitwise_xor(core_ref[0], side))
        )

    half = jax.ShapeDtypeStruct((length, width // 2), rows.dtype)
    block = pl.BlockSpec((length, size), lambda i, core_ref: (0, i))
    return pl.pallas_call(
        split_kernel,
        grid_spec=pltpu.PrefetchScalarGridSpec(
            num_scalar_prefetch=1,
            grid=(groups // 2,),
            in_specs=[chosen(0), chosen(1)],
            out_specs=[block, block],
        ),
        out_shape=[half, half],
        compiler_params=pltpu.CompilerParams(vmem_limit_bytes=VMEM_BYTES),
        cost_estimate=pl.CostEstimate(flops=0, bytes_accessed=4 * length * width, transcendentals=0),
        name="split_columns",
    )(core, rows, rows)


def both(*values):
    return lax.optimization_barrier(values)


def add_low(sums, added):
    return (sums + added.astype(jnp.float32)).astype(jnp.bfloat16)


def on_device(
    tokens,
    segments,
    buckets,
    w_query,
    w_key,
    w_value,
    w_attn_out,
    gain_attn,
    rel_table,
    w_gate,
    w_up,
    w_down,
    gain_ffn,
    out_grad,
):
    token_rows = tokens.shape[1]
    model_width = tokens.shape[2]
    ffn_width = w_gate.shape[1]
    segment_row = segments[0]
    row_length = segment_row.shape[0]
    seq_count = lax.axis_size("seq")
    fsdp_count = lax.axis_size("fsdp")
    seq_place = lax.axis_index("seq")
    fsdp_place = lax.axis_index("fsdp")
    place = seq_place.astype(jnp.int32).reshape(1)
    head_count = model_width // seq_count // DH
    column_count = model_width // seq_count
    unit_count = ffn_width // seq_count

    tile = 256 if unit_count % 256 == 0 else 128
    pairs = head_count // 2

    def gather_weights(piece):
        return lax.all_gather(piece, "fsdp", axis=0, tiled=True)

    qkv_moves = [
        (which, (3 * pair + which) * PAIR, pair * PAIR, PAIR)
        for pair in range(pairs)
        for which in range(3)
    ] + [(3, 3 * column_count, 0, column_count)]
    unit_moves = [
        (which, (2 * block + which) * tile, block * tile, tile)
        for block in range(unit_count // tile)
        for which in range(2)
    ]
    attn_part = take_columns(
        place, (w_query, w_key, w_value, w_attn_out), qkv_moves, [column_count] * 4
    )
    attn_w = gather_weights(attn_part)
    gains = lax.all_gather(jnp.stack([gain_attn, gain_ffn]), "fsdp", axis=1, tiled=True)
    attn_gain = gains[0].astype(jnp.float32)
    ffn_gain = gains[1].astype(jnp.float32)
    qkv_w = attn_w[:, : 3 * column_count]
    output_w = attn_w[:, 3 * column_count :]

    table_rows = jnp.pad(buckets[::-1], (0, 1), constant_values=-1)
    bucket_table = (
        table_rows[:, None] == jnp.arange(rel_table.shape[1], dtype=jnp.int32)[None, :]
    ).astype(jnp.float32)
    local_table = lax.dynamic_slice_in_dim(rel_table, seq_place * head_count, head_count, 0)
    bias_line = jnp.dot(local_table, jnp.transpose(bucket_table), precision=PRECISE)
    bias_line = bias_line.reshape(head_count // 2, 2, 2 * row_length)
    segment_wide = jnp.broadcast_to(segment_row[:, None], (row_length, TILE))

    stream = tokens[0].astype(jnp.float32)
    scale_attn = lax.rsqrt(jnp.mean(stream * stream, axis=-1, keepdims=True) + EPSILON)
    normed_attn = stream * scale_attn
    upstream = out_grad[0].astype(jnp.float32)

    stream_rows = gather_rows(tokens[0])
    gate_up_part = take_columns(place, (w_gate, w_up), unit_moves, [unit_count] * 2)
    gate_up_part, stream_rows = both(gate_up_part, stream_rows)
    gate_up_w = gather_weights(gate_up_part)
    stream_rows = stream_rows.astype(jnp.float32)
    rows_scale = lax.rsqrt(jnp.mean(stream_rows * stream_rows, axis=-1, keepdims=True) + EPSILON)
    attn_rows = (stream_rows * rows_scale * attn_gain).astype(jnp.bfloat16)
    ff_grad_rows = gather_rows(out_grad[0])
    attn_rows, ff_grad_rows = both(attn_rows, ff_grad_rows)

    qkv = jnp.dot(attn_rows, qkv_w, preferred_element_type=jnp.float32).astype(jnp.bfloat16)
    down_part, qkv = both(
        lax.dynamic_slice_in_dim(w_down, seq_place * unit_count, unit_count, 1), qkv
    )
    down_w = gather_weights(down_part)
    context, exponents, inverse = attention_forward(
        qkv, place, segments, segment_wide, bias_line, head_count, token_rows
    )

    attn_out = scatter_sum(context, output_w)
    chips = fsdp_count // 2
    core = (fsdp_place % 2).astype(jnp.int32).reshape(1)
    groups = [[2 * chip + side for chip in range(chips)] for side in range(2)]

    def scatter_grads(grads, axis_index_groups=None):
        return lax.psum_scatter(
            grads,
            "fsdp",
            scatter_dimension=0,
            tiled=True,
            axis_index_groups=axis_index_groups,
        )

    ff_grad_own, ff_grad_other = split_columns(ff_grad_rows, core, fsdp_count)
    ff_grad_own, ff_grad_other, attn_out = both(ff_grad_own, ff_grad_other, attn_out)
    resid = stream + attn_out
    scale_ffn = lax.rsqrt(jnp.mean(resid * resid, axis=-1, keepdims=True) + EPSILON)
    normed_ffn = resid * scale_ffn
    ffn_rows = gather_rows((normed_ffn * ffn_gain).astype(jnp.bfloat16))

    hidden, gelu, slope = feed_forward(ffn_rows, gate_up_w, tile)

    down_away = rows_dot(ff_grad_other, hidden).astype(jnp.bfloat16)
    down_away, hidden = both(down_away, hidden)
    down_added = swap(down_away, "fsdp", 1)
    ff_away = scatter_terms(hidden, down_w)
    ff_away, gelu = both(ff_away, gelu)
    ff_far = scatter_begin(ff_away)
    unit_grad = feed_forward_back(ff_grad_rows, down_w, gelu, slope, tile)
    ffn_in_away = scatter_terms(unit_grad, gate_up_w)
    ffn_in_away, hidden, unit_grad = both(ffn_in_away, hidden, unit_grad)
    ffn_in_far = scatter_begin(ffn_in_away)
    down_grad = add_low(rows_dot(ff_grad_own, hidden), down_added)
    ffn_own, ffn_other = split_columns(ffn_rows, core, fsdp_count)
    down_grad, unit_grad = both(down_grad, unit_grad)
    down_owned = scatter_grads(down_grad, groups)
    gate_up_away = rows_dot(ffn_other, unit_grad).astype(jnp.bfloat16)
    gate_up_away, *ffn_in_far = both(gate_up_away, *ffn_in_far)
    gate_up_added = swap(gate_up_away, "fsdp", 1)
    ffn_in_sums = scatter_add(ffn_in_away, ffn_in_far)
    *ffn_in_sums, unit_grad = both(*ffn_in_sums, unit_grad)
    ffn_in_parts = scatter_end(ffn_in_sums)
    gate_up_grad = add_low(rows_dot(ffn_own, unit_grad), gate_up_added)
    gate_up_grad, unit_grad, *ffn_in_parts = both(gate_up_grad, unit_grad, *ffn_in_parts)
    gate_up_owned = scatter_grads(gate_up_grad, groups)
    ffn_in_grad = scatter_own(unit_grad, gate_up_w, ffn_in_parts)

    gain_ffn_part = jnp.sum(ffn_in_grad * normed_ffn, axis=0)
    resid_grad = upstream + norm_back(ffn_in_grad * ffn_gain, normed_ffn, scale_ffn)
    attn_grad_rows = gather_rows(resid_grad.astype(jnp.bfloat16))
    ff_sums = scatter_add(ff_away, ff_far)
    attn_grad_rows, *ff_sums = both(attn_grad_rows, *ff_sums)
    context_grad = jnp.dot(
        attn_grad_rows, output_w, preferred_element_type=jnp.float32
    ).astype(jnp.bfloat16)
    context_grad, down_owned, *ff_sums = both(context_grad, down_owned, *ff_sums)
    ff_parts = scatter_end(ff_sums)
    down_pieces = gather_pieces(down_owned, relay=False)
    qkv_grad, line_grad = attention_backward(
        qkv, place, context_grad, exponents, inverse, head_count, token_rows
    )
    qkv_grad, ff_parts, down_pieces = both(qkv_grad, ff_parts, down_pieces)
    attn_grads = rows_dot(attn_rows, qkv_grad).astype(jnp.bfloat16)
    attn_grads, context, qkv_grad = both(attn_grads, context, qkv_grad)
    attn_owned = scatter_grads(attn_grads)
    output_grad = rows_dot(attn_grad_rows, context).astype(jnp.bfloat16)
    output_grad, qkv_grad, hidden = both(output_grad, qkv_grad, hidden)
    output_owned = scatter_grads(output_grad)
    attn_in_away = scatter_terms(qkv_grad, qkv_w)
    attn_in_away, gate_up_owned, qkv_grad = both(attn_in_away, gate_up_owned, qkv_grad)
    attn_in_far = scatter_begin(attn_in_away)
    gate_up_pieces = gather_pieces(gate_up_owned)
    attn_in_parts = scatter_end(scatter_add(attn_in_away, attn_in_far))
    attn_in_grad = scatter_own(qkv_grad, qkv_w, attn_in_parts)
    gain_attn_part = jnp.sum(attn_in_grad * normed_attn, axis=0)
    stream_grad = resid_grad + norm_back(attn_in_grad * attn_gain, normed_attn, scale_attn)
    ff_out = scatter_own(hidden, down_w, ff_parts)
    result = resid + ff_out

    (down_out,) = place_columns(down_pieces, place, [(0, 0, 0, unit_count)], [unit_count])
    gate_out, up_out = place_columns(gate_up_pieces, place, unit_moves, [unit_count] * 2)

    own_segments = lax.dynamic_slice_in_dim(segment_row, seq_place * token_rows, token_rows, 0)
    valid = (own_segments >= 0).astype(jnp.float32)
    stat_terms = jnp.stack(
        [
            jnp.sum(valid * jnp.sum(result * result, axis=-1)),
            jnp.sum(valid * jnp.sum(attn_out * attn_out, axis=-1)),
            jnp.sum(valid * jnp.sum(ff_out * ff_out, axis=-1)),
            jnp.sum(valid),
        ]
    )
    table_part = jnp.dot(
        line_grad.reshape(head_count, 2 * row_length), bucket_table, precision=PRECISE
    )
    full_table = lax.dynamic_update_slice_in_dim(
        jnp.zeros(rel_table.shape, jnp.float32), table_part, seq_place * head_count, 0
    )
    packed = jnp.concatenate(
        [gain_attn_part, gain_ffn_part, full_table.reshape(-1), jnp.pad(stat_terms, (0, 124))]
    ).reshape(-1, 128)
    summed = total_sum(total_sum(packed, "seq"), "fsdp").reshape(-1)
    attn_owned, summed, result, stream_grad, down_out, gate_out, up_out = both(
        attn_owned, summed, result, stream_grad, down_out, gate_out, up_out
    )
    attn_pieces = gather_pieces(attn_owned)
    query_out, key_out, value_out = place_columns(
        attn_pieces, place, qkv_moves[:-1], [column_count] * 3
    )
    output_owned, attn_pieces = both(output_owned, attn_pieces)
    (output_out,) = place_columns(
        gather_pieces(output_owned), place, [(0, 0, 0, column_count)], [column_count]
    )
    table_end = 2 * model_width + rel_table.size
    stat_totals = summed[table_end : table_end + 4]
    rms_stats = jnp.sqrt(stat_totals[0:3] / (stat_totals[3] * model_width))
    gain_rows = model_width // fsdp_count
    table_rows = rel_table.shape[0] // fsdp_count
    gain_attn_grad = lax.dynamic_slice_in_dim(summed, fsdp_place * gain_rows, gain_rows, 0)
    gain_ffn_grad = lax.dynamic_slice_in_dim(
        summed, model_width + fsdp_place * gain_rows, gain_rows, 0
    )
    rel_table_grad = lax.dynamic_slice_in_dim(
        summed[2 * model_width : table_end].reshape(rel_table.shape),
        fsdp_place * table_rows,
        table_rows,
        0,
    )
    return (
        result.astype(jnp.bfloat16)[None],
        stream_grad.astype(jnp.bfloat16)[None],
        query_out,
        key_out,
        value_out,
        output_out,
        gain_attn_grad,
        rel_table_grad,
        gate_out,
        up_out,
        down_out,
        gain_ffn_grad,
        rms_stats,
    )


def solution(mesh):
    in_specs = (
        P("fsdp", "seq", None),
        P("fsdp", None),
        P(),
        P("fsdp", None),
        P("fsdp", None),
        P("fsdp", None),
        P("fsdp", None),
        P("fsdp"),
        P(),
        P("fsdp", None),
        P("fsdp", None),
        P("fsdp", None),
        P("fsdp"),
        P("fsdp", "seq", None),
    )
    out_specs = (
        P("fsdp", "seq", None),
        P("fsdp", "seq", None),
        P("fsdp", None),
        P("fsdp", None),
        P("fsdp", None),
        P("fsdp", None),
        P("fsdp"),
        P("fsdp", None),
        P("fsdp", None),
        P("fsdp", None),
        P("fsdp", None),
        P("fsdp"),
        P(),
    )
    return jax.shard_map(
        on_device, mesh=mesh, in_specs=in_specs, out_specs=out_specs, check_vma=False
    )
```

time: 1510 us -> 654 us (0.43)
  waiting for transfers between devices: 1120 us -> 211 us
  Pallas kernels: 75.7 us -> 145 us
  starting transfers between devices: 1.81 us -> 66.8 us
  blocking collectives: 63.6 us -> 12.7 us
  matrix products: 151 us -> 126 us
  local copies, waits for them, and re-layouts: 53.4 us -> 37.7 us
    all_gather x18 -> x3, waiting for transfers between devices: 583 us -> 0.02 us  [gather_weights(): return lax.all_gather(piece, 'fsdp', axis=0, tiled=True)]
    reduce_scatter x5 -> x4, waiting for transfers between devices: 529 us -> 0.01 us  [scatter_grads(): lax.psum_scatter(grads, 'fsdp', scatter_dimension=0, tiled=True, axis_ind...]
    ppermute x0 -> x59, waiting for transfers between devices: none -> 211 us  [swap(): lax.ppermute(piece, axis, [(i, i ^ step) for i in range(lax.axis_size(axi...]
    pallas_call x2 -> x12, Pallas kernels: 75.7 us -> 145 us  [the longest x1 41.9 us: attention_backward(): pl.pallas_call(functools.partial(backward_kernel, block, token_rows), gri...]
    ppermute x0 -> x59, starting transfers between devices: none -> 66.3 us  [swap(): lax.ppermute(piece, axis, [(i, i ^ step) for i in range(lax.axis_size(axi...]
    dot_general x6 -> x1, matrix products: 56.1 us -> 12.2 us  [on_device(): jnp.dot(attn_rows, qkv_w, preferred_element_type=jnp.float32)]
    psum x1 -> x0, blocking collectives: 39.9 us -> none  [on_device(): lax.psum((gain_attn_part, gain_ffn_part, full_table, stat_terms), ('fsdp'...]
    dot_general x7 -> x8, matrix products: 46.7 us -> 57.2 us  [cols_dot(): lax.dot_general(left, right, (((1,), (1,)), ((), ())), preferred_element_...]
  transfers between devices with their start and end apart: 23 -> 66, of which waited for: 21 -> 35; matrix products, arithmetic and copies ran while one was open for 9% -> 28% of each run, Pallas kernels for 2% -> 21%
where the time goes in v2:
time: 654 us; the launch traced here: 646 us
  waiting for transfers between devices  211 us (32%)
  Pallas kernels  145 us (22%)
  matrix products  126 us (19%)
  starting transfers between devices  66.8 us (10%)
  local copies, waits for them, and re-layouts  37.7 us (6%)
  other arithmetic  31.1 us (5%)
  between operations  15.7 us (2%)
  blocking collectives  12.7 us (2%)
    ppermute x59, waiting for transfers between devices, swap(): lax.ppermute(piece, axis, [(i, i ^ step) for i in range(lax.axis_size(axi...  211 us
    ppermute x59, starting transfers between devices, swap(): lax.ppermute(piece, axis, [(i, i ^ step) for i in range(lax.axis_size(axi...  66.3 us
    dot_general x8, matrix products, cols_dot(): lax.dot_general(left, right, (((1,), (1,)), ((), ())), preferred_element_...  57.2 us
    dot_general x6, matrix products, rows_dot(): lax.dot_general(left, right, (((0,), (0,)), ((), ())), preferred_element_...  49.8 us
    pallas_call x1, Pallas kernels, attention_backward(): pl.pallas_call(functools.partial(backward_kernel, block, token_rows), gri...  41.9 us
    pallas_call x1, Pallas kernels, attention_forward(): pl.pallas_call(functools.partial(forward_kernel, block, token_rows), grid...  35.1 us
    unnamed x86, local copies, waits for them, and re-layouts  22.1 us
    pallas_call x4, Pallas kernels, place_columns(): pl.pallas_call(functools.partial(place_kernel, moves, count, widths), gri...  20.8 us
  transfers between devices with their start and end apart: 66, of which 35 were waited for; matrix products, arithmetic and copies ran while one was open for 28% of the time, Pallas kernels for 21%

profile of v2, /device:TPU:0, one launch (start us, length us, event | category | flops | bytes accessed | tf_op | source)
XLA Modules:
  0.0 646.4 jit_solution(17553753782813638678)
XLA Ops:
  15.4 21.9 %collective-permute-done.1 = bf16[256,2048]{1,0:T(8,128)(2,1)S(1)} collective-permute-done((bf16[256,2048]{1,0:T(8,128)(2,1)}, bf16[256,2048]{1,0:T(8,128)(2,1)S(1)}, u32[]{:S(2)}, u32[]{:S(2)}) %collective-permute-start.1) | collective-permute-done | bytes 1048608 | tf_op jit(solution)/shard_map/ppermute | solution.py:286
  67.5 12.7 %all_gather.12 = bf16[2,2048]{1,0:T(2,128)(2,1)S(1)} all-gather(bf16[2,256]{1,0:T(2,128)(2,1)S(1)} %pad_maximum_fusion.3), channel_id=1, replica_groups=mesh['fsdp'=8,'seq'=4] {'fsdp'}, dimensions={1}, use_global_device_ids=true | all-gather | bytes 9216 | tf_op jit(solution)/shard_map/all_gather | solution.py:583
  103.9 12.2 %fusion.11.qkv_ref = bf16[1024,1536]{1,0:T(8,128)(2,1)} fusion(bf16[1024,2048]{1,0:T(8,128)(2,1)} %fusion.2, bf16[2048,2048]{1,0:T(8,128)(2,1)} %all-gather.4.cloned.1.call-done), kind=kOutput, calls=%fused_computation.17 | convolution fusion | flops 6444023808 | bytes 13631488 | tf_op jit(solution)/shard_map/dot_general | solution.py:613
  117.4 35.1 %attention_forward.1 = (bf16[1024,512]{1,0:T(8,128)(2,1)}, bf16[8,1024,1024]{2,1,0:T(8,128)(2,1)}, f32[8,1,1024]{2,1,0:T(1,128)}) custom-call(s32[1]{0:T(128)} %bitcast.place_ref, bf16[1024,1536]{1,0:T(8,128)(2,1)} %fusion.11.qkv_ref, s32[1,1024]{1,0:T(1,128)} %row_ref.1, s32[1024,128]{1,0:T(8,128)} %broadcast_in_dim.11.col_ref, f32[4,2,2048]{2,1,0:T(2,128)} %reshape.99.bias_ref), custom_call_target="tpu_custom_call" | custom-call | flops 8589934592 | bytes 16777216 | tf_op jit(solution)/shard_map/attention_forward/pallas_call | solution.py:130
  157.6 8.1 %collective-permute-done.10 = bf16[128,2048]{1,0:T(8,128)(2,1)S(1)} collective-permute-done((bf16[128,2048]{1,0:T(8,128)(2,1)S(1)}, bf16[128,2048]{1,0:T(8,128)(2,1)S(1)}, u32[]{:S(2)}, u32[]{:S(2)}) %collective-permute-start.10) | collective-permute-done | bytes 524320 | tf_op jit(solution)/shard_map/ppermute | solution.py:286
  178.9 11.5 %collective-permute-done.11 = bf16[256,2048]{1,0:T(8,128)(2,1)} collective-permute-done((bf16[256,2048]{1,0:T(8,128)(2,1)}, bf16[256,2048]{1,0:T(8,128)(2,1)}, u32[]{:S(2)}, u32[]{:S(2)}) %collective-permute-start.11) | collective-permute-done | bytes 1048608 | tf_op jit(solution)/shard_map/ppermute | solution.py:286
  195.2 20.4 %collective-permute-done.13 = bf16[256,2048]{1,0:T(8,128)(2,1)S(1)} collective-permute-done((bf16[256,2048]{1,0:T(8,128)(2,1)S(1)}, bf16[256,2048]{1,0:T(8,128)(2,1)S(1)}, u32[]{:S(2)}, u32[]{:S(2)}) %collective-permute-start.13) | collective-permute-done | bytes 1048608 | tf_op jit(solution)/shard_map/ppermute | solution.py:286
  232.4 18.4 %feed_forward.1 = (bf16[1024,1280]{1,0:T(8,128)(2,1)}, bf16[1024,1280]{1,0:T(8,128)(2,1)}, bf16[1024,1280]{1,0:T(8,128)(2,1)}) custom-call(bf16[1024,2048]{1,0:T(8,128)(2,1)} %copy-done.2, bf16[2048,2560]{1,0:T(8,128)(2,1)} %all-gather.8.cloned.1.call-done.w_ref), custom_call_target="tpu_custom_call" | custom-call | flops 10737418240 | bytes 23592960 | tf_op jit(solution)/shard_map/feed_forward/pallas_call | solution.py:377
  257.1 9.0 %convolution_convert_fusion.4 = bf16[768,2048]{1,0:T(8,128)(2,1)} fusion(bf16[2048,1280]{1,0:T(8,128)(2,1)} %all-gather.6.cloned.1.call-done.w_ref, bf16[1024,1280]{1,0:T(8,128)(2,1)} %get-tuple-element.143), kind=kOutput, calls=%fused_computation.22 | convolution fusion | flops 4028104704 | bytes 10354688 | tf_op jit(solution)/shard_map/dot_general | solution.py:30
  266.0 11.8 %feed_forward_back.1 = bf16[1024,2560]{1,0:T(8,128)(2,1)} custom-call(bf16[1024,2048]{1,0:T(8,128)(2,1)} %constant_dynamic-update-slice_fusion.5.own_in.other_in.d_ref, bf16[2048,1280]{1,0:T(8,128)(2,1)} %all-gather.6.cloned.1.call-done.w_ref, bf16[1024,1280]{1,0:T(8,128)(2,1)} %get-tuple-element.104.gelu_ref, bf16[1024,1280]{1,0:T(8,128)(2,1)} %get-tuple-element.105.slope_ref), custom_call_target="tpu_custom_call" | custom-call | flops 5368709120 | bytes 20971520 | tf_op jit(solution)/shard_map/feed_forward_back/pallas_call | solution.py:414
  277.9 13.5 %fusion.14 = bf16[768,2048]{1,0:T(8,128)(2,1)} fusion(bf16[2048,2560]{1,0:T(8,128)(2,1)} %all-gather.8.cloned.1.call-done.w_ref, bf16[1024,2560]{1,0:T(8,128)(2,1)} %feed_forward_back.1), kind=kOutput, calls=%fused_computation.20 | convolution fusion | flops 8054636544 | bytes 17563648 | tf_op jit(solution)/shard_map/dot_general | solution.py:30
  300.7 10.2 %convolution_convert_fusion.1 = bf16[1024,2560]{1,0:T(8,128)(2,1)} fusion(bf16[1024,1024]{1,0:T(8,128)(2,1)} %get-tuple-element.107, bf16[1024,2560]{1,0:T(8,128)(2,1)} %feed_forward_back.1), kind=kOutput, calls=%fused_computation.7 | convolution fusion | flops 5371330560 | bytes 12582912 | tf_op jit(solution)/shard_map/dot_general | solution.py:24
  322.9 11.0 %add_convert_fusion = bf16[1024,2560]{1,0:T(8,128)(2,1)} fusion(bf16[1024,2560]{1,0:T(8,128)(2,1)} %collective-permute-done.19, bf16[1024,1024]{1,0:T(8,128)(2,1)S(1)} %copy-done.30, bf16[1024,2560]{1,0:T(8,128)(2,1)} %feed_forward_back.1), kind=kOutput, calls=%fused_computation.2 | convolution fusion | flops 5376573440 | bytes 17825792 | tf_op jit(solution)/shard_map/dot_general | solution.py:24
  333.9 9.5 %collective-permute-done.20 = bf16[256,2048]{1,0:T(8,128)(2,1)} collective-permute-done((bf16[256,2048]{1,0:T(8,128)(2,1)}, bf16[256,2048]{1,0:T(8,128)(2,1)}, u32[]{:S(2)}, u32[]{:S(2)}) %collective-permute-start.20) | collective-permute-done | bytes 1048608 | tf_op jit(solution)/shard_map/ppermute | solution.py:286
  343.7 8.2 %multiply_reduce_fusion.3 = (f32[2048]{0:T(1024)S(1)}, f32[256]{0:T(256)S(1)}, f32[256,2048]{1,0:T(8,128)S(1)}) fusion(f32[256,2048]{1,0:T(8,128)S(1)} %get-tuple-element.180, f32[256]{0:T(256)S(1)} %add_rsqrt_fusion.2, f32[2048]{0:T(1024)S(1)} %bitcast.65, bf16[256,2048]{1,0:T(8,128)(2,1)} %collective-permute-done.21, ...), kind=kOutput, calls=%fused_computation.42 | convolution fusion | flops 2689595136 | bytes 18106368 | tf_op jit(solution)/shard_map/dot_general | solution.py:30
  358.4 20.9 %collective-permute-done.23 = bf16[256,2048]{1,0:T(8,128)(2,1)S(1)} collective-permute-done((bf16[256,2048]{1,0:T(8,128)(2,1)S(1)}, bf16[256,2048]{1,0:T(8,128)(2,1)S(1)}, u32[]{:S(2)}, u32[]{:S(2)}) %collective-permute-start.23) | collective-permute-done | bytes 1048608 | tf_op jit(solution)/shard_map/ppermute | solution.py:286
  380.9 8.1 %collective-permute-done.26 = bf16[128,2048]{1,0:T(8,128)(2,1)S(1)} collective-permute-done((bf16[128,2048]{1,0:T(8,128)(2,1)S(1)}, bf16[128,2048]{1,0:T(8,128)(2,1)S(1)}, u32[]{:S(2)}, u32[]{:S(2)}) %collective-permute-start.26) | collective-permute-done | bytes 524320 | tf_op jit(solution)/shard_map/ppermute | solution.py:286
  394.7 8.3 %collective-permute-done.24 = bf16[128,2048]{1,0:T(8,128)(2,1)S(1)} collective-permute-done((bf16[128,2048]{1,0:T(8,128)(2,1)S(1)}, bf16[128,2048]{1,0:T(8,128)(2,1)S(1)}, u32[]{:S(2)}, u32[]{:S(2)}) %collective-permute-start.24) | collective-permute-done | bytes 524320 | tf_op jit(solution)/shard_map/ppermute | solution.py:286
  416.4 41.9 %attention_backward.1 = (bf16[1024,1536]{1,0:T(8,128)(2,1)}, f32[4,2,2048]{2,1,0:T(2,128)}) custom-call(s32[1]{0:T(128)} %bitcast.place_ref, bf16[1024,1536]{1,0:T(8,128)(2,1)} %fusion.11.qkv_ref, bf16[1024,512]{1,0:T(8,128)(2,1)} %fusion.36.d_ref, bf16[8,1024,1024]{2,1,0:T(8,128)(2,1)} %get-tuple-element.128.e_ref, f32[8,1,1024]{2,1,0:T(1,128)} %get-tuple-element.129.inv_ref), custom_call_target="tpu_custom_call" | custom-call | flops 21474836480 | bytes 16777216 | tf_op jit(solution)/shard_map/attention_backward/pallas_call | solution.py:253
  462.3 10.7 %convolution_convert_fusion = bf16[2048,1536]{1,0:T(8,128)(2,1)} fusion(bf16[1024,2048]{1,0:T(8,128)(2,1)S(1)} %copy-done.10, bf16[1024,1536]{1,0:T(8,128)(2,1)} %get-tuple-element.140), kind=kOutput, calls=%fused_computation.6 | convolution fusion | flops 6445596672 | bytes 13631488 | tf_op jit(solution)/shard_map/dot_general | solution.py:24
  479.2 9.4 %fusion.17 = bf16[768,2048]{1,0:T(8,128)(2,1)} fusion(bf16[2048,2048]{1,0:T(8,128)(2,1)} %all-gather.4.cloned.1.call-done, bf16[1024,1536]{1,0:T(8,128)(2,1)} %get-tuple-element.140), kind=kOutput, calls=%fused_computation.21 | convolution fusion | flops 4833411072 | bytes 11796480 | tf_op jit(solution)/shard_map/dot_general | solution.py:30
  519.3 11.3 %collective-permute-done.34 = bf16[256,2048]{1,0:T(8,128)(2,1)S(1)} collective-permute-done((bf16[256,2048]{1,0:T(8,128)(2,1)S(1)}, bf16[256,2048]{1,0:T(8,128)(2,1)S(1)}, u32[]{:S(2)}, u32[]{:S(2)}) %collective-permute-start.34) | collective-permute-done | bytes 1048608 | tf_op jit(solution)/shard_map/ppermute | solution.py:286
  581.0 7.0 %place_columns.5 = (f32[256,5120]{1,0:T(8,128)}, f32[256,5120]{1,0:T(8,128)}) custom-call(s32[1]{0:T(128)} %bitcast.place_ref, bf16[256,2560]{1,0:T(8,128)(2,1)} %reduce-scatter.9.cloned.1.call-done.refs_0_, bf16[256,2560]{1,0:T(8,128)(2,1)} %collective-permute-done.47.refs_1_, bf16[256,2560]{1,0:T(8,128)(2,1)} %copy-done.12, ...), custom_call_target="tpu_custom_call" | custom-call | bytes 15728640 | tf_op jit(solution)/shard_map/place_columns/pallas_call | solution.py:450
  590.1 16.8 %collective-permute-done.52.refs_2_ = bf16[256,1536]{1,0:T(8,128)(2,1)S(1)} collective-permute-done((bf16[256,1536]{1,0:T(8,128)(2,1)}, bf16[256,1536]{1,0:T(8,128)(2,1)S(1)}, u32[]{:S(2)}, u32[]{:S(2)}) %collective-permute-start.52) | collective-permute-done | bytes 786464 | tf_op jit(solution)/shard_map/ppermute | solution.py:286
  (297 shorter events, 282.8 us)
Async XLA Ops:
  7.2 96.7 %all-gather.4.cloned.1.call-start = ((), (), s32[]{:S(2)}) async-start(), calls=%async_computation.4 | async-start | bytes 9437184 | tf_op jit(solution)/shard_map/all_gather | solution.py:567
  10.8 221.6 %all-gather.8.cloned.1.call-start = ((), (), s32[]{:S(2)}) async-start(), calls=%async_computation.6 | async-start | bytes 11796480 | tf_op jit(solution)/shard_map/all_gather | solution.py:567
  10.9 26.4 %collective-permute-start.1 = (bf16[256,2048]{1,0:T(8,128)(2,1)}, bf16[256,2048]{1,0:T(8,128)(2,1)S(1)}, u32[]{:S(2)}, u32[]{:S(2)}) collective-permute-start(bf16[256,2048]{1,0:T(8,128)(2,1)} %bitcast.60), channel_id=1, source_target_pairs={{0,2},{1,3},{2,0},{3,1},{4,6},{5,7},{6,4},{7,5},{8,10},{9,11},{10,... | collective-permute-start | bytes 3145736 | tf_op jit(solution)/shard_map/ppermute | solution.py:286
  13.9 32.8 %collective-permute-start = (bf16[256,2048]{1,0:T(8,128)(2,1)}, bf16[256,2048]{1,0:T(8,128)(2,1)}, u32[]{:S(2)}, u32[]{:S(2)}) collective-permute-start(bf16[256,2048]{1,0:T(8,128)(2,1)} %bitcast.61), channel_id=1, source_target_pairs={{0,1},{1,0},{2,3},{3,2},{4,5},{5,4},{6,7},{7,6},{8,9},{9,8},{10,11... | collective-permute-start | bytes 3145736 | tf_op jit(solution)/shard_map/ppermute | solution.py:286
  61.4 195.7 %all-gather.6.cloned.1.call-start = ((), (), s32[]{:S(2)}) async-start(), calls=%async_computation.5 | async-start | bytes 5898240 | tf_op jit(solution)/shard_map/all_gather | solution.py:567
  61.4 26.3 %collective-permute-start.4 = (bf16[256,2048]{1,0:T(8,128)(2,1)}, bf16[256,2048]{1,0:T(8,128)(2,1)}, u32[]{:S(2)}, u32[]{:S(2)}) collective-permute-start(bf16[256,2048]{1,0:T(8,128)(2,1)} %bitcast.58), channel_id=1, source_target_pairs={{0,1},{1,0},{2,3},{3,2},{4,5},{5,4},{6,7},{7,6},{8,9},{9,8},{10,11... | collective-permute-start | bytes 3145736 | tf_op jit(solution)/shard_map/ppermute | solution.py:286
  116.2 294.8 %reduce-scatter.5.cloned.1.call-start = ((), (), s32[]{:S(2)}) async-start(), calls=%async_computation.7 | async-start | bytes 3276800 | tf_op jit(solution)/shard_map/reduce_scatter | solution.py:628
  257.0 34.4 %collective-permute-start.16 = (bf16[1024,1280]{1,0:T(8,128)(2,1)}, bf16[1024,1280]{1,0:T(8,128)(2,1)}, u32[]{:S(2)}, u32[]{:S(2)}) collective-permute-start(bf16[1024,1280]{1,0:T(8,128)(2,1)} %convolution_convert_fusion.2), channel_id=1, source_target_pairs={{0,4},{4,0},{8,12},{12,8},{16,20},{20,16},{24,28},{28,24},{1,5},{5... | collective-permute-start | bytes 7864328 | tf_op jit(solution)/shard_map/ppermute | solution.py:286
  313.9 174.7 %reduce-scatter.9.cloned.1.call-start = ((), (), s32[]{:S(2)}) async-start(), calls=%async_computation.9 | async-start | bytes 6553600 | tf_op jit(solution)/shard_map/reduce_scatter | solution.py:628
  343.7 244.3 %reduce-scatter.7.cloned.1.call-start = ((), (), s32[]{:S(2)}) async-start(), calls=%async_computation.8 | async-start | bytes 7077888 | tf_op jit(solution)/shard_map/reduce_scatter | solution.py:628
  353.3 26.1 %collective-permute-start.23 = (bf16[256,2048]{1,0:T(8,128)(2,1)S(1)}, bf16[256,2048]{1,0:T(8,128)(2,1)S(1)}, u32[]{:S(2)}, u32[]{:S(2)}) collective-permute-start(bf16[256,2048]{1,0:T(8,128)(2,1)S(1)} %get-tuple-element.176), channel_id=1, source_target_pairs={{0,2},{1,3},{2,0},{3,1},{4,6},{5,7},{6,4},{7,5},{8,10},{9,11},{10,... | collective-permute-start | bytes 3145736 | tf_op jit(solution)/shard_map/ppermute | solution.py:286
  355.0 34.0 %collective-permute-start.26 = (bf16[128,2048]{1,0:T(8,128)(2,1)S(1)}, bf16[128,2048]{1,0:T(8,128)(2,1)S(1)}, u32[]{:S(2)}, u32[]{:S(2)}) collective-permute-start(bf16[128,2048]{1,0:T(8,128)(2,1)S(1)} %get-tuple-element.189), channel_id=1, source_target_pairs={{0,2},{1,3},{2,0},{3,1},{4,6},{5,7},{6,4},{7,5},{8,10},{9,11},{10,... | collective-permute-start | bytes 1572872 | tf_op jit(solution)/shard_map/ppermute | solution.py:286
  356.4 32.6 %collective-permute-start.27 = (bf16[128,2048]{1,0:T(8,128)(2,1)S(1)}, bf16[128,2048]{1,0:T(8,128)(2,1)S(1)}, u32[]{:S(2)}, u32[]{:S(2)}) collective-permute-start(bf16[128,2048]{1,0:T(8,128)(2,1)S(1)} %get-tuple-element.188), channel_id=1, source_target_pairs={{0,1},{1,0},{2,3},{3,2},{4,5},{5,4},{6,7},{7,6},{8,9},{9,8},{10,11... | collective-permute-start | bytes 1572872 | tf_op jit(solution)/shard_map/ppermute | solution.py:286
  357.1 36.6 %collective-permute-start.22 = (bf16[256,2048]{1,0:T(8,128)(2,1)S(1)}, bf16[256,2048]{1,0:T(8,128)(2,1)S(1)}, u32[]{:S(2)}, u32[]{:S(2)}) collective-permute-start(bf16[256,2048]{1,0:T(8,128)(2,1)S(1)} %get-tuple-element.176), channel_id=1, source_target_pairs={{0,1},{1,0},{2,3},{3,2},{4,5},{5,4},{6,7},{7,6},{8,9},{9,8},{10,11... | collective-permute-start | bytes 3145736 | tf_op jit(solution)/shard_map/ppermute | solution.py:286
  411.0 47.3 %collective-permute-start.30 = (bf16[256,1280]{1,0:T(8,128)(2,1)}, bf16[256,1280]{1,0:T(8,128)(2,1)}, u32[]{:S(2)}, u32[]{:S(2)}) collective-permute-start(bf16[256,1280]{1,0:T(8,128)(2,1)} %reduce-scatter.5.cloned.1.call-done.refs_0_), channel_id=1, source_target_pairs={{0,1},{1,0},{2,3},{3,2},{4,5},{5,4},{6,7},{7,6},{8,9},{9,8},{10,11... | collective-permute-start | bytes 1966088 | tf_op jit(solution)/shard_map/ppermute | solution.py:286
  411.7 46.6 %collective-permute-start.31 = (bf16[256,1280]{1,0:T(8,128)(2,1)}, bf16[256,1280]{1,0:T(8,128)(2,1)}, u32[]{:S(2)}, u32[]{:S(2)}) collective-permute-start(bf16[256,1280]{1,0:T(8,128)(2,1)} %reduce-scatter.5.cloned.1.call-done.refs_0_), channel_id=1, source_target_pairs={{0,2},{1,3},{2,0},{3,1},{4,6},{5,7},{6,4},{7,5},{8,10},{9,11},{10,... | collective-permute-start | bytes 1966088 | tf_op jit(solution)/shard_map/ppermute | solution.py:286
  412.9 45.4 %collective-permute-start.32 = (bf16[256,1280]{1,0:T(8,128)(2,1)}, bf16[256,1280]{1,0:T(8,128)(2,1)}, u32[]{:S(2)}, u32[]{:S(2)}) collective-permute-start(bf16[256,1280]{1,0:T(8,128)(2,1)} %reduce-scatter.5.cloned.1.call-done.refs_0_), channel_id=1, source_target_pairs={{0,3},{1,2},{2,1},{3,0},{4,7},{5,6},{6,5},{7,4},{8,11},{9,10},{10,... | collective-permute-start | bytes 1966088 | tf_op jit(solution)/shard_map/ppermute | solution.py:286
  414.5 47.4 %collective-permute-start.28 = (bf16[256,2048]{1,0:T(8,128)(2,1)}, bf16[256,2048]{1,0:T(8,128)(2,1)}, u32[]{:S(2)}, u32[]{:S(2)}) collective-permute-start(bf16[256,2048]{1,0:T(8,128)(2,1)} %get-tuple-element.131), channel_id=1, source_target_pairs={{0,1},{1,0},{2,3},{3,2},{4,5},{5,4},{6,7},{7,6},{8,9},{9,8},{10,11... | collective-permute-start | bytes 3145736 | tf_op jit(solution)/shard_map/ppermute | solution.py:286
  415.2 47.1 %collective-permute-start.29 = (bf16[256,2048]{1,0:T(8,128)(2,1)}, bf16[256,2048]{1,0:T(8,128)(2,1)}, u32[]{:S(2)}, u32[]{:S(2)}) collective-permute-start(bf16[256,2048]{1,0:T(8,128)(2,1)} %get-tuple-element.132), channel_id=1, source_target_pairs={{0,2},{1,3},{2,0},{3,1},{4,6},{5,7},{6,4},{7,5},{8,10},{9,11},{10,... | collective-permute-start | bytes 3145736 | tf_op jit(solution)/shard_map/ppermute | solution.py:286
  473.0 137.8 %reduce-scatter.11.cloned.1.call-start = ((), (), s32[]{:S(2)}) async-start(), calls=%async_computation.10 | async-start | bytes 2359296 | tf_op jit(solution)/shard_map/reduce_scatter | solution.py:628
  504.4 26.2 %collective-permute-start.34 = (bf16[256,2048]{1,0:T(8,128)(2,1)S(1)}, bf16[256,2048]{1,0:T(8,128)(2,1)S(1)}, u32[]{:S(2)}, u32[]{:S(2)}) collective-permute-start(bf16[256,2048]{1,0:T(8,128)(2,1)S(1)} %get-tuple-element.182), channel_id=1, source_target_pairs={{0,1},{1,0},{2,3},{3,2},{4,5},{5,4},{6,7},{7,6},{8,9},{9,8},{10,11... | collective-permute-start | bytes 3145736 | tf_op jit(solution)/shard_map/ppermute | solution.py:286
  505.0 26.1 %collective-permute-start.36 = (bf16[256,2048]{1,0:T(8,128)(2,1)S(1)}, bf16[256,2048]{1,0:T(8,128)(2,1)S(1)}, u32[]{:S(2)}, u32[]{:S(2)}) collective-permute-start(bf16[256,2048]{1,0:T(8,128)(2,1)S(1)} %get-tuple-element.183), channel_id=1, source_target_pairs={{0,2},{1,3},{2,0},{3,1},{4,6},{5,7},{6,4},{7,5},{8,10},{9,11},{10,... | collective-permute-start | bytes 3145736 | tf_op jit(solution)/shard_map/ppermute | solution.py:286
  510.9 41.6 %collective-permute-start.48 = (bf16[256,2560]{1,0:T(8,128)(2,1)}, bf16[256,2560]{1,0:T(8,128)(2,1)S(1)}, u32[]{:S(2)}, u32[]{:S(2)}) collective-permute-start(bf16[256,2560]{1,0:T(8,128)(2,1)} %reduce-scatter.9.cloned.1.call-done.refs_0_), channel_id=1, source_target_pairs={{0,2},{1,3},{2,0},{3,1},{4,6},{5,7},{6,4},{7,5},{8,10},{9,11},{10,... | collective-permute-start | bytes 3932168 | tf_op jit(solution)/shard_map/ppermute | solution.py:286
  511.4 46.6 %collective-permute-start.47 = (bf16[256,2560]{1,0:T(8,128)(2,1)}, bf16[256,2560]{1,0:T(8,128)(2,1)}, u32[]{:S(2)}, u32[]{:S(2)}) collective-permute-start(bf16[256,2560]{1,0:T(8,128)(2,1)} %reduce-scatter.9.cloned.1.call-done.refs_0_), channel_id=1, source_target_pairs={{0,1},{1,0},{2,3},{3,2},{4,5},{5,4},{6,7},{7,6},{8,9},{9,8},{10,11... | collective-permute-start | bytes 3932168 | tf_op jit(solution)/shard_map/ppermute | solution.py:286
  (77 other events, 1068.0 us)
Sparse Core Ops, SparseCore 0:
  11.0 84.7 all-gather.3
  97.4 97.9 all-gather.7
  197.0 54.4 all-gather.5
  314.0 53.1 reduce-scatter.4
  369.9 93.4 reduce-scatter.8
  473.1 70.2 reduce-scatter.6
  546.2 35.4 reduce-scatter.10

commit v3 on v2

--- a/solution.py
+++ b/solution.py
@@ -17,6 +17,7 @@
 PAIR = 2 * DH
 GELU_SCALE = 0.7978845608
 GELU_CUBE = 0.044715
+NO_COST = pl.CostEstimate(flops=0, bytes_accessed=0, transcendentals=0)
 VMEM_BYTES = 56 * 1024 * 1024
 
 
@@ -45,8 +46,24 @@
     return jnp.sum(tile.reshape(tile.shape[0] // 8, 8, tile.shape[1]), axis=0)
 
 
+def query_block(length):
+    return min(length, max(256, 2**20 // length))
+
+
 def whole_place(row, token_rows, place):
     return jnp.bitwise_xor(row // token_rows, place) * token_rows + row % token_rows
+
+
+def bias_offsets(first, block, length, token_rows, place, tile):
+    reach = length - TILE
+    key_place = whole_place(tile * TILE, token_rows, place)
+    group = min(block, token_rows)
+    return [
+        pl.multiple_of(
+            whole_place(first + start, token_rows, place) + (reach - key_place), TILE
+        )
+        for start in range(0, block, group)
+    ], group
 
 
 def forward_kernel(
@@ -69,21 +86,27 @@
     v_ref = qkv_ref.at[:, 2 * PAIR :]
     tiles = length // TILE
     width = 2 * length
-    reach = length - TILE
     place = place_ref[0]
-    key_places = [
-        pl.multiple_of(whole_place(tile * TILE, token_rows, place), TILE) for tile in range(tiles)
-    ]
+    group = min(block, token_rows)
     values_t = jnp.transpose(v_ref[...])
     for head in range(2):
         wide = jnp.broadcast_to(bias_ref[0, head : head + 1, :], (TILE, width))
         strip_ref[head] = pltpu.roll(wide, width - (TILE - 1), 1, stride=1, stride_axis=0)
 
-    def one_block(index, carry):
-        first = pl.multiple_of(index * block, block)
-        query_place = pl.multiple_of(whole_place(first, token_rows, place), block)
+    def one_block(first):
         q_block = q_ref[pl.ds(first, block), :]
-        segment_q = row_ref[:, pl.ds(query_place, block)]
+        segment_q = jnp.concatenate(
+            [
+                row_ref[
+                    :,
+                    pl.ds(
+                        pl.multiple_of(whole_place(first + start, token_rows, place), TILE), group
+                    ),
+                ]
+                for start in range(0, block, group)
+            ],
+            axis=1,
+        )
         outs = []
         for head in range(2):
             q_head = jnp.where(half_lanes(q_block.shape, head), q_block, jnp.zeros_like(q_block))
@@ -91,12 +114,15 @@
             highest = jnp.full((8, block), -jnp.inf, jnp.float32)
             for tile in range(tiles):
                 rows = slice(tile * TILE, (tile + 1) * TILE)
-                offset = pl.multiple_of(query_place + (reach - key_places[tile]), TILE)
-                bias = strip_ref[head, :, pl.ds(offset, block)]
-                segment_k = col_ref[pl.ds(key_places[tile], TILE), :]
+                offsets, _ = bias_offsets(first, block, length, token_rows, place, tile)
+                bias = jnp.concatenate(
+                    [strip_ref[head, :, pl.ds(offset, group)] for offset in offsets], axis=1
+                )
+                key_place = whole_place(tile * TILE, token_rows, place)
+                segment_k = col_ref[pl.ds(pl.multiple_of(key_place, TILE), TILE), :]
                 segment_k = jnp.concatenate([segment_k] * (block // TILE), axis=1)
                 score = jnp.where(segment_k == segment_q, raw[rows, :] + bias, MASKED_SCORE)
-                score_ref[rows, :] = score
+                score_ref[head, rows, :] = score
                 highest = jnp.maximum(
                     highest, jnp.max(score.reshape(TILE // 8, 8, block), axis=0)
                 )
@@ -104,7 +130,7 @@
             total = jnp.zeros((8, block), jnp.float32)
             for tile in range(tiles):
                 rows = slice(tile * TILE, (tile + 1) * TILE)
-                exponent = jnp.exp(score_ref[rows, :] - top)
+                exponent = jnp.exp(score_ref[head, rows, :] - top)
                 total = total + fold_rows(exponent)
                 e_ref[head, rows, pl.ds(first, block)] = exponent.astype(jnp.bfloat16)
             inverse = 1.0 / jnp.sum(total, axis=0, keepdims=True)
@@ -118,14 +144,25 @@
         ctx_ref[pl.ds(first, block), :] = jnp.transpose(jnp.concatenate(outs, axis=0)).astype(
             jnp.bfloat16
         )
+
+    for_blocks(length // block, block, one_block)
+
+
+def for_blocks(count, block, body):
+    if count == 1:
+        body(0)
+        return
+
+    def step(index, carry):
+        body(pl.multiple_of(index * block, block))
         return carry
 
-    lax.fori_loop(0, length // block, one_block, 0)
+    lax.fori_loop(0, count, step, 0)
 
 
 def attention_forward(qkv, place, segment_row, segment_wide, bias_line, heads, token_rows):
     length = qkv.shape[0]
-    block = min(256, token_rows)
+    block = query_block(length)
     pairs = heads // 2
     return pl.pallas_call(
         functools.partial(forward_kernel, block, token_rows),
@@ -149,14 +186,10 @@
         ],
         scratch_shapes=[
             pltpu.VMEM((2, TILE, 2 * length), jnp.float32),
-            pltpu.VMEM((length, block), jnp.float32),
+            pltpu.VMEM((2, length, block), jnp.float32),
         ],
         compiler_params=pltpu.CompilerParams(vmem_limit_bytes=VMEM_BYTES),
-        cost_estimate=pl.CostEstimate(
-            flops=16 * heads * length * length * DH,
-            bytes_accessed=2 * heads * length * length,
-            transcendentals=heads * length * length,
-        ),
+        cost_estimate=NO_COST,
         name="attention_forward",
     )(place, qkv, segment_row, segment_wide, bias_line)
 
@@ -174,25 +207,21 @@
     strip_ref,
     prob_ref,
     low_ref,
-    dk_sum,
-    dv_sum,
+    key_sum,
+    value_sum,
 ):
     length = qkv_ref.shape[0]
     q_ref = qkv_ref.at[:, :PAIR]
     k_ref = qkv_ref.at[:, PAIR : 2 * PAIR]
     v_ref = qkv_ref.at[:, 2 * PAIR :]
     tiles = length // TILE
-    reach = length - TILE
     place = place_ref[0]
-    key_places = [whole_place(tile * TILE, token_rows, place) for tile in range(tiles)]
     keys_t = jnp.transpose(k_ref[...])
     strip_ref[...] = jnp.zeros_like(strip_ref)
-    dk_sum[...] = jnp.zeros_like(dk_sum)
-    dv_sum[...] = jnp.zeros_like(dv_sum)
-
-    def one_block(index, carry):
-        first = pl.multiple_of(index * block, block)
-        query_place = whole_place(first, token_rows, place)
+    key_sum[...] = jnp.zeros_like(key_sum)
+    value_sum[...] = jnp.zeros_like(value_sum)
+
+    def one_block(first):
         q_block = q_ref[pl.ds(first, block), :]
         d_block = d_ref[pl.ds(first, block), :]
         outs = []
@@ -203,40 +232,42 @@
             scale = jnp.transpose(jnp.broadcast_to(inverse, (PAIR, block)))
             d_head = jnp.where(mask, d_block.astype(jnp.float32) * scale, 0.0)
             d_head = d_head.astype(jnp.bfloat16)
-            prob_ref[...] = cols_dot(v_ref[...], d_head)
+            prob_ref[head] = cols_dot(v_ref[...], d_head)
+            value_sum[...] += jnp.dot(
+                e_ref[head, :, pl.ds(first, block)], d_head, preferred_element_type=jnp.float32
+            )
             total = jnp.zeros((8, block), jnp.float32)
             for tile in range(tiles):
                 rows = slice(tile * TILE, (tile + 1) * TILE)
                 exponent = e_ref[head, rows, pl.ds(first, block)].astype(jnp.float32)
-                total = total + fold_rows(exponent * prob_ref[rows, :])
+                total = total + fold_rows(exponent * prob_ref[head, rows, :])
             centre = jnp.sum(total, axis=0, keepdims=True) * inverse
             for tile in range(tiles):
                 rows = slice(tile * TILE, (tile + 1) * TILE)
                 exponent = e_ref[head, rows, pl.ds(first, block)].astype(jnp.float32)
-                grad = exponent * (prob_ref[rows, :] - centre)
-                offset = pl.multiple_of(query_place + (reach - key_places[tile]), TILE)
-                at = pl.ds(offset, block)
-                strip_ref[head, :, at] = strip_ref[head, :, at] + grad
-                low_ref[rows, :] = grad.astype(jnp.bfloat16)
-            dk_sum[...] += jnp.dot(low_ref[...], q_head, preferred_element_type=jnp.float32)
-            dv_sum[...] += jnp.dot(
-                e_ref[head, :, pl.ds(first, block)], d_head, preferred_element_type=jnp.float32
-            )
+                grad = exponent * (prob_ref[head, rows, :] - centre)
+                offsets, group = bias_offsets(first, block, length, token_rows, place, tile)
+                for part, offset in enumerate(offsets):
+                    at = pl.ds(offset, group)
+                    strip_ref[head, :, at] = (
+                        strip_ref[head, :, at] + grad[:, part * group : (part + 1) * group]
+                    )
+                low_ref[head, rows, :] = grad.astype(jnp.bfloat16)
+            key_sum[...] += jnp.dot(low_ref[head], q_head, preferred_element_type=jnp.float32)
             outs.append(
                 jnp.dot(
                     keys_t[head * DH : (head + 1) * DH, :],
-                    low_ref[...],
+                    low_ref[head],
                     preferred_element_type=jnp.float32,
                 )
             )
-        grad_ref[pl.ds(first, block), :PAIR] = jnp.transpose(jnp.concatenate(outs, axis=0)).astype(
-            jnp.bfloat16
-        )
-        return carry
-
-    lax.fori_loop(0, length // block, one_block, 0)
-    grad_ref[:, PAIR : 2 * PAIR] = dk_sum[...].astype(jnp.bfloat16)
-    grad_ref[:, 2 * PAIR :] = dv_sum[...].astype(jnp.bfloat16)
+        grad_ref[pl.ds(first, block), :PAIR] = jnp.transpose(
+            jnp.concatenate(outs, axis=0)
+        ).astype(jnp.bfloat16)
+
+    for_blocks(length // block, block, one_block)
+    grad_ref[:, PAIR : 2 * PAIR] = key_sum[...].astype(jnp.bfloat16)
+    grad_ref[:, 2 * PAIR :] = value_sum[...].astype(jnp.bfloat16)
     for head in range(2):
         turned = strip_ref[head]
         while turned.shape[0] > 1:
@@ -247,7 +278,7 @@
 
 def attention_backward(qkv, place, d, e, inv, heads, token_rows):
     length = qkv.shape[0]
-    block = min(256, token_rows)
+    block = query_block(length)
     pairs = heads // 2
     triple = pl.BlockSpec((length, 3 * PAIR), lambda i: (0, i))
     return pl.pallas_call(
@@ -267,17 +298,13 @@
         ],
         scratch_shapes=[
             pltpu.VMEM((2, TILE, 2 * length), jnp.float32),
-            pltpu.VMEM((length, block), jnp.float32),
-            pltpu.VMEM((length, block), jnp.bfloat16),
+            pltpu.VMEM((2, length, block), jnp.float32),
+            pltpu.VMEM((2, length, block), jnp.bfloat16),
             pltpu.VMEM((length, PAIR), jnp.float32),
             pltpu.VMEM((length, PAIR), jnp.float32),
         ],
         compiler_params=pltpu.CompilerParams(vmem_limit_bytes=VMEM_BYTES),
-        cost_estimate=pl.CostEstimate(
-            flops=40 * heads * length * length * DH,
-            bytes_accessed=2 * heads * length * length,
-            transcendentals=0,
-        ),
+        cost_estimate=NO_COST,
         name="attention_backward",
     )(place, qkv, d, e, inv)
 
@@ -286,63 +313,71 @@
     return lax.ppermute(piece, axis, [(i, i ^ step) for i in range(lax.axis_size(axis))])
 
 
-def gather_pieces(piece, relay=True):
+def gather_begin(piece, relay=True):
     count = lax.axis_size("seq")
-    if count != 4 or not relay:
-        return [[piece]] + [[swap(piece, "seq", step)] for step in range(1, count)]
+    steps = (1, 2) if count == 4 and relay else range(1, count)
+    return tuple(swap(piece, "seq", step) for step in steps)
+
+
+def gather_end(piece, near):
+    if len(near) != 2:
+        return [[part] for part in (piece, *near)]
+    first, second = near
     half = piece.shape[0] // 2
-    first = swap(piece, "seq", 1)
-    second = swap(piece, "seq", 2)
-    third_upper = swap(second[:half], "seq", 1)
-    third_lower = swap(first[half:], "seq", 2)
-    return [[piece], [first], [second], [third_upper, third_lower]]
+    upper = swap(second[:half], "seq", 1)
+    lower = swap(first[half:], "seq", 2)
+    return [[piece], [first], [second], [upper, lower]]
+
+
+def joined(parts):
+    return jnp.concatenate([part for pieces in parts for part in pieces], axis=0)
 
 
 def gather_rows(piece):
-    return jnp.concatenate([part for parts in gather_pieces(piece) for part in parts], axis=0)
-
-
-def scatter_terms(rows, weights):
-    size = rows.shape[0] // lax.axis_size("seq")
-    return cols_dot(rows[size:], weights).astype(jnp.bfloat16)
-
-
-def scatter_begin(terms):
+    return joined(gather_end(piece, gather_begin(piece)))
+
+
+def low_dot(rows, weights):
+    return cols_dot(rows, weights).astype(jnp.bfloat16)
+
+
+def split_terms(terms):
     count = lax.axis_size("seq")
     size = terms.shape[0] // (count - 1)
-    if count != 4:
-        return tuple(
-            swap(terms[k * size : (k + 1) * size], "seq", k + 1) for k in range(count - 1)
-        )
-    upper = swap(terms[2 * size : 2 * size + size // 2], "seq", 1)
-    lower = swap(terms[2 * size + size // 2 :], "seq", 2)
-    return upper, lower
-
-
-def scatter_add(terms, received):
-    if lax.axis_size("seq") != 4:
-        return received
-    size = terms.shape[0] // 3
-    upper, lower = (part.astype(jnp.float32) for part in received)
-    first = terms[:size].astype(jnp.float32) + jnp.pad(lower, ((size // 2, 0), (0, 0)))
-    second = terms[size : 2 * size].astype(jnp.float32) + jnp.pad(upper, ((0, size // 2), (0, 0)))
+    return (terms[: 2 * size], terms[2 * size :]) if count == 4 else (terms, None)
+
+
+def scatter_begin(far):
+    if far is None:
+        return ()
+    half = far.shape[0] // 2
+    return swap(far[:half], "seq", 1), swap(far[half:], "seq", 2)
+
+
+def scatter_add(near, passing):
+    if not passing:
+        size = near.shape[0] // (lax.axis_size("seq") - 1)
+        return tuple(near[start : start + size] for start in range(0, near.shape[0], size))
+    size = near.shape[0] // 2
+    upper, lower = (part.astype(jnp.float32) for part in passing)
+    first = near[:size].astype(jnp.float32) + jnp.pad(lower, ((size // 2, 0), (0, 0)))
+    second = near[size:].astype(jnp.float32) + jnp.pad(upper, ((0, size // 2), (0, 0)))
     return first.astype(jnp.bfloat16), second.astype(jnp.bfloat16)
 
 
 def scatter_end(sums):
-    if lax.axis_size("seq") != 4:
-        return sums
-    return swap(sums[0], "seq", 1), swap(sums[1], "seq", 2)
-
-
-def scatter_own(rows, weights, received):
-    own = cols_dot(rows[: rows.shape[0] // lax.axis_size("seq")], weights)
+    return tuple(swap(part, "seq", k + 1) for k, part in enumerate(sums))
+
+
+def add_parts(own, received):
     return own + sum(part.astype(jnp.float32) for part in received)
 
 
 def scatter_sum(rows, weights):
-    terms = scatter_terms(rows, weights)
-    return scatter_own(rows, weights, scatter_end(scatter_add(terms, scatter_begin(terms))))
+    size = rows.shape[0] // lax.axis_size("seq")
+    near, far = split_terms(low_dot(rows[size:], weights))
+    received = scatter_end(scatter_add(near, scatter_begin(far)))
+    return add_parts(cols_dot(rows[:size], weights), received)
 
 
 def total_sum(values, axis):
@@ -388,11 +423,7 @@
             jax.ShapeDtypeStruct((length, units), jnp.bfloat16),
         ],
         compiler_params=pltpu.CompilerParams(vmem_limit_bytes=VMEM_BYTES),
-        cost_estimate=pl.CostEstimate(
-            flops=4 * length * model_width * units,
-            bytes_accessed=4 * model_width * units + 10 * length * units,
-            transcendentals=length * units,
-        ),
+        cost_estimate=NO_COST,
         name="feed_forward",
     )(rows, weights)
 
@@ -423,11 +454,7 @@
         out_specs=pl.BlockSpec((length, 2 * tile), lambda j: (0, j)),
         out_shape=jax.ShapeDtypeStruct((length, 2 * units), jnp.bfloat16),
         compiler_params=pltpu.CompilerParams(vmem_limit_bytes=VMEM_BYTES),
-        cost_estimate=pl.CostEstimate(
-            flops=2 * length * model_width * units,
-            bytes_accessed=2 * model_width * units + 12 * length * units,
-            transcendentals=0,
-        ),
+        cost_estimate=NO_COST,
         name="feed_forward_back",
     )(grad_rows, weights, gelu, slope)
 
@@ -455,9 +482,7 @@
         out_specs=[pl.BlockSpec((block, count * size), lambda i: (i, 0)) for size in widths],
         out_shape=[jax.ShapeDtypeStruct((rows, count * size), jnp.float32) for size in widths],
         compiler_params=pltpu.CompilerParams(vmem_limit_bytes=VMEM_BYTES),
-        cost_estimate=pl.CostEstimate(
-            flops=0, bytes_accessed=6 * rows * count * width, transcendentals=0
-        ),
+        cost_estimate=NO_COST,
         name="place_columns",
     )(place, *pieces)
 
@@ -486,7 +511,7 @@
         ),
         out_shape=jax.ShapeDtypeStruct((rows, width), weights[0].dtype),
         compiler_params=pltpu.CompilerParams(vmem_limit_bytes=VMEM_BYTES),
-        cost_estimate=pl.CostEstimate(flops=0, bytes_accessed=4 * rows * width, transcendentals=0),
+        cost_estimate=NO_COST,
         name="take_columns",
     )(place, *weights)
 
@@ -517,7 +542,7 @@
         ),
         out_shape=[half, half],
         compiler_params=pltpu.CompilerParams(vmem_limit_bytes=VMEM_BYTES),
-        cost_estimate=pl.CostEstimate(flops=0, bytes_accessed=4 * length * width, transcendentals=0),
+        cost_estimate=NO_COST,
         name="split_columns",
     )(core, rows, rows)
 
@@ -581,8 +606,6 @@
     )
     attn_w = gather_weights(attn_part)
     gains = lax.all_gather(jnp.stack([gain_attn, gain_ffn]), "fsdp", axis=1, tiled=True)
-    attn_gain = gains[0].astype(jnp.float32)
-    ffn_gain = gains[1].astype(jnp.float32)
     qkv_w = attn_w[:, : 3 * column_count]
     output_w = attn_w[:, 3 * column_count :]
 
@@ -600,7 +623,11 @@
     normed_attn = stream * scale_attn
     upstream = out_grad[0].astype(jnp.float32)
 
-    stream_rows = gather_rows(tokens[0])
+    stream_near = gather_begin(tokens[0])
+    stream_near, gains = both(stream_near, gains)
+    attn_gain = gains[0].astype(jnp.float32)
+    ffn_gain = gains[1].astype(jnp.float32)
+    stream_rows = joined(gather_end(tokens[0], stream_near))
     gate_up_part = take_columns(place, (w_gate, w_up), unit_moves, [unit_count] * 2)
     gate_up_part, stream_rows = both(gate_up_part, stream_rows)
     gate_up_w = gather_weights(gate_up_part)
@@ -633,8 +660,6 @@
             axis_index_groups=axis_index_groups,
         )
 
-    ff_grad_own, ff_grad_other = split_columns(ff_grad_rows, core, fsdp_count)
-    ff_grad_own, ff_grad_other, attn_out = both(ff_grad_own, ff_grad_other, attn_out)
     resid = stream + attn_out
     scale_ffn = lax.rsqrt(jnp.mean(resid * resid, axis=-1, keepdims=True) + EPSILON)
     normed_ffn = resid * scale_ffn
@@ -642,63 +667,81 @@
 
     hidden, gelu, slope = feed_forward(ffn_rows, gate_up_w, tile)
 
-    down_away = rows_dot(ff_grad_other, hidden).astype(jnp.bfloat16)
-    down_away, hidden = both(down_away, hidden)
-    down_added = swap(down_away, "fsdp", 1)
-    ff_away = scatter_terms(hidden, down_w)
-    ff_away, gelu = both(ff_away, gelu)
-    ff_far = scatter_begin(ff_away)
+    down_grad = rows_dot(ff_grad_rows, hidden).astype(jnp.bfloat16)
+    ffn_own, ffn_other = split_columns(ffn_rows, core, fsdp_count)
+    down_owned = scatter_grads(down_grad)
+    down_grad, hidden, gelu, ffn_own, ffn_other = both(down_grad, hidden, gelu, ffn_own, ffn_other)
+    away = row_length // seq_count
+    passed = 3 * away if seq_count == 4 else row_length
+    ff_far = low_dot(hidden[passed:], down_w) if seq_count == 4 else None
+    ff_far, hidden, gelu = both(ff_far, hidden, gelu)
+    ff_passing = scatter_begin(ff_far)
     unit_grad = feed_forward_back(ff_grad_rows, down_w, gelu, slope, tile)
-    ffn_in_away = scatter_terms(unit_grad, gate_up_w)
-    ffn_in_away, hidden, unit_grad = both(ffn_in_away, hidden, unit_grad)
-    ffn_in_far = scatter_begin(ffn_in_away)
-    down_grad = add_low(rows_dot(ff_grad_own, hidden), down_added)
-    ffn_own, ffn_other = split_columns(ffn_rows, core, fsdp_count)
-    down_grad, unit_grad = both(down_grad, unit_grad)
-    down_owned = scatter_grads(down_grad, groups)
+    unit_terms = low_dot(unit_grad[away:], gate_up_w)
+    unit_terms, unit_grad, ff_passing = both(unit_terms, unit_grad, ff_passing)
+    unit_near, unit_far = split_terms(unit_terms)
+    unit_passing = scatter_begin(unit_far)
     gate_up_away = rows_dot(ffn_other, unit_grad).astype(jnp.bfloat16)
-    gate_up_away, *ffn_in_far = both(gate_up_away, *ffn_in_far)
+    gate_up_away, unit_grad, unit_passing = both(gate_up_away, unit_grad, unit_passing)
+    unit_sums = scatter_add(unit_near, unit_passing)
+    unit_sums, unit_grad, gate_up_away = both(unit_sums, unit_grad, gate_up_away)
+    unit_parts = scatter_end(unit_sums)
     gate_up_added = swap(gate_up_away, "fsdp", 1)
-    ffn_in_sums = scatter_add(ffn_in_away, ffn_in_far)
-    *ffn_in_sums, unit_grad = both(*ffn_in_sums, unit_grad)
-    ffn_in_parts = scatter_end(ffn_in_sums)
     gate_up_grad = add_low(rows_dot(ffn_own, unit_grad), gate_up_added)
-    gate_up_grad, unit_grad, *ffn_in_parts = both(gate_up_grad, unit_grad, *ffn_in_parts)
+    ffn_in_own = cols_dot(unit_grad[:away], gate_up_w)
+    ffn_in_own, gate_up_grad, unit_parts = both(ffn_in_own, gate_up_grad, unit_parts)
     gate_up_owned = scatter_grads(gate_up_grad, groups)
-    ffn_in_grad = scatter_own(unit_grad, gate_up_w, ffn_in_parts)
-
-    gain_ffn_part = jnp.sum(ffn_in_grad * normed_ffn, axis=0)
+    ffn_in_grad = add_parts(ffn_in_own, unit_parts)
+
     resid_grad = upstream + norm_back(ffn_in_grad * ffn_gain, normed_ffn, scale_ffn)
-    attn_grad_rows = gather_rows(resid_grad.astype(jnp.bfloat16))
-    ff_sums = scatter_add(ff_away, ff_far)
-    attn_grad_rows, *ff_sums = both(attn_grad_rows, *ff_sums)
+    attn_grad = resid_grad.astype(jnp.bfloat16)
+    attn_grad, hidden, down_owned = both(attn_grad, hidden, down_owned)
+    attn_grad_rows = gather_rows(attn_grad)
+    ff_near = low_dot(hidden[away:passed], down_w)
+    ff_sums = scatter_add(ff_near, ff_passing)
+    attn_grad_rows, ff_sums, down_owned = both(attn_grad_rows, ff_sums, down_owned)
     context_grad = jnp.dot(
         attn_grad_rows, output_w, preferred_element_type=jnp.float32
     ).astype(jnp.bfloat16)
-    context_grad, down_owned, *ff_sums = both(context_grad, down_owned, *ff_sums)
     ff_parts = scatter_end(ff_sums)
-    down_pieces = gather_pieces(down_owned, relay=False)
+    down_near = gather_begin(down_owned, relay=False)
     qkv_grad, line_grad = attention_backward(
         qkv, place, context_grad, exponents, inverse, head_count, token_rows
     )
-    qkv_grad, ff_parts, down_pieces = both(qkv_grad, ff_parts, down_pieces)
     attn_grads = rows_dot(attn_rows, qkv_grad).astype(jnp.bfloat16)
-    attn_grads, context, qkv_grad = both(attn_grads, context, qkv_grad)
+    attn_grads, context, qkv_grad, ff_parts, down_near, attn_grad_rows, gate_up_owned = both(
+        attn_grads, context, qkv_grad, ff_parts, down_near, attn_grad_rows, gate_up_owned
+    )
     attn_owned = scatter_grads(attn_grads)
-    output_grad = rows_dot(attn_grad_rows, context).astype(jnp.bfloat16)
-    output_grad, qkv_grad, hidden = both(output_grad, qkv_grad, hidden)
-    output_owned = scatter_grads(output_grad)
-    attn_in_away = scatter_terms(qkv_grad, qkv_w)
-    attn_in_away, gate_up_owned, qkv_grad = both(attn_in_away, gate_up_owned, qkv_grad)
-    attn_in_far = scatter_begin(attn_in_away)
-    gate_up_pieces = gather_pieces(gate_up_owned)
-    attn_in_parts = scatter_end(scatter_add(attn_in_away, attn_in_far))
-    attn_in_grad = scatter_own(qkv_grad, qkv_w, attn_in_parts)
+    gate_up_near = gather_begin(gate_up_owned)
+    output_own, output_other = split_columns(attn_grad_rows, core, fsdp_count)
+    output_away = rows_dot(output_other, context).astype(jnp.bfloat16)
+    qkv_terms = low_dot(qkv_grad[away:], qkv_w)
+    qkv_terms, qkv_grad, output_away, output_own, down_near, hidden = both(
+        qkv_terms, qkv_grad, output_away, output_own, down_near, hidden
+    )
+    qkv_near, qkv_far = split_terms(qkv_terms)
+    qkv_passing = scatter_begin(qkv_far)
+    output_added = swap(output_away, "fsdp", 1)
+    attn_in_own = cols_dot(qkv_grad[:away], qkv_w)
+    output_grad = add_low(rows_dot(output_own, context), output_added)
+    attn_in_own, output_grad, qkv_passing, hidden, ffn_in_grad, gate_up_near, down_near = both(
+        attn_in_own, output_grad, qkv_passing, hidden, ffn_in_grad, gate_up_near, down_near
+    )
+    output_owned = scatter_grads(output_grad, groups)
+    qkv_sums = scatter_add(qkv_near, qkv_passing)
+    qkv_sums, gate_up_near, down_near = both(qkv_sums, gate_up_near, down_near)
+    attn_in_parts = scatter_end(qkv_sums)
+    gate_up_pieces = gather_end(gate_up_owned, gate_up_near)
+    down_pieces = gather_end(down_owned, down_near)
+    ff_out = add_parts(cols_dot(hidden[:away], down_w), ff_parts)
+    result = resid + ff_out
+    gain_ffn_part = jnp.sum(ffn_in_grad * normed_ffn, axis=0)
+    attn_owned, result, gain_ffn_part = both(attn_owned, result, gain_ffn_part)
+    attn_near = gather_begin(attn_owned)
+    attn_in_grad = add_parts(attn_in_own, attn_in_parts)
     gain_attn_part = jnp.sum(attn_in_grad * normed_attn, axis=0)
     stream_grad = resid_grad + norm_back(attn_in_grad * attn_gain, normed_attn, scale_attn)
-    ff_out = scatter_own(hidden, down_w, ff_parts)
-    result = resid + ff_out
-
     (down_out,) = place_columns(down_pieces, place, [(0, 0, 0, unit_count)], [unit_count])
     gate_out, up_out = place_columns(gate_up_pieces, place, unit_moves, [unit_count] * 2)
 
@@ -721,17 +764,24 @@
     packed = jnp.concatenate(
         [gain_attn_part, gain_ffn_part, full_table.reshape(-1), jnp.pad(stat_terms, (0, 124))]
     ).reshape(-1, 128)
-    summed = total_sum(total_sum(packed, "seq"), "fsdp").reshape(-1)
-    attn_owned, summed, result, stream_grad, down_out, gate_out, up_out = both(
-        attn_owned, summed, result, stream_grad, down_out, gate_out, up_out
-    )
-    attn_pieces = gather_pieces(attn_owned)
+    summed = total_sum(packed, "fsdp")
+    attn_near, stream_grad, gain_attn_part, down_out, output_owned = both(
+        attn_near, stream_grad, gain_attn_part, down_out, output_owned
+    )
+    output_near = gather_begin(output_owned, relay=False)
+    attn_pieces = gather_end(attn_owned, attn_near)
+    summed, attn_pieces, output_near, gate_out, up_out = both(
+        summed, attn_pieces, output_near, gate_out, up_out
+    )
+    summed = total_sum(summed, "seq").reshape(-1)
     query_out, key_out, value_out = place_columns(
         attn_pieces, place, qkv_moves[:-1], [column_count] * 3
     )
-    output_owned, attn_pieces = both(output_owned, attn_pieces)
     (output_out,) = place_columns(
-        gather_pieces(output_owned), place, [(0, 0, 0, column_count)], [column_count]
+        gather_end(output_owned, output_near),
+        place,
+        [(0, 0, 0, column_count)],
+        [column_count],
     )
     table_end = 2 * model_width + rel_table.size
     stat_totals = summed[table_end : table_end + 4]

time: 654 us -> 588 us (0.90)
  waiting for transfers between devices: 211 us -> 182 us
  Pallas kernels: 145 us -> 120 us
  matrix products: 126 us -> 112 us
    ppermute x59 -> x58, waiting for transfers between devices: 211 us -> 177 us  [swap(): lax.ppermute(piece, axis, [(i, i ^ step) for i in range(lax.axis_size(axi...]
    pallas_call x1, Pallas kernels: 35.1 us -> 22.1 us  [attention_forward(): pl.pallas_call(functools.partial(forward_kernel, block, token_rows), grid...]
    pallas_call x1, Pallas kernels: 41.9 us -> 28.9 us  [attention_backward(): pl.pallas_call(functools.partial(backward_kernel, block, token_rows), gri...]
    dot_general x8 -> x9, matrix products: 57.2 us -> 48.4 us  [cols_dot(): lax.dot_general(left, right, (((1,), (1,)), ((), ())), preferred_element_...]
    reduce_sum x0 -> x2, other arithmetic: none -> 6.68 us  [the longest x1 3.79 us: on_device(): gain_attn_part = jnp.sum(attn_in_grad * normed_attn, axis=0)]
    ppermute x59 -> x58, starting transfers between devices: 66.3 us -> 60.2 us  [swap(): lax.ppermute(piece, axis, [(i, i ^ step) for i in range(lax.axis_size(axi...]
    unnamed x86 -> x101, local copies, waits for them, and re-layouts: 22.1 us -> 23.7 us
  transfers between devices with their start and end apart: 66 -> 65, of which waited for: 35 -> 36; matrix products, arithmetic and copies ran while one was open for 28% -> 32% of each run, Pallas kernels for 21% -> 20%
where the time goes in v3:
time: 588 us; the launch traced here: 582 us
  waiting for transfers between devices  182 us (31%)
  Pallas kernels  120 us (20%)
  matrix products  112 us (19%)
  starting transfers between devices  60.9 us (10%)
  local copies, waits for them, and re-layouts  42.9 us (7%)
  other arithmetic  35.7 us (6%)
  between operations  15.9 us (3%)
  blocking collectives  12.1 us (2%)
    ppermute x58, waiting for transfers between devices, swap(): lax.ppermute(piece, axis, [(i, i ^ step) for i in range(lax.axis_size(axi...  177 us
    ppermute x58, starting transfers between devices, swap(): lax.ppermute(piece, axis, [(i, i ^ step) for i in range(lax.axis_size(axi...  60.2 us
    dot_general x9, matrix products, cols_dot(): lax.dot_general(left, right, (((1,), (1,)), ((), ())), preferred_element_...  48.4 us
    dot_general x6, matrix products, rows_dot(): lax.dot_general(left, right, (((0,), (0,)), ((), ())), preferred_element_...  45.1 us
    pallas_call x1, Pallas kernels, attention_backward(): pl.pallas_call(functools.partial(backward_kernel, block, token_rows), gri...  28.9 us
    unnamed x101, local copies, waits for them, and re-layouts  23.7 us
    pallas_call x1, Pallas kernels, attention_forward(): pl.pallas_call(functools.partial(forward_kernel, block, token_rows), grid...  22.1 us
    pallas_call x4, Pallas kernels, place_columns(): pl.pallas_call(functools.partial(place_kernel, moves, count, widths), gri...  20.9 us
  transfers between devices with their start and end apart: 65, of which 36 were waited for; matrix products, arithmetic and copies ran while one was open for 32% of the time, Pallas kernels for 20%

profile of v3, /device:TPU:0, one launch (start us, length us, event | category | flops | bytes accessed | tf_op | source)
XLA Modules:
  0.0 581.5 jit_solution(325019974712757942)
XLA Ops:
  15.5 12.1 %all_gather.12 = bf16[2,2048]{1,0:T(2,128)(2,1)S(1)} all-gather(bf16[2,256]{1,0:T(2,128)(2,1)S(1)} %pad_maximum_fusion.2), channel_id=1, replica_groups=mesh['fsdp'=8,'seq'=4] {'fsdp'}, dimensions={1}, use_global_device_ids=true | all-gather | bytes 9216 | tf_op jit(solution)/shard_map/all_gather | solution.py:608
  27.6 9.7 %collective-permute-done.1 = bf16[256,2048]{1,0:T(8,128)(2,1)S(1)} collective-permute-done((bf16[256,2048]{1,0:T(8,128)(2,1)}, bf16[256,2048]{1,0:T(8,128)(2,1)S(1)}, u32[]{:S(2)}, u32[]{:S(2)}) %collective-permute-start.1) | collective-permute-done | bytes 1048608 | tf_op jit(solution)/shard_map/ppermute | solution.py:313
  53.6 6.9 %collective-permute-done.3 = bf16[128,2048]{1,0:T(8,128)(2,1)S(1)} collective-permute-done((bf16[128,2048]{1,0:T(8,128)(2,1)S(1)}, bf16[128,2048]{1,0:T(8,128)(2,1)S(1)}, u32[]{:S(2)}, u32[]{:S(2)}) %collective-permute-start.3) | collective-permute-done | bytes 524320 | tf_op jit(solution)/shard_map/ppermute | solution.py:313
  66.7 17.9 %collective-permute-done.5 = bf16[256,2048]{1,0:T(8,128)(2,1)} collective-permute-done((bf16[256,2048]{1,0:T(8,128)(2,1)}, bf16[256,2048]{1,0:T(8,128)(2,1)}, u32[]{:S(2)}, u32[]{:S(2)}) %collective-permute-start.5) | collective-permute-done | bytes 1048608 | tf_op jit(solution)/shard_map/ppermute | solution.py:313
  102.0 12.0 %fusion.11.qkv_ref = bf16[1024,1536]{1,0:T(8,128)(2,1)} fusion(bf16[1024,2048]{1,0:T(8,128)(2,1)} %fusion.2, bf16[2048,2048]{1,0:T(8,128)(2,1)} %all-gather.4.cloned.1.call-done), kind=kOutput, calls=%fused_computation.17 | convolution fusion | flops 6444023808 | bytes 13631488 | tf_op jit(solution)/shard_map/dot_general | solution.py:640
  117.7 22.1 %attention_forward.1 = (bf16[1024,512]{1,0:T(8,128)(2,1)}, bf16[8,1024,1024]{2,1,0:T(8,128)(2,1)}, f32[8,1,1024]{2,1,0:T(1,128)}) custom-call(s32[1]{0:T(128)} %bitcast.place_ref, bf16[1024,1536]{1,0:T(8,128)(2,1)} %fusion.11.qkv_ref, s32[1,1024]{1,0:T(1,128)} %row_ref.1, s32[1024,128]{1,0:T(8,128)} %broadcast_in_dim.11.col_ref, f32[4,2,2048]{2,1,0:T(2,128)} %reshape.92.bias_ref), custom_call_target="tpu_custom_call" | custom-call | tf_op jit(solution)/shard_map/attention_forward/pallas_call | solution.py:167
  162.0 15.5 %collective-permute-done.9 = bf16[256,2048]{1,0:T(8,128)(2,1)S(1)} collective-permute-done((bf16[256,2048]{1,0:T(8,128)(2,1)S(1)}, bf16[256,2048]{1,0:T(8,128)(2,1)S(1)}, u32[]{:S(2)}, u32[]{:S(2)}) %collective-permute-start.9) | collective-permute-done | bytes 1048608 | tf_op jit(solution)/shard_map/ppermute | solution.py:313
  182.4 17.6 %collective-permute-done.13 = bf16[256,2048]{1,0:T(8,128)(2,1)S(1)} collective-permute-done((bf16[256,2048]{1,0:T(8,128)(2,1)}, bf16[256,2048]{1,0:T(8,128)(2,1)S(1)}, u32[]{:S(2)}, u32[]{:S(2)}) %collective-permute-start.13) | collective-permute-done | bytes 1048608 | tf_op jit(solution)/shard_map/ppermute | solution.py:313
  221.0 18.2 %feed_forward.1 = (bf16[1024,1280]{1,0:T(8,128)(2,1)}, bf16[1024,1280]{1,0:T(8,128)(2,1)}, bf16[1024,1280]{1,0:T(8,128)(2,1)}) custom-call(bf16[1024,2048]{1,0:T(8,128)(2,1)} %constant_dynamic-update-slice_fusion.10.x_ref.own_in.other_in, bf16[2048,2560]{1,0:T(8,128)(2,1)} %all-gather.8.cloned.1.call-done.w_ref), custom_call_target="tpu_custom_call" | custom-call | tf_op jit(solution)/shard_map/feed_forward/pallas_call | solution.py:412
  239.2 9.8 %convolution_convert_fusion.1 = bf16[2048,1280]{1,0:T(8,128)(2,1)} fusion(bf16[1024,2048]{1,0:T(8,128)(2,1)} %constant_dynamic-update-slice_fusion.5.d_ref, bf16[1024,1280]{1,0:T(8,128)(2,1)} %get-tuple-element.190), kind=kOutput, calls=%fused_computation.7 | convolution fusion | flops 5371330560 | bytes 12058624 | tf_op jit(solution)/shard_map/dot_general | solution.py:25
  260.0 12.3 %feed_forward_back.1 = bf16[1024,2560]{1,0:T(8,128)(2,1)} custom-call(bf16[1024,2048]{1,0:T(8,128)(2,1)} %constant_dynamic-update-slice_fusion.5.d_ref, bf16[2048,1280]{1,0:T(8,128)(2,1)} %all-gather.6.cloned.1.call-done.w_ref, bf16[1024,1280]{1,0:T(8,128)(2,1)} %get-tuple-element.140.gelu_ref, bf16[1024,1280]{1,0:T(8,128)(2,1)} %get-tuple-element.141.slope_ref), custom_call_target="tpu_custom_call" | custom-call | tf_op jit(solution)/shard_map/feed_forward_back/pallas_call | solution.py:445
  272.3 12.4 %fusion.14 = bf16[768,2048]{1,0:T(8,128)(2,1)S(1)} fusion(bf16[2048,2560]{1,0:T(8,128)(2,1)} %all-gather.8.cloned.1.call-done.w_ref, bf16[1024,2560]{1,0:T(8,128)(2,1)} %feed_forward_back.1), kind=kOutput, calls=%fused_computation.19 | convolution fusion | flops 8054636544 | bytes 17563648 | tf_op jit(solution)/shard_map/dot_general | solution.py:31
  288.1 9.6 %convolution_convert_fusion.2 = bf16[1024,2560]{1,0:T(8,128)(2,1)} fusion(bf16[1024,1024]{1,0:T(8,128)(2,1)} %get-tuple-element.144, bf16[1024,2560]{1,0:T(8,128)(2,1)S(1)} %copy-done.11), kind=kOutput, calls=%fused_computation.8 | convolution fusion | flops 5371330560 | bytes 12582912 | tf_op jit(solution)/shard_map/dot_general | solution.py:25
  311.6 9.9 %add_convert_fusion = bf16[1024,2560]{1,0:T(8,128)(2,1)} fusion(bf16[1024,2560]{1,0:T(8,128)(2,1)} %collective-permute-done.20, bf16[1024,1024]{1,0:T(8,128)(2,1)} %get-tuple-element.151, bf16[1024,2560]{1,0:T(8,128)(2,1)S(1)} %copy-done.11), kind=kOutput, calls=%fused_computation.2 | convolution fusion | flops 5376573440 | bytes 17825792 | tf_op jit(solution)/shard_map/dot_general | solution.py:25
  321.5 7.0 %collective-permute-done.21 = bf16[256,2048]{1,0:T(8,128)(2,1)} collective-permute-done((bf16[256,2048]{1,0:T(8,128)(2,1)}, bf16[256,2048]{1,0:T(8,128)(2,1)}, u32[]{:S(2)}, u32[]{:S(2)}) %collective-permute-start.21) | collective-permute-done | bytes 1048608 | tf_op jit(solution)/shard_map/ppermute | solution.py:313
  345.0 14.5 %collective-permute-done.24 = bf16[256,2048]{1,0:T(8,128)(2,1)S(1)} collective-permute-done((bf16[256,2048]{1,0:T(8,128)(2,1)}, bf16[256,2048]{1,0:T(8,128)(2,1)S(1)}, u32[]{:S(2)}, u32[]{:S(2)}) %collective-permute-start.24) | collective-permute-done | bytes 1048608 | tf_op jit(solution)/shard_map/ppermute | solution.py:313
  362.6 9.5 %collective-permute-done.25 = bf16[128,2048]{1,0:T(8,128)(2,1)S(1)} collective-permute-done((bf16[128,2048]{1,0:T(8,128)(2,1)S(1)}, bf16[128,2048]{1,0:T(8,128)(2,1)S(1)}, u32[]{:S(2)}, u32[]{:S(2)}) %collective-permute-start.25) | collective-permute-done | bytes 524320 | tf_op jit(solution)/shard_map/ppermute | solution.py:313
  383.9 28.9 %attention_backward.1 = (bf16[1024,1536]{1,0:T(8,128)(2,1)}, f32[4,2,2048]{2,1,0:T(2,128)}) custom-call(s32[1]{0:T(128)} %bitcast.place_ref, bf16[1024,1536]{1,0:T(8,128)(2,1)} %fusion.11.qkv_ref, bf16[1024,512]{1,0:T(8,128)(2,1)} %fusion.35.d_ref, bf16[8,1024,1024]{2,1,0:T(8,128)(2,1)} %get-tuple-element.165.e_ref, f32[8,1,1024]{2,1,0:T(1,128)} %get-tuple-element.166.inv_ref), custom_call_target="tpu_custom_call" | custom-call | tf_op jit(solution)/shard_map/attention_backward/pallas_call | solution.py:284
  412.8 10.6 %convolution_convert_fusion = bf16[2048,1536]{1,0:T(8,128)(2,1)} fusion(bf16[1024,2048]{1,0:T(8,128)(2,1)S(1)} %copy-done.12, bf16[1024,1536]{1,0:T(8,128)(2,1)} %get-tuple-element.181), kind=kOutput, calls=%fused_computation.6 | convolution fusion | flops 6445596672 | bytes 13631488 | tf_op jit(solution)/shard_map/dot_general | solution.py:25
  451.5 16.6 %collective-permute-done.34 = bf16[128,2048]{1,0:T(8,128)(2,1)S(1)} collective-permute-done((bf16[128,2048]{1,0:T(8,128)(2,1)}, bf16[128,2048]{1,0:T(8,128)(2,1)S(1)}, u32[]{:S(2)}, u32[]{:S(2)}) %collective-permute-start.34) | collective-permute-done | bytes 524320 | tf_op jit(solution)/shard_map/ppermute | solution.py:313
  480.9 7.0 %multiply_reduce_fusion = (f32[256]{0:T(256)S(1)}, f32[256,2048]{1,0:T(8,128)}, f32[2048]{0:T(1024)S(1)}) fusion(f32[256,2048]{1,0:T(8,128)S(1)} %get-tuple-element.246, f32[256,2048]{1,0:T(8,128)} %copy-done.2, f32[256]{0:T(256)S(1)} %add_rsqrt_fusion.2, bf16[256,2048]{1,0:T(8,128)(2,1)} %collective-permute-done.28, ...), kind=kOutput, calls=%fused_computation.37 | convolution fusion | flops 1347417856 | bytes 14297088 | tf_op jit(solution)/shard_map/dot_general | solution.py:31
  519.0 9.2 %collective-permute-done.38.refs_2_ = bf16[256,1536]{1,0:T(8,128)(2,1)S(1)} collective-permute-done((bf16[256,1536]{1,0:T(8,128)(2,1)}, bf16[256,1536]{1,0:T(8,128)(2,1)S(1)}, u32[]{:S(2)}, u32[]{:S(2)}) %collective-permute-start.38) | collective-permute-done | bytes 786464 | tf_op jit(solution)/shard_map/ppermute | solution.py:313
  542.2 6.9 %place_columns.5 = (f32[256,5120]{1,0:T(8,128)}, f32[256,5120]{1,0:T(8,128)}) custom-call(s32[1]{0:T(128)} %bitcast.place_ref, bf16[256,2560]{1,0:T(8,128)(2,1)} %reduce-scatter.7.cloned.1.call-done.refs_0_, bf16[256,2560]{1,0:T(8,128)(2,1)} %collective-permute-done.35.refs_1_, bf16[256,2560]{1,0:T(8,128)(2,1)} %collective-permute-done.36.refs_2_, ...), custom_call_target="tpu_custom_call" | custom-call | tf_op jit(solution)/shard_map/place_columns/pallas_call | solution.py:477
  550.0 7.5 %collective-permute-done.48 = bf16[128,1536]{1,0:T(8,128)(2,1)S(1)} collective-permute-done((bf16[128,1536]{1,0:T(8,128)(2,1)S(1)}, bf16[128,1536]{1,0:T(8,128)(2,1)S(1)}, u32[]{:S(2)}, u32[]{:S(2)}) %collective-permute-start.48) | collective-permute-done | bytes 393248 | tf_op jit(solution)/shard_map/ppermute | solution.py:313
  (311 shorter events, 261.9 us)
Async XLA Ops:
  7.2 94.8 %all-gather.4.cloned.1.call-start = ((), (), s32[]{:S(2)}) async-start(), calls=%async_computation.4 | async-start | bytes 9437184 | tf_op jit(solution)/shard_map/all_gather | solution.py:592
  10.9 210.1 %all-gather.8.cloned.1.call-start = ((), (), s32[]{:S(2)}) async-start(), calls=%async_computation.6 | async-start | bytes 11796480 | tf_op jit(solution)/shard_map/all_gather | solution.py:592
  10.9 26.4 %collective-permute-start.1 = (bf16[256,2048]{1,0:T(8,128)(2,1)}, bf16[256,2048]{1,0:T(8,128)(2,1)S(1)}, u32[]{:S(2)}, u32[]{:S(2)}) collective-permute-start(bf16[256,2048]{1,0:T(8,128)(2,1)} %bitcast.56), channel_id=1, source_target_pairs={{0,2},{1,3},{2,0},{3,1},{4,6},{5,7},{6,4},{7,5},{8,10},{9,11},{10,... | collective-permute-start | bytes 3145736 | tf_op jit(solution)/shard_map/ppermute | solution.py:313
  61.4 191.2 %all-gather.6.cloned.1.call-start = ((), (), s32[]{:S(2)}) async-start(), calls=%async_computation.5 | async-start | bytes 5898240 | tf_op jit(solution)/shard_map/all_gather | solution.py:592
  114.0 220.7 %reduce-scatter.5.cloned.1.call-start = ((), (), s32[]{:S(2)}) async-start(), calls=%async_computation.7 | async-start | bytes 5898240 | tf_op jit(solution)/shard_map/reduce_scatter | solution.py:655
  249.0 176.2 %reduce-scatter.7.cloned.1.call-start = ((), (), s32[]{:S(2)}) async-start(), calls=%async_computation.8 | async-start | bytes 6553600 | tf_op jit(solution)/shard_map/reduce_scatter | solution.py:655
  256.9 27.8 %collective-permute-start.17 = (bf16[128,2048]{1,0:T(8,128)(2,1)S(1)}, bf16[128,2048]{1,0:T(8,128)(2,1)S(1)}, u32[]{:S(2)}, u32[]{:S(2)}) collective-permute-start(bf16[128,2048]{1,0:T(8,128)(2,1)S(1)} %get-tuple-element.268), channel_id=1, source_target_pairs={{0,2},{1,3},{2,0},{3,1},{4,6},{5,7},{6,4},{7,5},{8,10},{9,11},{10,... | collective-permute-start | bytes 1572872 | tf_op jit(solution)/shard_map/ppermute | solution.py:313
  258.5 26.2 %collective-permute-start.16 = (bf16[128,2048]{1,0:T(8,128)(2,1)S(1)}, bf16[128,2048]{1,0:T(8,128)(2,1)S(1)}, u32[]{:S(2)}, u32[]{:S(2)}) collective-permute-start(bf16[128,2048]{1,0:T(8,128)(2,1)S(1)} %get-tuple-element.269), channel_id=1, source_target_pairs={{0,1},{1,0},{2,3},{3,2},{4,5},{5,4},{6,7},{7,6},{8,9},{9,8},{10,11... | collective-permute-start | bytes 1572872 | tf_op jit(solution)/shard_map/ppermute | solution.py:313
  302.6 25.9 %collective-permute-start.21 = (bf16[256,2048]{1,0:T(8,128)(2,1)}, bf16[256,2048]{1,0:T(8,128)(2,1)}, u32[]{:S(2)}, u32[]{:S(2)}) collective-permute-start(bf16[256,2048]{1,0:T(8,128)(2,1)} %get-tuple-element.153), channel_id=1, source_target_pairs={{0,1},{1,0},{2,3},{3,2},{4,5},{5,4},{6,7},{7,6},{8,9},{9,8},{10,11... | collective-permute-start | bytes 3145736 | tf_op jit(solution)/shard_map/ppermute | solution.py:313
  328.7 165.2 %reduce-scatter.9.cloned.1.call-start = ((), (), s32[]{:S(2)}) async-start(), calls=%async_computation.9 | async-start | bytes 7077888 | tf_op jit(solution)/shard_map/reduce_scatter | solution.py:655
  373.4 50.0 %collective-permute-start.31 = (bf16[256,1280]{1,0:T(8,128)(2,1)S(1)}, bf16[256,1280]{1,0:T(8,128)(2,1)}, u32[]{:S(2)}, u32[]{:S(2)}) collective-permute-start(bf16[256,1280]{1,0:T(8,128)(2,1)S(1)} %copy-done.22), channel_id=1, source_target_pairs={{0,3},{1,2},{2,1},{3,0},{4,7},{5,6},{6,5},{7,4},{8,11},{9,10},{10,... | collective-permute-start | bytes 1966088 | tf_op jit(solution)/shard_map/ppermute | solution.py:313
  375.0 48.4 %collective-permute-start.30 = (bf16[256,1280]{1,0:T(8,128)(2,1)S(1)}, bf16[256,1280]{1,0:T(8,128)(2,1)}, u32[]{:S(2)}, u32[]{:S(2)}) collective-permute-start(bf16[256,1280]{1,0:T(8,128)(2,1)S(1)} %copy-done.22), channel_id=1, source_target_pairs={{0,2},{1,3},{2,0},{3,1},{4,6},{5,7},{6,4},{7,5},{8,10},{9,11},{10,... | collective-permute-start | bytes 1966088 | tf_op jit(solution)/shard_map/ppermute | solution.py:313
  375.7 47.8 %collective-permute-start.29 = (bf16[256,1280]{1,0:T(8,128)(2,1)S(1)}, bf16[256,1280]{1,0:T(8,128)(2,1)}, u32[]{:S(2)}, u32[]{:S(2)}) collective-permute-start(bf16[256,1280]{1,0:T(8,128)(2,1)S(1)} %copy-done.22), channel_id=1, source_target_pairs={{0,1},{1,0},{2,3},{3,2},{4,5},{5,4},{6,7},{7,6},{8,9},{9,8},{10,11... | collective-permute-start | bytes 1966088 | tf_op jit(solution)/shard_map/ppermute | solution.py:313
  377.0 47.9 %collective-permute-start.27 = (bf16[256,2048]{1,0:T(8,128)(2,1)}, bf16[256,2048]{1,0:T(8,128)(2,1)}, u32[]{:S(2)}, u32[]{:S(2)}) collective-permute-start(bf16[256,2048]{1,0:T(8,128)(2,1)} %get-tuple-element.168), channel_id=1, source_target_pairs={{0,1},{1,0},{2,3},{3,2},{4,5},{5,4},{6,7},{7,6},{8,9},{9,8},{10,11... | collective-permute-start | bytes 3145736 | tf_op jit(solution)/shard_map/ppermute | solution.py:313
  377.7 47.5 %collective-permute-start.28 = (bf16[256,2048]{1,0:T(8,128)(2,1)}, bf16[256,2048]{1,0:T(8,128)(2,1)}, u32[]{:S(2)}, u32[]{:S(2)}) collective-permute-start(bf16[256,2048]{1,0:T(8,128)(2,1)} %get-tuple-element.169), channel_id=1, source_target_pairs={{0,2},{1,3},{2,0},{3,1},{4,6},{5,7},{6,4},{7,5},{8,10},{9,11},{10,... | collective-permute-start | bytes 3145736 | tf_op jit(solution)/shard_map/ppermute | solution.py:313
  425.2 108.0 %reduce-scatter.11.cloned.1.call-start = ((), (), s32[]{:S(2)}) async-start(), calls=%async_computation.10 | async-start | bytes 1310720 | tf_op jit(solution)/shard_map/reduce_scatter | solution.py:655
  425.9 42.8 %collective-permute-start.36 = (bf16[256,2560]{1,0:T(8,128)(2,1)}, bf16[256,2560]{1,0:T(8,128)(2,1)}, u32[]{:S(2)}, u32[]{:S(2)}) collective-permute-start(bf16[256,2560]{1,0:T(8,128)(2,1)} %reduce-scatter.7.cloned.1.call-done.refs_0_), channel_id=1, source_target_pairs={{0,2},{1,3},{2,0},{3,1},{4,6},{5,7},{6,4},{7,5},{8,10},{9,11},{10,... | collective-permute-start | bytes 3932168 | tf_op jit(solution)/shard_map/ppermute | solution.py:313
  427.0 41.7 %collective-permute-start.35 = (bf16[256,2560]{1,0:T(8,128)(2,1)}, bf16[256,2560]{1,0:T(8,128)(2,1)}, u32[]{:S(2)}, u32[]{:S(2)}) collective-permute-start(bf16[256,2560]{1,0:T(8,128)(2,1)} %reduce-scatter.7.cloned.1.call-done.refs_0_), channel_id=1, source_target_pairs={{0,1},{1,0},{2,3},{3,2},{4,5},{5,4},{6,7},{7,6},{8,9},{9,8},{10,11... | collective-permute-start | bytes 3932168 | tf_op jit(solution)/shard_map/ppermute | solution.py:313
  472.2 26.4 %collective-permute-start.39 = (bf16[256,2048]{1,0:T(8,128)(2,1)}, bf16[256,2048]{1,0:T(8,128)(2,1)}, u32[]{:S(2)}, u32[]{:S(2)}) collective-permute-start(bf16[256,2048]{1,0:T(8,128)(2,1)} %get-tuple-element.204), channel_id=1, source_target_pairs={{0,1},{1,0},{2,3},{3,2},{4,5},{5,4},{6,7},{7,6},{8,9},{9,8},{10,11... | collective-permute-start | bytes 3145736 | tf_op jit(solution)/shard_map/ppermute | solution.py:313
  473.4 26.4 %collective-permute-start.40 = (bf16[256,2048]{1,0:T(8,128)(2,1)}, bf16[256,2048]{1,0:T(8,128)(2,1)}, u32[]{:S(2)}, u32[]{:S(2)}) collective-permute-start(bf16[256,2048]{1,0:T(8,128)(2,1)} %get-tuple-element.205), channel_id=1, source_target_pairs={{0,2},{1,3},{2,0},{3,1},{4,6},{5,7},{6,4},{7,5},{8,10},{9,11},{10,... | collective-permute-start | bytes 3145736 | tf_op jit(solution)/shard_map/ppermute | solution.py:313
  478.8 33.8 %collective-permute-start.53 = (bf16[128,2560]{1,0:T(8,128)(2,1)}, bf16[128,2560]{1,0:T(8,128)(2,1)}, u32[]{:S(2)}, u32[]{:S(2)}) collective-permute-start(bf16[128,2560]{1,0:T(8,128)(2,1)} %slice.193), channel_id=1, source_target_pairs={{0,1},{1,0},{2,3},{3,2},{4,5},{5,4},{6,7},{7,6},{8,9},{9,8},{10,11... | collective-permute-start | bytes 1966088 | tf_op jit(solution)/shard_map/ppermute | solution.py:313
  480.1 33.7 %collective-permute-start.54 = (bf16[128,2560]{1,0:T(8,128)(2,1)}, bf16[128,2560]{1,0:T(8,128)(2,1)}, u32[]{:S(2)}, u32[]{:S(2)}) collective-permute-start(bf16[128,2560]{1,0:T(8,128)(2,1)} %slice.194), channel_id=1, source_target_pairs={{0,2},{1,3},{2,0},{3,1},{4,6},{5,7},{6,4},{7,5},{8,10},{9,11},{10,... | collective-permute-start | bytes 1966088 | tf_op jit(solution)/shard_map/ppermute | solution.py:313
  493.9 34.3 %collective-permute-start.38 = (bf16[256,1536]{1,0:T(8,128)(2,1)}, bf16[256,1536]{1,0:T(8,128)(2,1)S(1)}, u32[]{:S(2)}, u32[]{:S(2)}) collective-permute-start(bf16[256,1536]{1,0:T(8,128)(2,1)} %reduce-scatter.9.cloned.1.call-done.refs_0_), channel_id=1, source_target_pairs={{0,2},{1,3},{2,0},{3,1},{4,6},{5,7},{6,4},{7,5},{8,10},{9,11},{10,... | collective-permute-start | bytes 2359304 | tf_op jit(solution)/shard_map/ppermute | solution.py:313
  498.6 29.6 %collective-permute-start.37 = (bf16[256,1536]{1,0:T(8,128)(2,1)}, bf16[256,1536]{1,0:T(8,128)(2,1)}, u32[]{:S(2)}, u32[]{:S(2)}) collective-permute-start(bf16[256,1536]{1,0:T(8,128)(2,1)} %reduce-scatter.9.cloned.1.call-done.refs_0_), channel_id=1, source_target_pairs={{0,1},{1,0},{2,3},{3,2},{4,5},{5,4},{6,7},{7,6},{8,9},{9,8},{10,11... | collective-permute-start | bytes 2359304 | tf_op jit(solution)/shard_map/ppermute | solution.py:313
  (83 other events, 1163.6 us)
Sparse Core Ops, SparseCore 0:
  11.0 84.7 all-gather.3
  98.0 97.9 all-gather.7
  198.2 54.4 all-gather.5
  255.3 58.6 reduce-scatter.4
  328.8 92.5 reduce-scatter.6
  425.3 68.5 reduce-scatter.8
  496.8 28.1 reduce-scatter.10

commit v4 on v3

--- a/solution.py
+++ b/solution.py
@@ -380,9 +380,8 @@
     return add_parts(cols_dot(rows[:size], weights), received)
 
 
-def total_sum(values, axis):
-    count = lax.axis_size(axis)
-    level = [values] + [swap(values, axis, step) for step in range(1, count)]
+def seq_sum(values):
+    level = [values] + [swap(values, "seq", step) for step in range(1, lax.axis_size("seq"))]
     while len(level) > 1:
         level = [level[i] + level[i + 1] for i in range(0, len(level), 2)]
     return level[0]
@@ -459,32 +458,109 @@
     )(grad_rows, weights, gelu, slope)
 
 
-def place_kernel(moves, count, widths, place_ref, *refs):
-    pieces, outs = refs[:count], refs[count:]
-    for step in range(count):
+def place_kernel(moves, lengths, block, widths, weighed, place_ref, *refs):
+    count = sum(lengths)
+    weights = refs[count : count + len(weighed)]
+    outs = refs[count + len(weighed) : count + len(weighed) + len(widths)]
+    total = jnp.zeros((block, TILE), jnp.float32)
+    first = 0
+    for step, length in enumerate(lengths):
+        pieces = refs[first : first + length]
+        first += length
         owner = jnp.bitwise_xor(place_ref[0], step)
         for out, source, target, size in moves:
-            at = pl.multiple_of(owner * widths[out] + target, TILE)
-            block = pieces[step][:, source : source + size]
-            outs[out][:, pl.ds(at, size)] = block.astype(jnp.float32)
-
-
-def place_columns(parts, place, moves, widths):
-    pieces = [part[0] if len(part) == 1 else jnp.concatenate(part, axis=0) for part in parts]
-    count = len(pieces)
-    rows, width = pieces[0].shape
-    block = min(64, rows)
+            at = pl.ds(pl.multiple_of(owner * widths[out] + target, TILE), size)
+            part = pieces[0][:, source : source + size]
+            if length == 2:
+                upper = pl.program_id(0) < pl.num_programs(0) // 2
+                part = jnp.where(upper, part, pieces[1][:, source : source + size])
+            part = part.astype(jnp.float32)
+            outs[out][:, at] = part
+            if out in weighed:
+                part = part * weights[weighed.index(out)][:, at].astype(jnp.float32)
+                for start in range(0, size, TILE):
+                    total = total + part[:, start : start + TILE]
+    if weighed:
+        refs[-1][...] = total
+
+
+def place_columns(parts, place, moves, widths, weights=()):
+    lengths = tuple(len(pieces) for pieces in parts)
+    count = lax.axis_size("seq")
+    rows, width = parts[0][0].shape
+    block = min(64, rows // 2)
+    steps = rows // block
+
+    def wide(size):
+        return pl.BlockSpec((block, size), lambda i: (i, 0))
+
+    def piece_specs(length):
+        if length == 1:
+            return [wide(width)]
+        half = steps // 2
+        return [
+            pl.BlockSpec((block, width), lambda i: (jnp.minimum(i, half - 1), 0)),
+            pl.BlockSpec((block, width), lambda i: (jnp.maximum(i - half, 0), 0)),
+        ]
+
+    whole = [wide(count * size) for size in widths]
+    sums = [wide(TILE)] if weights else []
+    shapes = [count * size for size in widths] + [TILE] * len(sums)
+    weighed = tuple(range(len(weights)))
     return pl.pallas_call(
-        functools.partial(place_kernel, moves, count, widths),
-        grid=(rows // block,),
+        functools.partial(place_kernel, moves, lengths, block, widths, weighed),
+        grid=(steps,),
         in_specs=[pl.BlockSpec(memory_space=pltpu.SMEM)]
-        + [pl.BlockSpec((block, width), lambda i: (i, 0))] * count,
-        out_specs=[pl.BlockSpec((block, count * size), lambda i: (i, 0)) for size in widths],
-        out_shape=[jax.ShapeDtypeStruct((rows, count * size), jnp.float32) for size in widths],
+        + [spec for length in lengths for spec in piece_specs(length)]
+        + whole[: len(weights)],
+        out_specs=whole + sums,
+        out_shape=[jax.ShapeDtypeStruct((rows, size), jnp.float32) for size in shapes],
+        compiler_params=pltpu.CompilerParams(vmem_limit_bytes=VMEM_BYTES),
+        cost_estimate=pl.CostEstimate(
+            flops=0, bytes_accessed=8 * rows * sum(shapes), transcendentals=0
+        ),
+        name="place_columns",
+    )(place, *[piece for pieces in parts for piece in pieces], *weights)
+
+
+def place_far_kernel(moves, half, count, place_ref, upper_ref, lower_ref, *refs):
+    weights, outs, sums_ref = refs[:count], refs[2 * count : 3 * count], refs[-1]
+    for rows, piece in ((slice(0, half), upper_ref), (slice(half, 2 * half), lower_ref)):
+        total = jnp.zeros((half, TILE), jnp.float32)
+        for out, source, target, size in moves:
+            at = slice(target, target + size)
+            part = piece[:, source : source + size].astype(jnp.float32)
+            outs[out][rows, at] = part
+            part = part * weights[out][rows, at].astype(jnp.float32)
+            for start in range(0, size, TILE):
+                total = total + part[:, start : start + TILE]
+        sums_ref[rows, :] = total
+
+
+def place_far(halves, place, moves, widths, weights, outs):
+    upper, lower = halves
+    half, width = upper.shape
+    count = len(widths)
+    whole = pl.BlockSpec((half, width), lambda i, place_ref: (0, 0))
+    column = [
+        pl.BlockSpec((2 * half, size), lambda i, place_ref: (0, jnp.bitwise_xor(place_ref[0], 3)))
+        for size in widths
+    ]
+    return pl.pallas_call(
+        functools.partial(place_far_kernel, moves, half, count),
+        grid_spec=pltpu.PrefetchScalarGridSpec(
+            num_scalar_prefetch=1,
+            grid=(1,),
+            in_specs=[whole, whole] + column + [pl.BlockSpec(memory_space=pl.ANY)] * count,
+            out_specs=column + [pl.BlockSpec((2 * half, TILE), lambda i, place_ref: (0, 0))],
+        ),
+        out_shape=[jax.ShapeDtypeStruct(out.shape, out.dtype) for out in outs]
+        + [jax.ShapeDtypeStruct((2 * half, TILE), jnp.float32)],
+        input_output_aliases={3 + count + k: k for k in range(count)},
         compiler_params=pltpu.CompilerParams(vmem_limit_bytes=VMEM_BYTES),
         cost_estimate=NO_COST,
-        name="place_columns",
-    )(place, *pieces)
+        name="place_far",
+    )(place, upper, lower, *weights, *outs)
 
 
 def take_kernel(moves, count, place_ref, *refs):
@@ -495,7 +571,7 @@
 
 def take_columns(place, weights, moves, counts):
     rows = weights[0].shape[0]
-    block = min(64, rows)
+    block = min(128, rows)
     width = sum(counts)
 
     def chosen(count):
@@ -516,12 +592,12 @@
     )(place, *weights)
 
 
-def split_kernel(core_ref, own_in, other_in, own_ref, other_ref):
-    own_ref[...] = own_in[...]
-    other_ref[...] = other_in[...]
-
-
-def split_columns(rows, core, groups):
+def turn_kernel(core_ref, own_in, other_in, own_ref, other_ref):
+    own_ref[...] = jnp.transpose(own_in[...])
+    other_ref[...] = jnp.transpose(other_in[...])
+
+
+def turn_halves(rows, core, groups):
     length, width = rows.shape
     size = width // groups
 
@@ -530,10 +606,10 @@
             (length, size), lambda i, core_ref: (0, 2 * i + jnp.bitwise_xor(core_ref[0], side))
         )
 
-    half = jax.ShapeDtypeStruct((length, width // 2), rows.dtype)
-    block = pl.BlockSpec((length, size), lambda i, core_ref: (0, i))
+    half = jax.ShapeDtypeStruct((width // 2, length), rows.dtype)
+    block = pl.BlockSpec((size, length), lambda i, core_ref: (i, 0))
     return pl.pallas_call(
-        split_kernel,
+        turn_kernel,
         grid_spec=pltpu.PrefetchScalarGridSpec(
             num_scalar_prefetch=1,
             grid=(groups // 2,),
@@ -543,16 +619,42 @@
         out_shape=[half, half],
         compiler_params=pltpu.CompilerParams(vmem_limit_bytes=VMEM_BYTES),
         cost_estimate=NO_COST,
-        name="split_columns",
+        name="turn_halves",
     )(core, rows, rows)
+
+
+def added_dot_kernel(left_ref, right_ref, added_ref, out_ref):
+    rows = left_ref.shape[0]
+    chunk = min(512, rows)
+    for start in range(0, rows, chunk):
+        at = slice(start, start + chunk)
+        product = jnp.dot(left_ref[at, :], right_ref[...], preferred_element_type=jnp.float32)
+        out_ref[at, :] = (product + added_ref[at, :].astype(jnp.float32)).astype(jnp.bfloat16)
+
+
+def added_dot(left, right, added):
+    rows, depth = left.shape
+    width = right.shape[1]
+    tile = next(t for t in (512, 256, 128) if width % t == 0)
+    column = pl.BlockSpec((rows, tile), lambda j: (0, j))
+    return pl.pallas_call(
+        added_dot_kernel,
+        grid=(width // tile,),
+        in_specs=[
+            pl.BlockSpec((rows, depth), lambda j: (0, 0)),
+            pl.BlockSpec((depth, tile), lambda j: (0, j)),
+            column,
+        ],
+        out_specs=column,
+        out_shape=jax.ShapeDtypeStruct((rows, width), jnp.bfloat16),
+        compiler_params=pltpu.CompilerParams(vmem_limit_bytes=VMEM_BYTES),
+        cost_estimate=NO_COST,
+        name="added_dot",
+    )(left, right, added)
 
 
 def both(*values):
     return lax.optimization_barrier(values)
-
-
-def add_low(sums, added):
-    return (sums + added.astype(jnp.float32)).astype(jnp.bfloat16)
 
 
 def on_device(
@@ -668,7 +770,7 @@
     hidden, gelu, slope = feed_forward(ffn_rows, gate_up_w, tile)
 
     down_grad = rows_dot(ff_grad_rows, hidden).astype(jnp.bfloat16)
-    ffn_own, ffn_other = split_columns(ffn_rows, core, fsdp_count)
+    ffn_own, ffn_other = turn_halves(ffn_rows, core, fsdp_count)
     down_owned = scatter_grads(down_grad)
     down_grad, hidden, gelu, ffn_own, ffn_other = both(down_grad, hidden, gelu, ffn_own, ffn_other)
     away = row_length // seq_count
@@ -677,17 +779,21 @@
     ff_far, hidden, gelu = both(ff_far, hidden, gelu)
     ff_passing = scatter_begin(ff_far)
     unit_grad = feed_forward_back(ff_grad_rows, down_w, gelu, slope, tile)
-    unit_terms = low_dot(unit_grad[away:], gate_up_w)
-    unit_terms, unit_grad, ff_passing = both(unit_terms, unit_grad, ff_passing)
-    unit_near, unit_far = split_terms(unit_terms)
+    unit_far = low_dot(unit_grad[passed:], gate_up_w) if seq_count == 4 else None
+    unit_far, unit_grad, ff_passing = both(unit_far, unit_grad, ff_passing)
     unit_passing = scatter_begin(unit_far)
-    gate_up_away = rows_dot(ffn_other, unit_grad).astype(jnp.bfloat16)
-    gate_up_away, unit_grad, unit_passing = both(gate_up_away, unit_grad, unit_passing)
+    unit_near = low_dot(unit_grad[away:passed], gate_up_w)
+    gate_up_away = jnp.dot(
+        ffn_other, unit_grad, preferred_element_type=jnp.float32
+    ).astype(jnp.bfloat16)
+    unit_near, unit_grad, unit_passing, gate_up_away, hidden = both(
+        unit_near, unit_grad, unit_passing, gate_up_away, hidden
+    )
     unit_sums = scatter_add(unit_near, unit_passing)
-    unit_sums, unit_grad, gate_up_away = both(unit_sums, unit_grad, gate_up_away)
+    unit_sums, unit_grad = both(unit_sums, unit_grad)
     unit_parts = scatter_end(unit_sums)
     gate_up_added = swap(gate_up_away, "fsdp", 1)
-    gate_up_grad = add_low(rows_dot(ffn_own, unit_grad), gate_up_added)
+    gate_up_grad = added_dot(ffn_own, unit_grad, gate_up_added)
     ffn_in_own = cols_dot(unit_grad[:away], gate_up_w)
     ffn_in_own, gate_up_grad, unit_parts = both(ffn_in_own, gate_up_grad, unit_parts)
     gate_up_owned = scatter_grads(gate_up_grad, groups)
@@ -714,8 +820,10 @@
     )
     attn_owned = scatter_grads(attn_grads)
     gate_up_near = gather_begin(gate_up_owned)
-    output_own, output_other = split_columns(attn_grad_rows, core, fsdp_count)
-    output_away = rows_dot(output_other, context).astype(jnp.bfloat16)
+    output_own, output_other = turn_halves(attn_grad_rows, core, fsdp_count)
+    output_away = jnp.dot(
+        output_other, context, preferred_element_type=jnp.float32
+    ).astype(jnp.bfloat16)
     qkv_terms = low_dot(qkv_grad[away:], qkv_w)
     qkv_terms, qkv_grad, output_away, output_own, down_near, hidden = both(
         qkv_terms, qkv_grad, output_away, output_own, down_near, hidden
@@ -724,7 +832,7 @@
     qkv_passing = scatter_begin(qkv_far)
     output_added = swap(output_away, "fsdp", 1)
     attn_in_own = cols_dot(qkv_grad[:away], qkv_w)
-    output_grad = add_low(rows_dot(output_own, context), output_added)
+    output_grad = added_dot(output_own, context, output_added)
     attn_in_own, output_grad, qkv_passing, hidden, ffn_in_grad, gate_up_near, down_near = both(
         attn_in_own, output_grad, qkv_passing, hidden, ffn_in_grad, gate_up_near, down_near
     )
@@ -736,15 +844,7 @@
     down_pieces = gather_end(down_owned, down_near)
     ff_out = add_parts(cols_dot(hidden[:away], down_w), ff_parts)
     result = resid + ff_out
-    gain_ffn_part = jnp.sum(ffn_in_grad * normed_ffn, axis=0)
-    attn_owned, result, gain_ffn_part = both(attn_owned, result, gain_ffn_part)
-    attn_near = gather_begin(attn_owned)
-    attn_in_grad = add_parts(attn_in_own, attn_in_parts)
-    gain_attn_part = jnp.sum(attn_in_grad * normed_attn, axis=0)
-    stream_grad = resid_grad + norm_back(attn_in_grad * attn_gain, normed_attn, scale_attn)
     (down_out,) = place_columns(down_pieces, place, [(0, 0, 0, unit_count)], [unit_count])
-    gate_out, up_out = place_columns(gate_up_pieces, place, unit_moves, [unit_count] * 2)
-
     own_segments = lax.dynamic_slice_in_dim(segment_row, seq_place * token_rows, token_rows, 0)
     valid = (own_segments >= 0).astype(jnp.float32)
     stat_terms = jnp.stack(
@@ -761,46 +861,59 @@
     full_table = lax.dynamic_update_slice_in_dim(
         jnp.zeros(rel_table.shape, jnp.float32), table_part, seq_place * head_count, 0
     )
-    packed = jnp.concatenate(
-        [gain_attn_part, gain_ffn_part, full_table.reshape(-1), jnp.pad(stat_terms, (0, 124))]
-    ).reshape(-1, 128)
-    summed = total_sum(packed, "fsdp")
-    attn_near, stream_grad, gain_attn_part, down_out, output_owned = both(
-        attn_near, stream_grad, gain_attn_part, down_out, output_owned
-    )
+    packed = jnp.concatenate([full_table.reshape(-1), jnp.pad(stat_terms, (0, TILE - 4))])
+    summed = jnp.sum(lax.all_gather(packed.reshape(-1, TILE), "fsdp"), axis=0)
+    attn_owned, result, summed, down_out, gate_up_pieces, attn_in_parts = both(
+        attn_owned, result, summed, down_out, gate_up_pieces, attn_in_parts
+    )
+    attn_near = gather_begin(attn_owned)
+    attn_in_grad = add_parts(attn_in_own, attn_in_parts)
+    stream_grad = resid_grad + norm_back(attn_in_grad * attn_gain, normed_attn, scale_attn)
+    stream_grad = stream_grad.astype(jnp.bfloat16)
+    gate_out, up_out, ffn_sums = place_columns(
+        gate_up_pieces, place, unit_moves, [unit_count] * 2, (w_gate, w_up)
+    )
+    attn_near, stream_grad, gate_out, up_out, output_owned = both(
+        attn_near, stream_grad, gate_out, up_out, output_owned
+    )
+    attn_pieces = gather_end(attn_owned, attn_near)
     output_near = gather_begin(output_owned, relay=False)
-    attn_pieces = gather_end(attn_owned, attn_near)
-    summed, attn_pieces, output_near, gate_out, up_out = both(
-        summed, attn_pieces, output_near, gate_out, up_out
-    )
-    summed = total_sum(summed, "seq").reshape(-1)
-    query_out, key_out, value_out = place_columns(
-        attn_pieces, place, qkv_moves[:-1], [column_count] * 3
-    )
+    attn_weights, attn_widths = (w_query, w_key, w_value), [column_count] * 3
+    attn_outs = place_columns(
+        attn_pieces[:3] if seq_count == 4 else attn_pieces,
+        place,
+        qkv_moves[:-1],
+        attn_widths,
+        attn_weights,
+    )
+    attn_pieces, output_near, summed, attn_outs = both(
+        attn_pieces, output_near, summed, attn_outs
+    )
+    summed = seq_sum(summed).reshape(-1)
+    *attn_outs, attn_sums = attn_outs
+    if seq_count == 4:
+        *attn_outs, far_sums = place_far(
+            attn_pieces[3], place, qkv_moves[:-1], attn_widths, attn_weights, attn_outs
+        )
+        attn_sums = attn_sums + far_sums
+    query_out, key_out, value_out = attn_outs
     (output_out,) = place_columns(
-        gather_end(output_owned, output_near),
-        place,
-        [(0, 0, 0, column_count)],
-        [column_count],
-    )
-    table_end = 2 * model_width + rel_table.size
-    stat_totals = summed[table_end : table_end + 4]
+        gather_end(output_owned, output_near), place, [(0, 0, 0, column_count)], [column_count]
+    )
+    gain_attn_grad = jnp.sum(attn_sums, axis=1) / gain_attn.astype(jnp.float32)
+    gain_ffn_grad = jnp.sum(ffn_sums, axis=1) / gain_ffn.astype(jnp.float32)
+    stat_totals = summed[rel_table.size : rel_table.size + 4]
     rms_stats = jnp.sqrt(stat_totals[0:3] / (stat_totals[3] * model_width))
-    gain_rows = model_width // fsdp_count
-    table_rows = rel_table.shape[0] // fsdp_count
-    gain_attn_grad = lax.dynamic_slice_in_dim(summed, fsdp_place * gain_rows, gain_rows, 0)
-    gain_ffn_grad = lax.dynamic_slice_in_dim(
-        summed, model_width + fsdp_place * gain_rows, gain_rows, 0
-    )
+    table_share = rel_table.shape[0] // fsdp_count
     rel_table_grad = lax.dynamic_slice_in_dim(
-        summed[2 * model_width : table_end].reshape(rel_table.shape),
-        fsdp_place * table_rows,
-        table_rows,
+        summed[: rel_table.size].reshape(rel_table.shape),
+        fsdp_place * table_share,
+        table_share,
         0,
     )
     return (
         result.astype(jnp.bfloat16)[None],
-        stream_grad.astype(jnp.bfloat16)[None],
+        stream_grad[None],
         query_out,
         key_out,
         value_out,

time: 588 us -> 578 us (0.983)
  waiting for transfers between devices: 182 us -> 157 us
  Pallas kernels: 120 us -> 138 us
  blocking collectives: 12.1 us -> 26 us
  matrix products: 112 us -> 105 us
    ppermute x58 -> x51, waiting for transfers between devices: 177 us -> 150 us  [swap(): lax.ppermute(piece, axis, [(i, i ^ step) for i in range(lax.axis_size(axi...]
    dot_general x6 -> x2, matrix products: 45.1 us -> 20.5 us  [rows_dot(): lax.dot_general(left, right, (((0,), (0,)), ((), ())), preferred_element_...]
    pallas_call x6 -> x9, Pallas kernels: 31.2 us -> 52.5 us  [the longest x4 23.8 us: place_columns(): pl.pallas_call(functools.partial(place_kernel, moves, lengths, block, wid...]
    all_gather x0 -> x1, blocking collectives: none -> 14 us  [on_device(): summed = jnp.sum(lax.all_gather(packed.reshape(-1, TILE), 'fsdp'), axis=0)]
    dot_general x9 -> x10, matrix products: 48.4 us -> 57.6 us  [cols_dot(): lax.dot_general(left, right, (((1,), (1,)), ((), ())), preferred_element_...]
    dot_general x0 -> x2, matrix products: none -> 8.55 us  [the longest x1 7.29 us: on_device(): jnp.dot(ffn_other, unit_grad, preferred_element_type=jnp.float32)]
    ppermute x58 -> x51, starting transfers between devices: 60.2 us -> 57.7 us  [swap(): lax.ppermute(piece, axis, [(i, i ^ step) for i in range(lax.axis_size(axi...]
    unnamed x101 -> x97, local copies, waits for them, and re-layouts: 23.7 us -> 21.3 us
  transfers between devices with their start and end apart: 65 -> 58, of which waited for: 36 -> 29; matrix products, arithmetic and copies ran while one was open for 32% -> 30% of each run, Pallas kernels for 20% -> 24%
where the time goes in v4:
time: 578 us; the launch traced here: 571 us
  waiting for transfers between devices  157 us (27%)
  Pallas kernels  138 us (24%)
  matrix products  105 us (18%)
  starting transfers between devices  58.3 us (10%)
  local copies, waits for them, and re-layouts  38.1 us (7%)
  other arithmetic  32.5 us (6%)
  blocking collectives  26 us (4%)
  between operations  15.8 us (3%)
    ppermute x51, waiting for transfers between devices, swap(): lax.ppermute(piece, axis, [(i, i ^ step) for i in range(lax.axis_size(axi...  150 us
    ppermute x51, starting transfers between devices, swap(): lax.ppermute(piece, axis, [(i, i ^ step) for i in range(lax.axis_size(axi...  57.7 us
    dot_general x10, matrix products, cols_dot(): lax.dot_general(left, right, (((1,), (1,)), ((), ())), preferred_element_...  57.6 us
    pallas_call x1, Pallas kernels, attention_backward(): pl.pallas_call(functools.partial(backward_kernel, block, token_rows), gri...  28.9 us
    pallas_call x4, Pallas kernels, place_columns(): pl.pallas_call(functools.partial(place_kernel, moves, lengths, block, wid...  23.8 us
    pallas_call x1, Pallas kernels, attention_forward(): pl.pallas_call(functools.partial(forward_kernel, block, token_rows), grid...  22.1 us
    unnamed x97, local copies, waits for them, and re-layouts  21.3 us
    dot_general x2, matrix products, rows_dot(): lax.dot_general(left, right, (((0,), (0,)), ((), ())), preferred_element_...  20.5 us
  transfers between devices with their start and end apart: 58, of which 29 were waited for; matrix products, arithmetic and copies ran while one was open for 30% of the time, Pallas kernels for 24%

profile of v4, /device:TPU:0, one launch (start us, length us, event | category | flops | bytes accessed | tf_op | source)
XLA Modules:
  0.0 570.9 jit_solution(4765540930686451252)
XLA Ops:
  14.3 12.0 %all_gather.15 = bf16[2,2048]{1,0:T(2,128)(2,1)S(1)} all-gather(bf16[2,256]{1,0:T(2,128)(2,1)S(1)} %pad_maximum_fusion), channel_id=1, replica_groups=mesh['fsdp'=8,'seq'=4] {'fsdp'}, dimensions={1}, use_global_device_ids=true | all-gather | bytes 9216 | tf_op jit(solution)/shard_map/all_gather | solution.py:710
  26.3 9.8 %collective-permute-done.1 = bf16[256,2048]{1,0:T(8,128)(2,1)S(1)} collective-permute-done((bf16[256,2048]{1,0:T(8,128)(2,1)}, bf16[256,2048]{1,0:T(8,128)(2,1)S(1)}, u32[]{:S(2)}, u32[]{:S(2)}) %collective-permute-start.1) | collective-permute-done | bytes 1048608 | tf_op jit(solution)/shard_map/ppermute | solution.py:313
  64.2 17.9 %collective-permute-done.5 = bf16[256,2048]{1,0:T(8,128)(2,1)} collective-permute-done((bf16[256,2048]{1,0:T(8,128)(2,1)}, bf16[256,2048]{1,0:T(8,128)(2,1)}, u32[]{:S(2)}, u32[]{:S(2)}) %collective-permute-start.5) | collective-permute-done | bytes 1048608 | tf_op jit(solution)/shard_map/ppermute | solution.py:313
  99.4 11.5 %fusion.9.qkv_ref = bf16[1024,1536]{1,0:T(8,128)(2,1)} fusion(bf16[1024,2048]{1,0:T(8,128)(2,1)} %fusion.2, bf16[2048,2048]{1,0:T(8,128)(2,1)} %all-gather.4.cloned.1.call-done), kind=kOutput, calls=%fused_computation.14 | convolution fusion | flops 6444023808 | bytes 13631488 | tf_op jit(solution)/shard_map/dot_general | solution.py:742
  114.6 22.1 %attention_forward.1 = (bf16[1024,512]{1,0:T(8,128)(2,1)}, bf16[8,1024,1024]{2,1,0:T(8,128)(2,1)}, f32[8,1,1024]{2,1,0:T(1,128)}) custom-call(s32[1]{0:T(128)} %bitcast.place_ref, bf16[1024,1536]{1,0:T(8,128)(2,1)} %fusion.9.qkv_ref, s32[1,1024]{1,0:T(1,128)} %row_ref.1, s32[1024,128]{1,0:T(8,128)} %broadcast_in_dim.11.col_ref, f32[4,2,2048]{2,1,0:T(2,128)} %reshape.89.bias_ref), custom_call_target="tpu_custom_call" | custom-call | tf_op jit(solution)/shard_map/attention_forward/pallas_call | solution.py:167
  143.8 7.3 %collective-permute-done.8 = bf16[128,2048]{1,0:T(8,128)(2,1)S(1)} collective-permute-done((bf16[128,2048]{1,0:T(8,128)(2,1)S(1)}, bf16[128,2048]{1,0:T(8,128)(2,1)S(1)}, u32[]{:S(2)}, u32[]{:S(2)}) %collective-permute-start.8) | collective-permute-done | bytes 524320 | tf_op jit(solution)/shard_map/ppermute | solution.py:313
  158.3 15.7 %collective-permute-done.9 = bf16[256,2048]{1,0:T(8,128)(2,1)S(1)} collective-permute-done((bf16[256,2048]{1,0:T(8,128)(2,1)S(1)}, bf16[256,2048]{1,0:T(8,128)(2,1)S(1)}, u32[]{:S(2)}, u32[]{:S(2)}) %collective-permute-start.9) | collective-permute-done | bytes 1048608 | tf_op jit(solution)/shard_map/ppermute | solution.py:313
  179.0 19.8 %collective-permute-done.13 = bf16[256,2048]{1,0:T(8,128)(2,1)S(1)} collective-permute-done((bf16[256,2048]{1,0:T(8,128)(2,1)S(1)}, bf16[256,2048]{1,0:T(8,128)(2,1)S(1)}, u32[]{:S(2)}, u32[]{:S(2)}) %collective-permute-start.13) | collective-permute-done | bytes 1048608 | tf_op jit(solution)/shard_map/ppermute | solution.py:313
  211.5 18.3 %feed_forward.1 = (bf16[1024,1280]{1,0:T(8,128)(2,1)}, bf16[1024,1280]{1,0:T(8,128)(2,1)}, bf16[1024,1280]{1,0:T(8,128)(2,1)}) custom-call(bf16[1024,2048]{1,0:T(8,128)(2,1)} %constant_dynamic-update-slice_fusion.10.x_ref.own_in.other_in, bf16[2048,2560]{1,0:T(8,128)(2,1)} %all-gather.8.cloned.1.call-done.w_ref), custom_call_target="tpu_custom_call" | custom-call | tf_op jit(solution)/shard_map/feed_forward/pallas_call | solution.py:411
  229.8 9.8 %convolution_convert_fusion.1 = bf16[2048,1280]{1,0:T(8,128)(2,1)} fusion(bf16[1024,2048]{1,0:T(8,128)(2,1)} %constant_dynamic-update-slice_fusion.5.d_ref, bf16[1024,1280]{1,0:T(8,128)(2,1)} %get-tuple-element.205), kind=kOutput, calls=%fused_computation.6 | convolution fusion | flops 5371330560 | bytes 12058624 | tf_op jit(solution)/shard_map/dot_general | solution.py:25
  259.2 11.9 %feed_forward_back.1.right_ref = bf16[1024,2560]{1,0:T(8,128)(2,1)} custom-call(bf16[1024,2048]{1,0:T(8,128)(2,1)} %constant_dynamic-update-slice_fusion.5.d_ref, bf16[2048,1280]{1,0:T(8,128)(2,1)} %all-gather.6.cloned.1.call-done.w_ref, bf16[1024,1280]{1,0:T(8,128)(2,1)} %get-tuple-element.154.gelu_ref, bf16[1024,1280]{1,0:T(8,128)(2,1)} %get-tuple-element.155.slope_ref), custom_call_target="tpu_custom_call" | custom-call | tf_op jit(solution)/shard_map/feed_forward_back/pallas_call | solution.py:444
  271.1 7.5 %convolution_convert_fusion.6 = bf16[256,2048]{1,0:T(8,128)(2,1)S(1)} fusion(bf16[2048,2560]{1,0:T(8,128)(2,1)} %all-gather.8.cloned.1.call-done.w_ref, bf16[1024,2560]{1,0:T(8,128)(2,1)} %feed_forward_back.1.right_ref), kind=kOutput, calls=%fused_computation.24 | convolution fusion | flops 2684878848 | bytes 12845056 | tf_op jit(solution)/shard_map/dot_general | solution.py:31
  280.3 9.5 %convolution_convert_fusion.5 = bf16[512,2048]{1,0:T(8,128)(2,1)S(1)} fusion(bf16[2048,2560]{1,0:T(8,128)(2,1)} %all-gather.8.cloned.1.call-done.w_ref, bf16[1024,2560]{1,0:T(8,128)(2,1)S(1)} %copy-done.4), kind=kOutput, calls=%fused_computation.21 | convolution fusion | flops 5369757696 | bytes 15204352 | tf_op jit(solution)/shard_map/dot_general | solution.py:31
  289.8 7.3 %convolution_convert_fusion.2 = bf16[1024,2560]{1,0:T(8,128)(2,1)} fusion(bf16[1024,1024]{1,0:T(8,128)(2,1)S(1)} %copy-done.35, bf16[1024,2560]{1,0:T(8,128)(2,1)S(1)} %copy-done.4), kind=kOutput, calls=%fused_computation.7 | convolution fusion | flops 5371330560 | bytes 12582912 | tf_op jit(solution)/shard_map/dot_general | solution.py:786
  306.3 11.0 %added_dot.2 = bf16[1024,2560]{1,0:T(8,128)(2,1)} custom-call(bf16[1024,1024]{1,0:T(8,128)(2,1)} %get-tuple-element.166.left_ref, bf16[1024,2560]{1,0:T(8,128)(2,1)} %feed_forward_back.1.right_ref, bf16[1024,2560]{1,0:T(8,128)(2,1)} %collective-permute-done.20.added_ref), custom_call_target="tpu_custom_call" | custom-call | tf_op jit(solution)/shard_map/added_dot/pallas_call | solution.py:640
  317.3 7.4 %collective-permute-done.21 = bf16[256,2048]{1,0:T(8,128)(2,1)} collective-permute-done((bf16[256,2048]{1,0:T(8,128)(2,1)}, bf16[256,2048]{1,0:T(8,128)(2,1)}, u32[]{:S(2)}, u32[]{:S(2)}) %collective-permute-start.21) | collective-permute-done | bytes 1048608 | tf_op jit(solution)/shard_map/ppermute | solution.py:313
  341.7 15.1 %collective-permute-done.24 = bf16[256,2048]{1,0:T(8,128)(2,1)S(1)} collective-permute-done((bf16[256,2048]{1,0:T(8,128)(2,1)}, bf16[256,2048]{1,0:T(8,128)(2,1)S(1)}, u32[]{:S(2)}, u32[]{:S(2)}) %collective-permute-start.24) | collective-permute-done | bytes 1048608 | tf_op jit(solution)/shard_map/ppermute | solution.py:313
  359.2 9.9 %collective-permute-done.25 = bf16[128,2048]{1,0:T(8,128)(2,1)S(1)} collective-permute-done((bf16[128,2048]{1,0:T(8,128)(2,1)S(1)}, bf16[128,2048]{1,0:T(8,128)(2,1)S(1)}, u32[]{:S(2)}, u32[]{:S(2)}) %collective-permute-start.25) | collective-permute-done | bytes 524320 | tf_op jit(solution)/shard_map/ppermute | solution.py:313
  380.8 28.9 %attention_backward.1 = (bf16[1024,1536]{1,0:T(8,128)(2,1)}, f32[4,2,2048]{2,1,0:T(2,128)}) custom-call(s32[1]{0:T(128)} %bitcast.place_ref, bf16[1024,1536]{1,0:T(8,128)(2,1)} %fusion.9.qkv_ref, bf16[1024,512]{1,0:T(8,128)(2,1)} %fusion.30.d_ref, bf16[8,1024,1024]{2,1,0:T(8,128)(2,1)} %get-tuple-element.180.e_ref, f32[8,1,1024]{2,1,0:T(1,128)} %get-tuple-element.181.inv_ref), custom_call_target="tpu_custom_call" | custom-call | tf_op jit(solution)/shard_map/attention_backward/pallas_call | solution.py:284
  409.6 10.7 %convolution_convert_fusion = bf16[2048,1536]{1,0:T(8,128)(2,1)} fusion(bf16[1024,2048]{1,0:T(8,128)(2,1)S(1)} %copy-done.11, bf16[1024,1536]{1,0:T(8,128)(2,1)} %get-tuple-element.196), kind=kOutput, calls=%fused_computation.5 | convolution fusion | flops 6445596672 | bytes 13631488 | tf_op jit(solution)/shard_map/dot_general | solution.py:25
  430.2 8.2 %fusion.12 = bf16[768,2048]{1,0:T(8,128)(2,1)S(1)} fusion(bf16[2048,2048]{1,0:T(8,128)(2,1)} %all-gather.4.cloned.1.call-done, bf16[1024,1536]{1,0:T(8,128)(2,1)S(1)} %copy-done.34), kind=kOutput, calls=%fused_computation.16 | convolution fusion | flops 4833411072 | bytes 11796480 | tf_op jit(solution)/shard_map/dot_general | solution.py:31
  454.5 10.4 %collective-permute-done.34 = bf16[128,2048]{1,0:T(8,128)(2,1)S(1)} collective-permute-done((bf16[128,2048]{1,0:T(8,128)(2,1)}, bf16[128,2048]{1,0:T(8,128)(2,1)S(1)}, u32[]{:S(2)}, u32[]{:S(2)}) %collective-permute-start.34) | collective-permute-done | bytes 524320 | tf_op jit(solution)/shard_map/ppermute | solution.py:313
  486.4 14.0 %all_gather.19 = f32[8,9,128]{2,1,0:T(8,128)S(1)} all-gather(f32[1,9,128]{2,1,0:T(8,128)S(1)} %maximum_bitcast_fusion), channel_id=1, replica_groups=mesh['fsdp'=8,'seq'=4] {'fsdp'}, dimensions={0}, use_global_device_ids=true | all-gather | bytes 41472 | tf_op jit(solution)/shard_map/all_gather | solution.py:865
  513.6 9.3 %place_columns.5 = (f32[256,5120]{1,0:T(8,128)}, f32[256,5120]{1,0:T(8,128)}, f32[256,128]{1,0:T(8,128)}) custom-call(s32[1]{0:T(128)} %bitcast.place_ref, bf16[256,2560]{1,0:T(8,128)(2,1)} %reduce-scatter.7.cloned.1.call-done.refs_0_, bf16[256,2560]{1,0:T(8,128)(2,1)} %collective-permute-done.35.refs_1_, bf16[256,2560]{1,0:T(8,128)(2,1)} %collective-permute-done.36.refs_2_, ...), custom_call_target="tpu_custom_call" | custom-call | bytes 21233664 | tf_op jit(solution)/shard_map/place_columns/pallas_call | solution.py:510
  (295 shorter events, 249.8 us)
Async XLA Ops:
  7.2 92.2 %all-gather.4.cloned.1.call-start = ((), (), s32[]{:S(2)}) async-start(), calls=%async_computation.4 | async-start | bytes 9437184 | tf_op jit(solution)/shard_map/all_gather | solution.py:694
  9.7 201.9 %all-gather.8.cloned.1.call-start = ((), (), s32[]{:S(2)}) async-start(), calls=%async_computation.6 | async-start | bytes 11796480 | tf_op jit(solution)/shard_map/all_gather | solution.py:694
  9.7 26.4 %collective-permute-start.1 = (bf16[256,2048]{1,0:T(8,128)(2,1)}, bf16[256,2048]{1,0:T(8,128)(2,1)S(1)}, u32[]{:S(2)}, u32[]{:S(2)}) collective-permute-start(bf16[256,2048]{1,0:T(8,128)(2,1)} %bitcast.49), channel_id=1, source_target_pairs={{0,2},{1,3},{2,0},{3,1},{4,6},{5,7},{6,4},{7,5},{8,10},{9,11},{10,... | collective-permute-start | bytes 3145736 | tf_op jit(solution)/shard_map/ppermute | solution.py:313
  12.7 24.9 %collective-permute-start = (bf16[256,2048]{1,0:T(8,128)(2,1)}, bf16[256,2048]{1,0:T(8,128)(2,1)}, u32[]{:S(2)}, u32[]{:S(2)}) collective-permute-start(bf16[256,2048]{1,0:T(8,128)(2,1)} %bitcast.50), channel_id=1, source_target_pairs={{0,1},{1,0},{2,3},{3,2},{4,5},{5,4},{6,7},{7,6},{8,9},{9,8},{10,11... | collective-permute-start | bytes 3145736 | tf_op jit(solution)/shard_map/ppermute | solution.py:313
  58.8 193.0 %all-gather.6.cloned.1.call-start = ((), (), s32[]{:S(2)}) async-start(), calls=%async_computation.5 | async-start | bytes 5898240 | tf_op jit(solution)/shard_map/all_gather | solution.py:694
  110.9 221.2 %reduce-scatter.5.cloned.1.call-start = ((), (), s32[]{:S(2)}) async-start(), calls=%async_computation.7 | async-start | bytes 5898240 | tf_op jit(solution)/shard_map/reduce_scatter | solution.py:757
  239.7 182.1 %reduce-scatter.7.cloned.1.call-start = ((), (), s32[]{:S(2)}) async-start(), calls=%async_computation.8 | async-start | bytes 6553600 | tf_op jit(solution)/shard_map/reduce_scatter | solution.py:757
  298.9 25.9 %collective-permute-start.21 = (bf16[256,2048]{1,0:T(8,128)(2,1)}, bf16[256,2048]{1,0:T(8,128)(2,1)}, u32[]{:S(2)}, u32[]{:S(2)}) collective-permute-start(bf16[256,2048]{1,0:T(8,128)(2,1)} %get-tuple-element.168), channel_id=1, source_target_pairs={{0,1},{1,0},{2,3},{3,2},{4,5},{5,4},{6,7},{7,6},{8,9},{9,8},{10,11... | collective-permute-start | bytes 3145736 | tf_op jit(solution)/shard_map/ppermute | solution.py:313
  300.4 25.6 %collective-permute-start.22 = (bf16[256,2048]{1,0:T(8,128)(2,1)}, bf16[256,2048]{1,0:T(8,128)(2,1)}, u32[]{:S(2)}, u32[]{:S(2)}) collective-permute-start(bf16[256,2048]{1,0:T(8,128)(2,1)} %get-tuple-element.169), channel_id=1, source_target_pairs={{0,2},{1,3},{2,0},{3,1},{4,6},{5,7},{6,4},{7,5},{8,10},{9,11},{10,... | collective-permute-start | bytes 3145736 | tf_op jit(solution)/shard_map/ppermute | solution.py:313
  326.0 182.4 %reduce-scatter.9.cloned.1.call-start = ((), (), s32[]{:S(2)}) async-start(), calls=%async_computation.9 | async-start | bytes 7077888 | tf_op jit(solution)/shard_map/reduce_scatter | solution.py:757
  332.1 24.6 %collective-permute-start.24 = (bf16[256,2048]{1,0:T(8,128)(2,1)}, bf16[256,2048]{1,0:T(8,128)(2,1)S(1)}, u32[]{:S(2)}, u32[]{:S(2)}) collective-permute-start(bf16[256,2048]{1,0:T(8,128)(2,1)} %fusion.48), channel_id=1, source_target_pairs={{0,2},{1,3},{2,0},{3,1},{4,6},{5,7},{6,4},{7,5},{8,10},{9,11},{10,... | collective-permute-start | bytes 3145736 | tf_op jit(solution)/shard_map/ppermute | solution.py:313
  333.1 24.4 %collective-permute-start.23 = (bf16[256,2048]{1,0:T(8,128)(2,1)}, bf16[256,2048]{1,0:T(8,128)(2,1)S(1)}, u32[]{:S(2)}, u32[]{:S(2)}) collective-permute-start(bf16[256,2048]{1,0:T(8,128)(2,1)} %fusion.48), channel_id=1, source_target_pairs={{0,1},{1,0},{2,3},{3,2},{4,5},{5,4},{6,7},{7,6},{8,9},{9,8},{10,11... | collective-permute-start | bytes 3145736 | tf_op jit(solution)/shard_map/ppermute | solution.py:313
  370.0 50.3 %collective-permute-start.31 = (bf16[256,1280]{1,0:T(8,128)(2,1)S(1)}, bf16[256,1280]{1,0:T(8,128)(2,1)}, u32[]{:S(2)}, u32[]{:S(2)}) collective-permute-start(bf16[256,1280]{1,0:T(8,128)(2,1)S(1)} %copy-done.19), channel_id=1, source_target_pairs={{0,3},{1,2},{2,1},{3,0},{4,7},{5,6},{6,5},{7,4},{8,11},{9,10},{10,... | collective-permute-start | bytes 1966088 | tf_op jit(solution)/shard_map/ppermute | solution.py:313
  371.8 48.5 %collective-permute-start.30 = (bf16[256,1280]{1,0:T(8,128)(2,1)S(1)}, bf16[256,1280]{1,0:T(8,128)(2,1)}, u32[]{:S(2)}, u32[]{:S(2)}) collective-permute-start(bf16[256,1280]{1,0:T(8,128)(2,1)S(1)} %copy-done.19), channel_id=1, source_target_pairs={{0,2},{1,3},{2,0},{3,1},{4,6},{5,7},{6,4},{7,5},{8,10},{9,11},{10,... | collective-permute-start | bytes 1966088 | tf_op jit(solution)/shard_map/ppermute | solution.py:313
  372.7 47.6 %collective-permute-start.29 = (bf16[256,1280]{1,0:T(8,128)(2,1)S(1)}, bf16[256,1280]{1,0:T(8,128)(2,1)}, u32[]{:S(2)}, u32[]{:S(2)}) collective-permute-start(bf16[256,1280]{1,0:T(8,128)(2,1)S(1)} %copy-done.19), channel_id=1, source_target_pairs={{0,1},{1,0},{2,3},{3,2},{4,5},{5,4},{6,7},{7,6},{8,9},{9,8},{10,11... | collective-permute-start | bytes 1966088 | tf_op jit(solution)/shard_map/ppermute | solution.py:313
  373.5 48.0 %collective-permute-start.27 = (bf16[256,2048]{1,0:T(8,128)(2,1)}, bf16[256,2048]{1,0:T(8,128)(2,1)}, u32[]{:S(2)}, u32[]{:S(2)}) collective-permute-start(bf16[256,2048]{1,0:T(8,128)(2,1)} %get-tuple-element.183), channel_id=1, source_target_pairs={{0,1},{1,0},{2,3},{3,2},{4,5},{5,4},{6,7},{7,6},{8,9},{9,8},{10,11... | collective-permute-start | bytes 3145736 | tf_op jit(solution)/shard_map/ppermute | solution.py:313
  374.7 47.1 %collective-permute-start.28 = (bf16[256,2048]{1,0:T(8,128)(2,1)}, bf16[256,2048]{1,0:T(8,128)(2,1)}, u32[]{:S(2)}, u32[]{:S(2)}) collective-permute-start(bf16[256,2048]{1,0:T(8,128)(2,1)} %get-tuple-element.184), channel_id=1, source_target_pairs={{0,2},{1,3},{2,0},{3,1},{4,6},{5,7},{6,4},{7,5},{8,10},{9,11},{10,... | collective-permute-start | bytes 3145736 | tf_op jit(solution)/shard_map/ppermute | solution.py:313
  421.8 105.7 %reduce-scatter.11.cloned.1.call-start = ((), (), s32[]{:S(2)}) async-start(), calls=%async_computation.10 | async-start | bytes 1310720 | tf_op jit(solution)/shard_map/reduce_scatter | solution.py:757
  422.7 43.1 %collective-permute-start.36 = (bf16[256,2560]{1,0:T(8,128)(2,1)}, bf16[256,2560]{1,0:T(8,128)(2,1)}, u32[]{:S(2)}, u32[]{:S(2)}) collective-permute-start(bf16[256,2560]{1,0:T(8,128)(2,1)} %reduce-scatter.7.cloned.1.call-done.refs_0_), channel_id=1, source_target_pairs={{0,2},{1,3},{2,0},{3,1},{4,6},{5,7},{6,4},{7,5},{8,10},{9,11},{10,... | collective-permute-start | bytes 3932168 | tf_op jit(solution)/shard_map/ppermute | solution.py:313
  423.9 41.9 %collective-permute-start.35 = (bf16[256,2560]{1,0:T(8,128)(2,1)}, bf16[256,2560]{1,0:T(8,128)(2,1)}, u32[]{:S(2)}, u32[]{:S(2)}) collective-permute-start(bf16[256,2560]{1,0:T(8,128)(2,1)} %reduce-scatter.7.cloned.1.call-done.refs_0_), channel_id=1, source_target_pairs={{0,1},{1,0},{2,3},{3,2},{4,5},{5,4},{6,7},{7,6},{8,9},{9,8},{10,11... | collective-permute-start | bytes 3932168 | tf_op jit(solution)/shard_map/ppermute | solution.py:313
  469.2 39.2 %collective-permute-start.39 = (bf16[256,2048]{1,0:T(8,128)(2,1)}, bf16[256,2048]{1,0:T(8,128)(2,1)}, u32[]{:S(2)}, u32[]{:S(2)}) collective-permute-start(bf16[256,2048]{1,0:T(8,128)(2,1)} %get-tuple-element.221), channel_id=1, source_target_pairs={{0,1},{1,0},{2,3},{3,2},{4,5},{5,4},{6,7},{7,6},{8,9},{9,8},{10,11... | collective-permute-start | bytes 3145736 | tf_op jit(solution)/shard_map/ppermute | solution.py:313
  470.3 38.2 %collective-permute-start.40 = (bf16[256,2048]{1,0:T(8,128)(2,1)}, bf16[256,2048]{1,0:T(8,128)(2,1)}, u32[]{:S(2)}, u32[]{:S(2)}) collective-permute-start(bf16[256,2048]{1,0:T(8,128)(2,1)} %get-tuple-element.222), channel_id=1, source_target_pairs={{0,2},{1,3},{2,0},{3,1},{4,6},{5,7},{6,4},{7,5},{8,10},{9,11},{10,... | collective-permute-start | bytes 3145736 | tf_op jit(solution)/shard_map/ppermute | solution.py:313
  474.9 32.7 %collective-permute-start.37 = (bf16[128,2560]{1,0:T(8,128)(2,1)}, bf16[128,2560]{1,0:T(8,128)(2,1)}, u32[]{:S(2)}, u32[]{:S(2)}) collective-permute-start(bf16[128,2560]{1,0:T(8,128)(2,1)} %slice.189), channel_id=1, source_target_pairs={{0,1},{1,0},{2,3},{3,2},{4,5},{5,4},{6,7},{7,6},{8,9},{9,8},{10,11... | collective-permute-start | bytes 1966088 | tf_op jit(solution)/shard_map/ppermute | solution.py:313
  475.9 32.6 %collective-permute-start.38 = (bf16[128,2560]{1,0:T(8,128)(2,1)S(1)}, bf16[128,2560]{1,0:T(8,128)(2,1)}, u32[]{:S(2)}, u32[]{:S(2)}) collective-permute-start(bf16[128,2560]{1,0:T(8,128)(2,1)S(1)} %slice.190), channel_id=1, source_target_pairs={{0,2},{1,3},{2,0},{3,1},{4,6},{5,7},{6,4},{7,5},{8,10},{9,11},{10,... | collective-permute-start | bytes 1966088 | tf_op jit(solution)/shard_map/ppermute | solution.py:313
  (74 other events, 949.7 us)
Sparse Core Ops, SparseCore 0:
  10.2 84.7 all-gather.3
  97.2 97.9 all-gather.7
  197.4 54.4 all-gather.5
  254.6 58.6 reduce-scatter.4
  326.2 91.6 reduce-scatter.6
  422.0 68.3 reduce-scatter.8
  493.2 25.4 reduce-scatter.10

commit v5 on v4

--- a/solution.py
+++ b/solution.py
@@ -523,46 +523,6 @@
     )(place, *[piece for pieces in parts for piece in pieces], *weights)
 
 
-def place_far_kernel(moves, half, count, place_ref, upper_ref, lower_ref, *refs):
-    weights, outs, sums_ref = refs[:count], refs[2 * count : 3 * count], refs[-1]
-    for rows, piece in ((slice(0, half), upper_ref), (slice(half, 2 * half), lower_ref)):
-        total = jnp.zeros((half, TILE), jnp.float32)
-        for out, source, target, size in moves:
-            at = slice(target, target + size)
-            part = piece[:, source : source + size].astype(jnp.float32)
-            outs[out][rows, at] = part
-            part = part * weights[out][rows, at].astype(jnp.float32)
-            for start in range(0, size, TILE):
-                total = total + part[:, start : start + TILE]
-        sums_ref[rows, :] = total
-
-
-def place_far(halves, place, moves, widths, weights, outs):
-    upper, lower = halves
-    half, width = upper.shape
-    count = len(widths)
-    whole = pl.BlockSpec((half, width), lambda i, place_ref: (0, 0))
-    column = [
-        pl.BlockSpec((2 * half, size), lambda i, place_ref: (0, jnp.bitwise_xor(place_ref[0], 3)))
-        for size in widths
-    ]
-    return pl.pallas_call(
-        functools.partial(place_far_kernel, moves, half, count),
-        grid_spec=pltpu.PrefetchScalarGridSpec(
-            num_scalar_prefetch=1,
-            grid=(1,),
-            in_specs=[whole, whole] + column + [pl.BlockSpec(memory_space=pl.ANY)] * count,
-            out_specs=column + [pl.BlockSpec((2 * half, TILE), lambda i, place_ref: (0, 0))],
-        ),
-        out_shape=[jax.ShapeDtypeStruct(out.shape, out.dtype) for out in outs]
-        + [jax.ShapeDtypeStruct((2 * half, TILE), jnp.float32)],
-        input_output_aliases={3 + count + k: k for k in range(count)},
-        compiler_params=pltpu.CompilerParams(vmem_limit_bytes=VMEM_BYTES),
-        cost_estimate=NO_COST,
-        name="place_far",
-    )(place, upper, lower, *weights, *outs)
-
-
 def take_kernel(moves, count, place_ref, *refs):
     out_ref = refs[count]
     for which, source, target, size in moves:
@@ -770,9 +730,8 @@
     hidden, gelu, slope = feed_forward(ffn_rows, gate_up_w, tile)
 
     down_grad = rows_dot(ff_grad_rows, hidden).astype(jnp.bfloat16)
-    ffn_own, ffn_other = turn_halves(ffn_rows, core, fsdp_count)
     down_owned = scatter_grads(down_grad)
-    down_grad, hidden, gelu, ffn_own, ffn_other = both(down_grad, hidden, gelu, ffn_own, ffn_other)
+    down_grad, hidden, gelu = both(down_grad, hidden, gelu)
     away = row_length // seq_count
     passed = 3 * away if seq_count == 4 else row_length
     ff_far = low_dot(hidden[passed:], down_w) if seq_count == 4 else None
@@ -783,20 +742,14 @@
     unit_far, unit_grad, ff_passing = both(unit_far, unit_grad, ff_passing)
     unit_passing = scatter_begin(unit_far)
     unit_near = low_dot(unit_grad[away:passed], gate_up_w)
-    gate_up_away = jnp.dot(
-        ffn_other, unit_grad, preferred_element_type=jnp.float32
-    ).astype(jnp.bfloat16)
-    unit_near, unit_grad, unit_passing, gate_up_away, hidden = both(
-        unit_near, unit_grad, unit_passing, gate_up_away, hidden
-    )
+    unit_near, unit_grad, unit_passing = both(unit_near, unit_grad, unit_passing)
     unit_sums = scatter_add(unit_near, unit_passing)
     unit_sums, unit_grad = both(unit_sums, unit_grad)
     unit_parts = scatter_end(unit_sums)
-    gate_up_added = swap(gate_up_away, "fsdp", 1)
-    gate_up_grad = added_dot(ffn_own, unit_grad, gate_up_added)
+    gate_up_grad = rows_dot(ffn_rows, unit_grad).astype(jnp.bfloat16)
     ffn_in_own = cols_dot(unit_grad[:away], gate_up_w)
     ffn_in_own, gate_up_grad, unit_parts = both(ffn_in_own, gate_up_grad, unit_parts)
-    gate_up_owned = scatter_grads(gate_up_grad, groups)
+    gate_up_owned = scatter_grads(gate_up_grad)
     ffn_in_grad = add_parts(ffn_in_own, unit_parts)
 
     resid_grad = upstream + norm_back(ffn_in_grad * ffn_gain, normed_ffn, scale_ffn)
@@ -814,32 +767,28 @@
     qkv_grad, line_grad = attention_backward(
         qkv, place, context_grad, exponents, inverse, head_count, token_rows
     )
+    qkv_terms = low_dot(qkv_grad[away:], qkv_w)
+    qkv_terms, qkv_grad = both(qkv_terms, qkv_grad)
     attn_grads = rows_dot(attn_rows, qkv_grad).astype(jnp.bfloat16)
-    attn_grads, context, qkv_grad, ff_parts, down_near, attn_grad_rows, gate_up_owned = both(
-        attn_grads, context, qkv_grad, ff_parts, down_near, attn_grad_rows, gate_up_owned
+    attn_grads, context, qkv_grad, ff_parts, down_near, attn_grad_rows, qkv_terms = both(
+        attn_grads, context, qkv_grad, ff_parts, down_near, attn_grad_rows, qkv_terms
     )
     attn_owned = scatter_grads(attn_grads)
-    gate_up_near = gather_begin(gate_up_owned)
+    qkv_near, qkv_far = split_terms(qkv_terms)
+    qkv_passing = scatter_begin(qkv_far)
     output_own, output_other = turn_halves(attn_grad_rows, core, fsdp_count)
     output_away = jnp.dot(
         output_other, context, preferred_element_type=jnp.float32
     ).astype(jnp.bfloat16)
-    qkv_terms = low_dot(qkv_grad[away:], qkv_w)
-    qkv_terms, qkv_grad, output_away, output_own, down_near, hidden = both(
-        qkv_terms, qkv_grad, output_away, output_own, down_near, hidden
-    )
-    qkv_near, qkv_far = split_terms(qkv_terms)
-    qkv_passing = scatter_begin(qkv_far)
+    qkv_passing, gate_up_owned, output_away, output_own, hidden, down_near, qkv_grad = both(
+        qkv_passing, gate_up_owned, output_away, output_own, hidden, down_near, qkv_grad
+    )
+    attn_in_own = cols_dot(qkv_grad[:away], qkv_w)
+    gate_up_near = gather_begin(gate_up_owned)
     output_added = swap(output_away, "fsdp", 1)
-    attn_in_own = cols_dot(qkv_grad[:away], qkv_w)
     output_grad = added_dot(output_own, context, output_added)
-    attn_in_own, output_grad, qkv_passing, hidden, ffn_in_grad, gate_up_near, down_near = both(
-        attn_in_own, output_grad, qkv_passing, hidden, ffn_in_grad, gate_up_near, down_near
-    )
     output_owned = scatter_grads(output_grad, groups)
-    qkv_sums = scatter_add(qkv_near, qkv_passing)
-    qkv_sums, gate_up_near, down_near = both(qkv_sums, gate_up_near, down_near)
-    attn_in_parts = scatter_end(qkv_sums)
+    attn_in_parts = scatter_end(scatter_add(qkv_near, qkv_passing))
     gate_up_pieces = gather_end(gate_up_owned, gate_up_near)
     down_pieces = gather_end(down_owned, down_near)
     ff_out = add_parts(cols_dot(hidden[:away], down_w), ff_parts)
@@ -873,30 +822,20 @@
     gate_out, up_out, ffn_sums = place_columns(
         gate_up_pieces, place, unit_moves, [unit_count] * 2, (w_gate, w_up)
     )
-    attn_near, stream_grad, gate_out, up_out, output_owned = both(
-        attn_near, stream_grad, gate_out, up_out, output_owned
-    )
+    attn_near, stream_grad, gate_out, up_out = both(attn_near, stream_grad, gate_out, up_out)
     attn_pieces = gather_end(attn_owned, attn_near)
+    summed = seq_sum(summed).reshape(-1)
+    attn_pieces, output_owned, summed = both(attn_pieces, output_owned, summed)
     output_near = gather_begin(output_owned, relay=False)
-    attn_weights, attn_widths = (w_query, w_key, w_value), [column_count] * 3
     attn_outs = place_columns(
-        attn_pieces[:3] if seq_count == 4 else attn_pieces,
+        attn_pieces,
         place,
         qkv_moves[:-1],
-        attn_widths,
-        attn_weights,
-    )
-    attn_pieces, output_near, summed, attn_outs = both(
-        attn_pieces, output_near, summed, attn_outs
-    )
-    summed = seq_sum(summed).reshape(-1)
-    *attn_outs, attn_sums = attn_outs
-    if seq_count == 4:
-        *attn_outs, far_sums = place_far(
-            attn_pieces[3], place, qkv_moves[:-1], attn_widths, attn_weights, attn_outs
-        )
-        attn_sums = attn_sums + far_sums
-    query_out, key_out, value_out = attn_outs
+        [column_count] * 3,
+        (w_query, w_key, w_value),
+    )
+    output_near, attn_outs = both(output_near, attn_outs)
+    query_out, key_out, value_out, attn_sums = attn_outs
     (output_out,) = place_columns(
         gather_end(output_owned, output_near), place, [(0, 0, 0, column_count)], [column_count]
     )

time: 578 us -> 572 us (0.990)
  Pallas kernels: 138 us -> 119 us
  matrix products: 105 us -> 118 us
  waiting for transfers between devices: 157 us -> 163 us
    dot_general x2 -> x3, matrix products: 20.5 us -> 34.4 us  [rows_dot(): lax.dot_general(left, right, (((0,), (0,)), ((), ())), preferred_element_...]
    pallas_call x2 -> x1, Pallas kernels: 15.4 us -> 4.51 us  [added_dot(): pl.pallas_call(added_dot_kernel, grid=(width // tile,), in_specs=[pl.Bloc...]
    dot_general x1 -> x0, matrix products: 7.29 us -> none  [on_device(): jnp.dot(ffn_other, unit_grad, preferred_element_type=jnp.float32)]
    unnamed x97 -> x73, local copies, waits for them, and re-layouts: 21.3 us -> 18.9 us
    ppermute x51 -> x50, waiting for transfers between devices: 150 us -> 151 us  [swap(): lax.ppermute(piece, axis, [(i, i ^ step) for i in range(lax.axis_size(axi...]
    ppermute x51 -> x50, starting transfers between devices: 57.7 us -> 57.2 us  [swap(): lax.ppermute(piece, axis, [(i, i ^ step) for i in range(lax.axis_size(axi...]
  transfers between devices with their start and end apart: 58 -> 57, of which waited for: 29 -> 26; matrix products, arithmetic and copies ran while one was open for 30% -> 32% of each run, Pallas kernels for 24% -> 20%
where the time goes in v5:
time: 572 us; the launch traced here: 565 us
  waiting for transfers between devices  163 us (28%)
  Pallas kernels  119 us (21%)
  matrix products  118 us (21%)
  starting transfers between devices  58.1 us (10%)
  local copies, waits for them, and re-layouts  35.3 us (6%)
  other arithmetic  30.4 us (5%)
  blocking collectives  26.2 us (5%)
  between operations  15.6 us (3%)
    ppermute x50, waiting for transfers between devices, swap(): lax.ppermute(piece, axis, [(i, i ^ step) for i in range(lax.axis_size(axi...  151 us
    dot_general x10, matrix products, cols_dot(): lax.dot_general(left, right, (((1,), (1,)), ((), ())), preferred_element_...  61.6 us
    ppermute x50, starting transfers between devices, swap(): lax.ppermute(piece, axis, [(i, i ^ step) for i in range(lax.axis_size(axi...  57.2 us
    dot_general x3, matrix products, rows_dot(): lax.dot_general(left, right, (((0,), (0,)), ((), ())), preferred_element_...  34.4 us
    pallas_call x1, Pallas kernels, attention_backward(): pl.pallas_call(functools.partial(backward_kernel, block, token_rows), gri...  29 us
    pallas_call x4, Pallas kernels, place_columns(): pl.pallas_call(functools.partial(place_kernel, moves, lengths, block, wid...  23.4 us
    pallas_call x1, Pallas kernels, attention_forward(): pl.pallas_call(functools.partial(forward_kernel, block, token_rows), grid...  22.1 us
    unnamed x73, local copies, waits for them, and re-layouts  18.9 us
  transfers between devices with their start and end apart: 57, of which 26 were waited for; matrix products, arithmetic and copies ran while one was open for 32% of the time, Pallas kernels for 20%

profile of v5, /device:TPU:0, one launch (start us, length us, event | category | flops | bytes accessed | tf_op | source)
XLA Modules:
  0.0 565.4 jit_solution(3464502089496733571)
XLA Ops:
  14.3 12.0 %all_gather.15 = bf16[2,2048]{1,0:T(2,128)(2,1)S(1)} all-gather(bf16[2,256]{1,0:T(2,128)(2,1)S(1)} %pad_maximum_fusion), channel_id=1, replica_groups=mesh['fsdp'=8,'seq'=4] {'fsdp'}, dimensions={1}, use_global_device_ids=true | all-gather | bytes 9216 | tf_op jit(solution)/shard_map/all_gather | solution.py:670
  26.3 9.8 %collective-permute-done.1 = bf16[256,2048]{1,0:T(8,128)(2,1)S(1)} collective-permute-done((bf16[256,2048]{1,0:T(8,128)(2,1)}, bf16[256,2048]{1,0:T(8,128)(2,1)S(1)}, u32[]{:S(2)}, u32[]{:S(2)}) %collective-permute-start.1) | collective-permute-done | bytes 1048608 | tf_op jit(solution)/shard_map/ppermute | solution.py:313
  64.2 17.9 %collective-permute-done.5 = bf16[256,2048]{1,0:T(8,128)(2,1)} collective-permute-done((bf16[256,2048]{1,0:T(8,128)(2,1)}, bf16[256,2048]{1,0:T(8,128)(2,1)}, u32[]{:S(2)}, u32[]{:S(2)}) %collective-permute-start.5) | collective-permute-done | bytes 1048608 | tf_op jit(solution)/shard_map/ppermute | solution.py:313
  99.5 11.4 %fusion.9.qkv_ref = bf16[1024,1536]{1,0:T(8,128)(2,1)} fusion(bf16[1024,2048]{1,0:T(8,128)(2,1)} %fusion.2, bf16[2048,2048]{1,0:T(8,128)(2,1)} %all-gather.4.cloned.1.call-done), kind=kOutput, calls=%fused_computation.14 | convolution fusion | flops 6444023808 | bytes 13631488 | tf_op jit(solution)/shard_map/dot_general | solution.py:702
  114.6 22.1 %attention_forward.1 = (bf16[1024,512]{1,0:T(8,128)(2,1)}, bf16[8,1024,1024]{2,1,0:T(8,128)(2,1)}, f32[8,1,1024]{2,1,0:T(1,128)}) custom-call(s32[1]{0:T(128)} %bitcast.place_ref, bf16[1024,1536]{1,0:T(8,128)(2,1)} %fusion.9.qkv_ref, s32[1,1024]{1,0:T(1,128)} %row_ref.1, s32[1024,128]{1,0:T(8,128)} %broadcast_in_dim.11.col_ref, f32[4,2,2048]{2,1,0:T(2,128)} %reshape.95.bias_ref), custom_call_target="tpu_custom_call" | custom-call | tf_op jit(solution)/shard_map/attention_forward/pallas_call | solution.py:167
  143.8 7.4 %collective-permute-done.8 = bf16[128,2048]{1,0:T(8,128)(2,1)S(1)} collective-permute-done((bf16[128,2048]{1,0:T(8,128)(2,1)S(1)}, bf16[128,2048]{1,0:T(8,128)(2,1)S(1)}, u32[]{:S(2)}, u32[]{:S(2)}) %collective-permute-start.8) | collective-permute-done | bytes 524320 | tf_op jit(solution)/shard_map/ppermute | solution.py:313
  158.2 15.7 %collective-permute-done.9 = bf16[256,2048]{1,0:T(8,128)(2,1)S(1)} collective-permute-done((bf16[256,2048]{1,0:T(8,128)(2,1)S(1)}, bf16[256,2048]{1,0:T(8,128)(2,1)S(1)}, u32[]{:S(2)}, u32[]{:S(2)}) %collective-permute-start.9) | collective-permute-done | bytes 1048608 | tf_op jit(solution)/shard_map/ppermute | solution.py:313
  178.8 19.9 %collective-permute-done.13 = bf16[256,2048]{1,0:T(8,128)(2,1)S(1)} collective-permute-done((bf16[256,2048]{1,0:T(8,128)(2,1)S(1)}, bf16[256,2048]{1,0:T(8,128)(2,1)S(1)}, u32[]{:S(2)}, u32[]{:S(2)}) %collective-permute-start.13) | collective-permute-done | bytes 1048608 | tf_op jit(solution)/shard_map/ppermute | solution.py:313
  211.4 18.2 %feed_forward.1 = (bf16[1024,1280]{1,0:T(8,128)(2,1)}, bf16[1024,1280]{1,0:T(8,128)(2,1)}, bf16[1024,1280]{1,0:T(8,128)(2,1)}) custom-call(bf16[1024,2048]{1,0:T(8,128)(2,1)} %constant_dynamic-update-slice_fusion.10.x_ref, bf16[2048,2560]{1,0:T(8,128)(2,1)} %all-gather.8.cloned.1.call-done.w_ref), custom_call_target="tpu_custom_call" | custom-call | tf_op jit(solution)/shard_map/feed_forward/pallas_call | solution.py:411
  229.7 10.0 %convolution_convert_fusion.2 = bf16[2048,1280]{1,0:T(8,128)(2,1)} fusion(bf16[1024,2048]{1,0:T(8,128)(2,1)} %constant_dynamic-update-slice_fusion.5.d_ref, bf16[1024,1280]{1,0:T(8,128)(2,1)} %get-tuple-element.173), kind=kOutput, calls=%fused_computation.7 | convolution fusion | flops 5371330560 | bytes 12058624 | tf_op jit(solution)/shard_map/dot_general | solution.py:25
  239.8 12.1 %all-gather.6.cloned.1.call-done.w_ref = bf16[2048,1280]{1,0:T(8,128)(2,1)} async-done(((bf16[256,1280]{1,0:T(8,128)(2,1)}), bf16[2048,1280]{1,0:T(8,128)(2,1)}) %all-gather.6.cloned.1.call-update) | async-done | bytes 5242896 | tf_op jit(solution)/shard_map/all_gather | solution.py:654
  259.2 11.9 %feed_forward_back.1 = bf16[1024,2560]{1,0:T(8,128)(2,1)} custom-call(bf16[1024,2048]{1,0:T(8,128)(2,1)} %constant_dynamic-update-slice_fusion.5.d_ref, bf16[2048,1280]{1,0:T(8,128)(2,1)} %all-gather.6.cloned.1.call-done.w_ref, bf16[1024,1280]{1,0:T(8,128)(2,1)} %get-tuple-element.132.gelu_ref, bf16[1024,1280]{1,0:T(8,128)(2,1)} %get-tuple-element.133.slope_ref), custom_call_target="tpu_custom_call" | custom-call | tf_op jit(solution)/shard_map/feed_forward_back/pallas_call | solution.py:444
  271.1 7.5 %convolution_convert_fusion.6 = bf16[256,2048]{1,0:T(8,128)(2,1)S(1)} fusion(bf16[2048,2560]{1,0:T(8,128)(2,1)} %all-gather.8.cloned.1.call-done.w_ref, bf16[1024,2560]{1,0:T(8,128)(2,1)} %feed_forward_back.1), kind=kOutput, calls=%fused_computation.26 | convolution fusion | flops 2684878848 | bytes 12845056 | tf_op jit(solution)/shard_map/dot_general | solution.py:31
  280.3 8.4 %convolution_convert_fusion.5 = bf16[512,2048]{1,0:T(8,128)(2,1)S(1)} fusion(bf16[2048,2560]{1,0:T(8,128)(2,1)} %all-gather.8.cloned.1.call-done.w_ref, bf16[1024,2560]{1,0:T(8,128)(2,1)S(1)} %copy-done.8), kind=kOutput, calls=%fused_computation.21 | convolution fusion | flops 5369757696 | bytes 15204352 | tf_op jit(solution)/shard_map/dot_general | solution.py:31
  296.8 15.6 %convolution_convert_fusion = bf16[2048,2560]{1,0:T(8,128)(2,1)} fusion(bf16[1024,2048]{1,0:T(8,128)(2,1)} %constant_dynamic-update-slice_fusion.10.x_ref, bf16[1024,2560]{1,0:T(8,128)(2,1)S(1)} %copy-done.8), kind=kOutput, calls=%fused_computation | convolution fusion | flops 10742661120 | bytes 19922944 | tf_op jit(solution)/shard_map/dot_general | solution.py:25
  312.5 8.7 %fusion.41 = f32[256,2048]{1,0:T(8,128)} fusion(bf16[2048,2560]{1,0:T(8,128)(2,1)} %all-gather.8.cloned.1.call-done.w_ref, bf16[1024,2560]{1,0:T(8,128)(2,1)} %feed_forward_back.1), kind=kOutput, calls=%fused_computation.63 | convolution fusion | flops 2684354560 | bytes 13893632 | tf_op jit(solution)/shard_map/dot_general | solution.py:31
  338.7 13.6 %collective-permute-done.23 = bf16[256,2048]{1,0:T(8,128)(2,1)S(1)} collective-permute-done((bf16[256,2048]{1,0:T(8,128)(2,1)}, bf16[256,2048]{1,0:T(8,128)(2,1)S(1)}, u32[]{:S(2)}, u32[]{:S(2)}) %collective-permute-start.23) | collective-permute-done | bytes 1048608 | tf_op jit(solution)/shard_map/ppermute | solution.py:313
  355.3 8.9 %collective-permute-done.24 = bf16[128,2048]{1,0:T(8,128)(2,1)S(1)} collective-permute-done((bf16[128,2048]{1,0:T(8,128)(2,1)S(1)}, bf16[128,2048]{1,0:T(8,128)(2,1)S(1)}, u32[]{:S(2)}, u32[]{:S(2)}) %collective-permute-start.24) | collective-permute-done | bytes 524320 | tf_op jit(solution)/shard_map/ppermute | solution.py:313
  375.5 29.0 %attention_backward.1 = (bf16[1024,1536]{1,0:T(8,128)(2,1)}, f32[4,2,2048]{2,1,0:T(2,128)}) custom-call(s32[1]{0:T(128)} %bitcast.place_ref, bf16[1024,1536]{1,0:T(8,128)(2,1)} %fusion.9.qkv_ref, bf16[1024,512]{1,0:T(8,128)(2,1)} %fusion.36.d_ref, bf16[8,1024,1024]{2,1,0:T(8,128)(2,1)} %get-tuple-element.154.e_ref, f32[8,1,1024]{2,1,0:T(1,128)} %get-tuple-element.155.inv_ref), custom_call_target="tpu_custom_call" | custom-call | tf_op jit(solution)/shard_map/attention_backward/pallas_call | solution.py:284
  404.5 9.2 %fusion.12 = bf16[768,2048]{1,0:T(8,128)(2,1)} fusion(bf16[2048,2048]{1,0:T(8,128)(2,1)} %all-gather.4.cloned.1.call-done, bf16[1024,1536]{1,0:T(8,128)(2,1)} %get-tuple-element.185), kind=kOutput, calls=%fused_computation.16 | convolution fusion | flops 4833411072 | bytes 11796480 | tf_op jit(solution)/shard_map/dot_general | solution.py:31
  413.7 8.7 %convolution_convert_fusion.1 = bf16[2048,1536]{1,0:T(8,128)(2,1)} fusion(bf16[1024,2048]{1,0:T(8,128)(2,1)S(1)} %copy-done.11, bf16[1024,1536]{1,0:T(8,128)(2,1)S(1)} %copy-done.27), kind=kOutput, calls=%fused_computation.6 | convolution fusion | flops 6445596672 | bytes 13631488 | tf_op jit(solution)/shard_map/dot_general | solution.py:25
  444.8 23.1 %collective-permute-done.34.refs_2_ = bf16[256,2560]{1,0:T(8,128)(2,1)} collective-permute-done((bf16[256,2560]{1,0:T(8,128)(2,1)}, bf16[256,2560]{1,0:T(8,128)(2,1)}, u32[]{:S(2)}, u32[]{:S(2)}) %collective-permute-start.34) | collective-permute-done | bytes 1310752 | tf_op jit(solution)/shard_map/ppermute | solution.py:313
  487.2 14.2 %all_gather.19 = f32[8,9,128]{2,1,0:T(8,128)S(1)} all-gather(f32[1,9,128]{2,1,0:T(8,128)S(1)} %maximum_bitcast_fusion), channel_id=1, replica_groups=mesh['fsdp'=8,'seq'=4] {'fsdp'}, dimensions={0}, use_global_device_ids=true | all-gather | bytes 41472 | tf_op jit(solution)/shard_map/all_gather | solution.py:814
  511.6 8.6 %place_columns.5 = (f32[256,5120]{1,0:T(8,128)}, f32[256,5120]{1,0:T(8,128)}, f32[256,128]{1,0:T(8,128)}) custom-call(s32[1]{0:T(128)} %bitcast.place_ref, bf16[256,2560]{1,0:T(8,128)(2,1)} %reduce-scatter.9.cloned.1.call-done.refs_0_, bf16[256,2560]{1,0:T(8,128)(2,1)} %collective-permute-done.33.refs_1_, bf16[256,2560]{1,0:T(8,128)(2,1)} %collective-permute-done.34.refs_2_, ...), custom_call_target="tpu_custom_call" | custom-call | bytes 21233664 | tf_op jit(solution)/shard_map/place_columns/pallas_call | solution.py:510
  (264 shorter events, 225.9 us)
Async XLA Ops:
  7.2 92.3 %all-gather.4.cloned.1.call-start = ((), (), s32[]{:S(2)}) async-start(), calls=%async_computation.4 | async-start | bytes 9437184 | tf_op jit(solution)/shard_map/all_gather | solution.py:654
  9.7 201.7 %all-gather.8.cloned.1.call-start = ((), (), s32[]{:S(2)}) async-start(), calls=%async_computation.6 | async-start | bytes 11796480 | tf_op jit(solution)/shard_map/all_gather | solution.py:654
  9.7 26.4 %collective-permute-start.1 = (bf16[256,2048]{1,0:T(8,128)(2,1)}, bf16[256,2048]{1,0:T(8,128)(2,1)S(1)}, u32[]{:S(2)}, u32[]{:S(2)}) collective-permute-start(bf16[256,2048]{1,0:T(8,128)(2,1)} %bitcast.47), channel_id=1, source_target_pairs={{0,2},{1,3},{2,0},{3,1},{4,6},{5,7},{6,4},{7,5},{8,10},{9,11},{10,... | collective-permute-start | bytes 3145736 | tf_op jit(solution)/shard_map/ppermute | solution.py:313
  58.8 193.0 %all-gather.6.cloned.1.call-start = ((), (), s32[]{:S(2)}) async-start(), calls=%async_computation.5 | async-start | bytes 5898240 | tf_op jit(solution)/shard_map/all_gather | solution.py:654
  110.9 218.5 %reduce-scatter.5.cloned.1.call-start = ((), (), s32[]{:S(2)}) async-start(), calls=%async_computation.7 | async-start | bytes 5898240 | tf_op jit(solution)/shard_map/reduce_scatter | solution.py:717
  239.7 196.2 %reduce-scatter.9.cloned.1.call-start = ((), (), s32[]{:S(2)}) async-start(), calls=%async_computation.9 | async-start | bytes 11796480 | tf_op jit(solution)/shard_map/reduce_scatter | solution.py:717
  294.8 26.3 %collective-permute-start.20 = (bf16[256,2048]{1,0:T(8,128)(2,1)}, bf16[256,2048]{1,0:T(8,128)(2,1)}, u32[]{:S(2)}, u32[]{:S(2)}) collective-permute-start(bf16[256,2048]{1,0:T(8,128)(2,1)} %get-tuple-element.142), channel_id=1, source_target_pairs={{0,1},{1,0},{2,3},{3,2},{4,5},{5,4},{6,7},{7,6},{8,9},{9,8},{10,11... | collective-permute-start | bytes 3145736 | tf_op jit(solution)/shard_map/ppermute | solution.py:313
  295.2 26.0 %collective-permute-start.21 = (bf16[256,2048]{1,0:T(8,128)(2,1)}, bf16[256,2048]{1,0:T(8,128)(2,1)}, u32[]{:S(2)}, u32[]{:S(2)}) collective-permute-start(bf16[256,2048]{1,0:T(8,128)(2,1)} %get-tuple-element.143), channel_id=1, source_target_pairs={{0,2},{1,3},{2,0},{3,1},{4,6},{5,7},{6,4},{7,5},{8,10},{9,11},{10,... | collective-permute-start | bytes 3145736 | tf_op jit(solution)/shard_map/ppermute | solution.py:313
  321.1 185.0 %reduce-scatter.7.cloned.1.call-start = ((), (), s32[]{:S(2)}) async-start(), calls=%async_computation.8 | async-start | bytes 7077888 | tf_op jit(solution)/shard_map/reduce_scatter | solution.py:717
  364.6 57.8 %collective-permute-start.30 = (bf16[256,1280]{1,0:T(8,128)(2,1)S(1)}, bf16[256,1280]{1,0:T(8,128)(2,1)}, u32[]{:S(2)}, u32[]{:S(2)}) collective-permute-start(bf16[256,1280]{1,0:T(8,128)(2,1)S(1)} %copy-done.17), channel_id=1, source_target_pairs={{0,3},{1,2},{2,1},{3,0},{4,7},{5,6},{6,5},{7,4},{8,11},{9,10},{10,... | collective-permute-start | bytes 1966088 | tf_op jit(solution)/shard_map/ppermute | solution.py:313
  366.5 55.8 %collective-permute-start.29 = (bf16[256,1280]{1,0:T(8,128)(2,1)S(1)}, bf16[256,1280]{1,0:T(8,128)(2,1)}, u32[]{:S(2)}, u32[]{:S(2)}) collective-permute-start(bf16[256,1280]{1,0:T(8,128)(2,1)S(1)} %copy-done.17), channel_id=1, source_target_pairs={{0,2},{1,3},{2,0},{3,1},{4,6},{5,7},{6,4},{7,5},{8,10},{9,11},{10,... | collective-permute-start | bytes 1966088 | tf_op jit(solution)/shard_map/ppermute | solution.py:313
  367.4 55.0 %collective-permute-start.28 = (bf16[256,1280]{1,0:T(8,128)(2,1)S(1)}, bf16[256,1280]{1,0:T(8,128)(2,1)}, u32[]{:S(2)}, u32[]{:S(2)}) collective-permute-start(bf16[256,1280]{1,0:T(8,128)(2,1)S(1)} %copy-done.17), channel_id=1, source_target_pairs={{0,1},{1,0},{2,3},{3,2},{4,5},{5,4},{6,7},{7,6},{8,9},{9,8},{10,11... | collective-permute-start | bytes 1966088 | tf_op jit(solution)/shard_map/ppermute | solution.py:313
  368.1 54.3 %collective-permute-start.26 = (bf16[256,2048]{1,0:T(8,128)(2,1)}, bf16[256,2048]{1,0:T(8,128)(2,1)}, u32[]{:S(2)}, u32[]{:S(2)}) collective-permute-start(bf16[256,2048]{1,0:T(8,128)(2,1)} %get-tuple-element.158), channel_id=1, source_target_pairs={{0,1},{1,0},{2,3},{3,2},{4,5},{5,4},{6,7},{7,6},{8,9},{9,8},{10,11... | collective-permute-start | bytes 3145736 | tf_op jit(solution)/shard_map/ppermute | solution.py:313
  369.4 53.0 %collective-permute-start.27 = (bf16[256,2048]{1,0:T(8,128)(2,1)}, bf16[256,2048]{1,0:T(8,128)(2,1)}, u32[]{:S(2)}, u32[]{:S(2)}) collective-permute-start(bf16[256,2048]{1,0:T(8,128)(2,1)} %get-tuple-element.159), channel_id=1, source_target_pairs={{0,2},{1,3},{2,0},{3,1},{4,6},{5,7},{6,4},{7,5},{8,10},{9,11},{10,... | collective-permute-start | bytes 3145736 | tf_op jit(solution)/shard_map/ppermute | solution.py:313
  422.4 118.3 %reduce-scatter.11.cloned.1.call-start = ((), (), s32[]{:S(2)}) async-start(), calls=%async_computation.10 | async-start | bytes 1310720 | tf_op jit(solution)/shard_map/reduce_scatter | solution.py:717
  435.9 32.0 %collective-permute-start.34 = (bf16[256,2560]{1,0:T(8,128)(2,1)}, bf16[256,2560]{1,0:T(8,128)(2,1)}, u32[]{:S(2)}, u32[]{:S(2)}) collective-permute-start(bf16[256,2560]{1,0:T(8,128)(2,1)} %reduce-scatter.9.cloned.1.call-done.refs_0_), channel_id=1, source_target_pairs={{0,2},{1,3},{2,0},{3,1},{4,6},{5,7},{6,4},{7,5},{8,10},{9,11},{10,... | collective-permute-start | bytes 3932168 | tf_op jit(solution)/shard_map/ppermute | solution.py:313
  437.4 32.8 %collective-permute-start.33 = (bf16[256,2560]{1,0:T(8,128)(2,1)}, bf16[256,2560]{1,0:T(8,128)(2,1)}, u32[]{:S(2)}, u32[]{:S(2)}) collective-permute-start(bf16[256,2560]{1,0:T(8,128)(2,1)} %reduce-scatter.9.cloned.1.call-done.refs_0_), channel_id=1, source_target_pairs={{0,1},{1,0},{2,3},{3,2},{4,5},{5,4},{6,7},{7,6},{8,9},{9,8},{10,11... | collective-permute-start | bytes 3932168 | tf_op jit(solution)/shard_map/ppermute | solution.py:313
  442.4 63.7 %collective-permute-start.38 = (bf16[256,2048]{1,0:T(8,128)(2,1)}, bf16[256,2048]{1,0:T(8,128)(2,1)}, u32[]{:S(2)}, u32[]{:S(2)}) collective-permute-start(bf16[256,2048]{1,0:T(8,128)(2,1)} %get-tuple-element.236), channel_id=1, source_target_pairs={{0,2},{1,3},{2,0},{3,1},{4,6},{5,7},{6,4},{7,5},{8,10},{9,11},{10,... | collective-permute-start | bytes 3145736 | tf_op jit(solution)/shard_map/ppermute | solution.py:313
  443.1 63.0 %collective-permute-start.37 = (bf16[256,2048]{1,0:T(8,128)(2,1)}, bf16[256,2048]{1,0:T(8,128)(2,1)}, u32[]{:S(2)}, u32[]{:S(2)}) collective-permute-start(bf16[256,2048]{1,0:T(8,128)(2,1)} %get-tuple-element.237), channel_id=1, source_target_pairs={{0,1},{1,0},{2,3},{3,2},{4,5},{5,4},{6,7},{7,6},{8,9},{9,8},{10,11... | collective-permute-start | bytes 3145736 | tf_op jit(solution)/shard_map/ppermute | solution.py:313
  444.1 38.6 %collective-permute-start.43 = (bf16[1024,512]{1,0:T(8,128)(2,1)}, bf16[1024,512]{1,0:T(8,128)(2,1)}, u32[]{:S(2)}, u32[]{:S(2)}) collective-permute-start(bf16[1024,512]{1,0:T(8,128)(2,1)} %convolution_convert_fusion.8), channel_id=1, source_target_pairs={{0,4},{4,0},{8,12},{12,8},{16,20},{20,16},{24,28},{28,24},{1,5},{5... | collective-permute-start | bytes 3145736 | tf_op jit(solution)/shard_map/ppermute | solution.py:313
  469.0 37.1 %collective-permute-start.35 = (bf16[128,2560]{1,0:T(8,128)(2,1)S(1)}, bf16[128,2560]{1,0:T(8,128)(2,1)}, u32[]{:S(2)}, u32[]{:S(2)}) collective-permute-start(bf16[128,2560]{1,0:T(8,128)(2,1)S(1)} %slice.218), channel_id=1, source_target_pairs={{0,1},{1,0},{2,3},{3,2},{4,5},{5,4},{6,7},{7,6},{8,9},{9,8},{10,11... | collective-permute-start | bytes 1966088 | tf_op jit(solution)/shard_map/ppermute | solution.py:313
  472.1 34.1 %collective-permute-start.36 = (bf16[128,2560]{1,0:T(8,128)(2,1)}, bf16[128,2560]{1,0:T(8,128)(2,1)}, u32[]{:S(2)}, u32[]{:S(2)}) collective-permute-start(bf16[128,2560]{1,0:T(8,128)(2,1)} %slice.219), channel_id=1, source_target_pairs={{0,2},{1,3},{2,0},{3,1},{4,6},{5,7},{6,4},{7,5},{8,10},{9,11},{10,... | collective-permute-start | bytes 1966088 | tf_op jit(solution)/shard_map/ppermute | solution.py:313
  506.2 27.2 %collective-permute-start.46 = (f32[9,128]{1,0:T(8,128)S(1)}, f32[9,128]{1,0:T(8,128)S(1)}, u32[]{:S(2)}, u32[]{:S(2)}) collective-permute-start(f32[9,128]{1,0:T(8,128)S(1)} %reduce_sum.145), channel_id=1, source_target_pairs={{0,3},{1,2},{2,1},{3,0},{4,7},{5,6},{6,5},{7,4},{8,11},{9,10},{10,... | collective-permute-start | bytes 13832 | tf_op jit(solution)/shard_map/ppermute | solution.py:313
  507.5 25.9 %collective-permute-start.45 = (f32[9,128]{1,0:T(8,128)S(1)}, f32[9,128]{1,0:T(8,128)S(1)}, u32[]{:S(2)}, u32[]{:S(2)}) collective-permute-start(f32[9,128]{1,0:T(8,128)S(1)} %reduce_sum.145), channel_id=1, source_target_pairs={{0,2},{1,3},{2,0},{3,1},{4,6},{5,7},{6,4},{7,5},{8,10},{9,11},{10,... | collective-permute-start | bytes 13832 | tf_op jit(solution)/shard_map/ppermute | solution.py:313
  (61 other events, 837.5 us)
Sparse Core Ops, SparseCore 0:
  10.2 84.7 all-gather.3
  97.2 97.9 all-gather.7
  197.4 54.4 all-gather.5
  254.6 58.6 reduce-scatter.4
  321.3 107.1 reduce-scatter.8
  430.6 68.5 reduce-scatter.6
  501.6 25.5 reduce-scatter.10

commit v6 on v5

--- a/solution.py
+++ b/solution.py
@@ -768,32 +768,25 @@
         qkv, place, context_grad, exponents, inverse, head_count, token_rows
     )
     qkv_terms = low_dot(qkv_grad[away:], qkv_w)
-    qkv_terms, qkv_grad = both(qkv_terms, qkv_grad)
-    attn_grads = rows_dot(attn_rows, qkv_grad).astype(jnp.bfloat16)
-    attn_grads, context, qkv_grad, ff_parts, down_near, attn_grad_rows, qkv_terms = both(
-        attn_grads, context, qkv_grad, ff_parts, down_near, attn_grad_rows, qkv_terms
-    )
-    attn_owned = scatter_grads(attn_grads)
+    qkv_terms, qkv_grad, ff_parts, down_near = both(qkv_terms, qkv_grad, ff_parts, down_near)
     qkv_near, qkv_far = split_terms(qkv_terms)
     qkv_passing = scatter_begin(qkv_far)
+    attn_grads = rows_dot(attn_rows, qkv_grad).astype(jnp.bfloat16)
+    attn_grads, context, qkv_grad, attn_grad_rows, qkv_passing, gate_up_owned, hidden = both(
+        attn_grads, context, qkv_grad, attn_grad_rows, qkv_passing, gate_up_owned, hidden
+    )
+    attn_owned = scatter_grads(attn_grads)
+    gate_up_near = gather_begin(gate_up_owned)
+    attn_in_parts = scatter_end(scatter_add(qkv_near, qkv_passing))
     output_own, output_other = turn_halves(attn_grad_rows, core, fsdp_count)
     output_away = jnp.dot(
         output_other, context, preferred_element_type=jnp.float32
     ).astype(jnp.bfloat16)
-    qkv_passing, gate_up_owned, output_away, output_own, hidden, down_near, qkv_grad = both(
-        qkv_passing, gate_up_owned, output_away, output_own, hidden, down_near, qkv_grad
-    )
+    output_added = swap(output_away, "fsdp", 1)
     attn_in_own = cols_dot(qkv_grad[:away], qkv_w)
-    gate_up_near = gather_begin(gate_up_owned)
-    output_added = swap(output_away, "fsdp", 1)
     output_grad = added_dot(output_own, context, output_added)
-    output_owned = scatter_grads(output_grad, groups)
-    attn_in_parts = scatter_end(scatter_add(qkv_near, qkv_passing))
-    gate_up_pieces = gather_end(gate_up_owned, gate_up_near)
-    down_pieces = gather_end(down_owned, down_near)
     ff_out = add_parts(cols_dot(hidden[:away], down_w), ff_parts)
     result = resid + ff_out
-    (down_out,) = place_columns(down_pieces, place, [(0, 0, 0, unit_count)], [unit_count])
     own_segments = lax.dynamic_slice_in_dim(segment_row, seq_place * token_rows, token_rows, 0)
     valid = (own_segments >= 0).astype(jnp.float32)
     stat_terms = jnp.stack(
@@ -811,9 +804,18 @@
         jnp.zeros(rel_table.shape, jnp.float32), table_part, seq_place * head_count, 0
     )
     packed = jnp.concatenate([full_table.reshape(-1), jnp.pad(stat_terms, (0, TILE - 4))])
+    gate_up_near, packed, output_grad, attn_in_own, result = both(
+        gate_up_near, packed, output_grad, attn_in_own, result
+    )
+    output_owned = scatter_grads(output_grad, groups)
+    gate_up_pieces = gather_end(gate_up_owned, gate_up_near)
+    down_pieces = gather_end(down_owned, down_near)
+    (down_out,) = place_columns(down_pieces, place, [(0, 0, 0, unit_count)], [unit_count])
     summed = jnp.sum(lax.all_gather(packed.reshape(-1, TILE), "fsdp"), axis=0)
-    attn_owned, result, summed, down_out, gate_up_pieces, attn_in_parts = both(
-        attn_owned, result, summed, down_out, gate_up_pieces, attn_in_parts
+    summed, attn_in_parts = both(summed, attn_in_parts)
+    summed = seq_sum(summed)
+    attn_owned, summed, down_out, gate_up_pieces, attn_in_parts = both(
+        attn_owned, summed, down_out, gate_up_pieces, attn_in_parts
     )
     attn_near = gather_begin(attn_owned)
     attn_in_grad = add_parts(attn_in_own, attn_in_parts)
@@ -824,8 +826,8 @@
     )
     attn_near, stream_grad, gate_out, up_out = both(attn_near, stream_grad, gate_out, up_out)
     attn_pieces = gather_end(attn_owned, attn_near)
-    summed = seq_sum(summed).reshape(-1)
-    attn_pieces, output_owned, summed = both(attn_pieces, output_owned, summed)
+    attn_pieces[-1][0], output_owned = both(attn_pieces[-1][0], output_owned)
+    summed = summed.reshape(-1)
     output_near = gather_begin(output_owned, relay=False)
     attn_outs = place_columns(
         attn_pieces,

time: 572 us -> 562 us (0.983)
  waiting for transfers between devices: 163 us -> 153 us
    ppermute x50, waiting for transfers between devices: 151 us -> 137 us  [swap(): lax.ppermute(piece, axis, [(i, i ^ step) for i in range(lax.axis_size(axi...]
    unnamed x73 -> x97, local copies, waits for them, and re-layouts: 18.9 us -> 20.3 us
  transfers between devices with their start and end apart: 57 -> 57, of which waited for: 26 -> 30; matrix products, arithmetic and copies ran while one was open for 32% -> 32% of each run, Pallas kernels for 20% -> 20%
where the time goes in v6:
time: 562 us; the launch traced here: 555 us
  waiting for transfers between devices  153 us (27%)
  Pallas kernels  119 us (21%)
  matrix products  114 us (20%)
  starting transfers between devices  58.5 us (10%)
  local copies, waits for them, and re-layouts  34.7 us (6%)
  other arithmetic  33.5 us (6%)
  blocking collectives  26.6 us (5%)
  between operations  16 us (3%)
    ppermute x50, waiting for transfers between devices, swap(): lax.ppermute(piece, axis, [(i, i ^ step) for i in range(lax.axis_size(axi...  137 us
    dot_general x10, matrix products, cols_dot(): lax.dot_general(left, right, (((1,), (1,)), ((), ())), preferred_element_...  57.7 us
    ppermute x50, starting transfers between devices, swap(): lax.ppermute(piece, axis, [(i, i ^ step) for i in range(lax.axis_size(axi...  57.6 us
    dot_general x3, matrix products, rows_dot(): lax.dot_general(left, right, (((0,), (0,)), ((), ())), preferred_element_...  34.5 us
    pallas_call x1, Pallas kernels, attention_backward(): pl.pallas_call(functools.partial(backward_kernel, block, token_rows), gri...  29 us
    pallas_call x4, Pallas kernels, place_columns(): pl.pallas_call(functools.partial(place_kernel, moves, lengths, block, wid...  23.3 us
    pallas_call x1, Pallas kernels, attention_forward(): pl.pallas_call(functools.partial(forward_kernel, block, token_rows), grid...  22.1 us
    unnamed x97, local copies, waits for them, and re-layouts  20.3 us
  transfers between devices with their start and end apart: 57, of which 30 were waited for; matrix products, arithmetic and copies ran while one was open for 32% of the time, Pallas kernels for 20%

profile of v6, /device:TPU:0, one launch (start us, length us, event | category | flops | bytes accessed | tf_op | source)
XLA Modules:
  0.0 554.8 jit_solution(15972781812506756145)
XLA Ops:
  14.3 12.0 %all_gather.15 = bf16[2,2048]{1,0:T(2,128)(2,1)S(1)} all-gather(bf16[2,256]{1,0:T(2,128)(2,1)S(1)} %pad_maximum_fusion.1), channel_id=1, replica_groups=mesh['fsdp'=8,'seq'=4] {'fsdp'}, dimensions={1}, use_global_device_ids=true | all-gather | bytes 9216 | tf_op jit(solution)/shard_map/all_gather | solution.py:670
  26.3 9.8 %collective-permute-done.1 = bf16[256,2048]{1,0:T(8,128)(2,1)S(1)} collective-permute-done((bf16[256,2048]{1,0:T(8,128)(2,1)}, bf16[256,2048]{1,0:T(8,128)(2,1)S(1)}, u32[]{:S(2)}, u32[]{:S(2)}) %collective-permute-start.1) | collective-permute-done | bytes 1048608 | tf_op jit(solution)/shard_map/ppermute | solution.py:313
  64.2 17.9 %collective-permute-done.5 = bf16[256,2048]{1,0:T(8,128)(2,1)} collective-permute-done((bf16[256,2048]{1,0:T(8,128)(2,1)}, bf16[256,2048]{1,0:T(8,128)(2,1)}, u32[]{:S(2)}, u32[]{:S(2)}) %collective-permute-start.5) | collective-permute-done | bytes 1048608 | tf_op jit(solution)/shard_map/ppermute | solution.py:313
  99.5 11.4 %fusion.9.qkv_ref = bf16[1024,1536]{1,0:T(8,128)(2,1)} fusion(bf16[1024,2048]{1,0:T(8,128)(2,1)} %fusion.2, bf16[2048,2048]{1,0:T(8,128)(2,1)} %all-gather.4.cloned.1.call-done), kind=kOutput, calls=%fused_computation.14 | convolution fusion | flops 6444023808 | bytes 13631488 | tf_op jit(solution)/shard_map/dot_general | solution.py:702
  114.6 22.1 %attention_forward.1 = (bf16[1024,512]{1,0:T(8,128)(2,1)}, bf16[8,1024,1024]{2,1,0:T(8,128)(2,1)}, f32[8,1,1024]{2,1,0:T(1,128)}) custom-call(s32[1]{0:T(128)} %bitcast.place_ref, bf16[1024,1536]{1,0:T(8,128)(2,1)} %fusion.9.qkv_ref, s32[1,1024]{1,0:T(1,128)} %row_ref.1, s32[1024,128]{1,0:T(8,128)} %broadcast_in_dim.11.col_ref, f32[4,2,2048]{2,1,0:T(2,128)} %reshape.89.bias_ref), custom_call_target="tpu_custom_call" | custom-call | tf_op jit(solution)/shard_map/attention_forward/pallas_call | solution.py:167
  143.8 7.3 %collective-permute-done.8 = bf16[128,2048]{1,0:T(8,128)(2,1)S(1)} collective-permute-done((bf16[128,2048]{1,0:T(8,128)(2,1)S(1)}, bf16[128,2048]{1,0:T(8,128)(2,1)S(1)}, u32[]{:S(2)}, u32[]{:S(2)}) %collective-permute-start.8) | collective-permute-done | bytes 524320 | tf_op jit(solution)/shard_map/ppermute | solution.py:313
  158.3 15.7 %collective-permute-done.9 = bf16[256,2048]{1,0:T(8,128)(2,1)S(1)} collective-permute-done((bf16[256,2048]{1,0:T(8,128)(2,1)S(1)}, bf16[256,2048]{1,0:T(8,128)(2,1)S(1)}, u32[]{:S(2)}, u32[]{:S(2)}) %collective-permute-start.9) | collective-permute-done | bytes 1048608 | tf_op jit(solution)/shard_map/ppermute | solution.py:313
  178.9 19.7 %collective-permute-done.13 = bf16[256,2048]{1,0:T(8,128)(2,1)S(1)} collective-permute-done((bf16[256,2048]{1,0:T(8,128)(2,1)S(1)}, bf16[256,2048]{1,0:T(8,128)(2,1)S(1)}, u32[]{:S(2)}, u32[]{:S(2)}) %collective-permute-start.13) | collective-permute-done | bytes 1048608 | tf_op jit(solution)/shard_map/ppermute | solution.py:313
  211.5 18.3 %feed_forward.1 = (bf16[1024,1280]{1,0:T(8,128)(2,1)}, bf16[1024,1280]{1,0:T(8,128)(2,1)}, bf16[1024,1280]{1,0:T(8,128)(2,1)}) custom-call(bf16[1024,2048]{1,0:T(8,128)(2,1)} %constant_dynamic-update-slice_fusion.10.x_ref, bf16[2048,2560]{1,0:T(8,128)(2,1)} %all-gather.8.cloned.1.call-done.w_ref), custom_call_target="tpu_custom_call" | custom-call | tf_op jit(solution)/shard_map/feed_forward/pallas_call | solution.py:411
  229.8 10.2 %convolution_convert_fusion.2 = bf16[2048,1280]{1,0:T(8,128)(2,1)} fusion(bf16[1024,2048]{1,0:T(8,128)(2,1)} %constant_dynamic-update-slice_fusion.5.d_ref, bf16[1024,1280]{1,0:T(8,128)(2,1)} %get-tuple-element.161), kind=kOutput, calls=%fused_computation.7 | convolution fusion | flops 5371330560 | bytes 12058624 | tf_op jit(solution)/shard_map/dot_general | solution.py:25
  240.1 11.7 %all-gather.6.cloned.1.call-done.w_ref = bf16[2048,1280]{1,0:T(8,128)(2,1)} async-done(((bf16[256,1280]{1,0:T(8,128)(2,1)}), bf16[2048,1280]{1,0:T(8,128)(2,1)}) %all-gather.6.cloned.1.call-update) | async-done | bytes 5242896 | tf_op jit(solution)/shard_map/all_gather | solution.py:654
  259.2 11.9 %feed_forward_back.1 = bf16[1024,2560]{1,0:T(8,128)(2,1)} custom-call(bf16[1024,2048]{1,0:T(8,128)(2,1)} %constant_dynamic-update-slice_fusion.5.d_ref, bf16[2048,1280]{1,0:T(8,128)(2,1)} %all-gather.6.cloned.1.call-done.w_ref, bf16[1024,1280]{1,0:T(8,128)(2,1)} %get-tuple-element.128.gelu_ref, bf16[1024,1280]{1,0:T(8,128)(2,1)} %get-tuple-element.129.slope_ref), custom_call_target="tpu_custom_call" | custom-call | tf_op jit(solution)/shard_map/feed_forward_back/pallas_call | solution.py:444
  271.1 7.5 %convolution_convert_fusion.6 = bf16[256,2048]{1,0:T(8,128)(2,1)S(1)} fusion(bf16[2048,2560]{1,0:T(8,128)(2,1)} %all-gather.8.cloned.1.call-done.w_ref, bf16[1024,2560]{1,0:T(8,128)(2,1)} %feed_forward_back.1), kind=kOutput, calls=%fused_computation.24 | convolution fusion | flops 2684878848 | bytes 12845056 | tf_op jit(solution)/shard_map/dot_general | solution.py:31
  280.3 8.4 %convolution_convert_fusion.5 = bf16[512,2048]{1,0:T(8,128)(2,1)S(1)} fusion(bf16[2048,2560]{1,0:T(8,128)(2,1)} %all-gather.8.cloned.1.call-done.w_ref, bf16[1024,2560]{1,0:T(8,128)(2,1)S(1)} %copy-done.9), kind=kOutput, calls=%fused_computation.21 | convolution fusion | flops 5369757696 | bytes 15204352 | tf_op jit(solution)/shard_map/dot_general | solution.py:31
  296.8 15.6 %convolution_convert_fusion = bf16[2048,2560]{1,0:T(8,128)(2,1)} fusion(bf16[1024,2048]{1,0:T(8,128)(2,1)} %constant_dynamic-update-slice_fusion.10.x_ref, bf16[1024,2560]{1,0:T(8,128)(2,1)S(1)} %copy-done.9), kind=kOutput, calls=%fused_computation | convolution fusion | flops 10742661120 | bytes 19922944 | tf_op jit(solution)/shard_map/dot_general | solution.py:25
  312.5 8.7 %fusion.35 = f32[256,2048]{1,0:T(8,128)} fusion(bf16[2048,2560]{1,0:T(8,128)(2,1)} %all-gather.8.cloned.1.call-done.w_ref, bf16[1024,2560]{1,0:T(8,128)(2,1)} %feed_forward_back.1), kind=kOutput, calls=%fused_computation.62 | convolution fusion | flops 2684354560 | bytes 13893632 | tf_op jit(solution)/shard_map/dot_general | solution.py:31
  337.1 15.0 %collective-permute-done.23 = bf16[256,2048]{1,0:T(8,128)(2,1)S(1)} collective-permute-done((bf16[256,2048]{1,0:T(8,128)(2,1)}, bf16[256,2048]{1,0:T(8,128)(2,1)S(1)}, u32[]{:S(2)}, u32[]{:S(2)}) %collective-permute-start.23) | collective-permute-done | bytes 1048608 | tf_op jit(solution)/shard_map/ppermute | solution.py:313
  355.0 8.9 %collective-permute-done.24 = bf16[128,2048]{1,0:T(8,128)(2,1)S(1)} collective-permute-done((bf16[128,2048]{1,0:T(8,128)(2,1)S(1)}, bf16[128,2048]{1,0:T(8,128)(2,1)S(1)}, u32[]{:S(2)}, u32[]{:S(2)}) %collective-permute-start.24) | collective-permute-done | bytes 524320 | tf_op jit(solution)/shard_map/ppermute | solution.py:313
  375.1 29.0 %attention_backward.1 = (bf16[1024,1536]{1,0:T(8,128)(2,1)}, f32[4,2,2048]{2,1,0:T(2,128)}) custom-call(s32[1]{0:T(128)} %bitcast.place_ref, bf16[1024,1536]{1,0:T(8,128)(2,1)} %fusion.9.qkv_ref, bf16[1024,512]{1,0:T(8,128)(2,1)} %fusion.30.d_ref, bf16[8,1024,1024]{2,1,0:T(8,128)(2,1)} %get-tuple-element.150.e_ref, f32[8,1,1024]{2,1,0:T(1,128)} %get-tuple-element.151.inv_ref), custom_call_target="tpu_custom_call" | custom-call | tf_op jit(solution)/shard_map/attention_backward/pallas_call | solution.py:284
  404.1 8.1 %fusion.12 = bf16[768,2048]{1,0:T(8,128)(2,1)S(1)} fusion(bf16[2048,2048]{1,0:T(8,128)(2,1)} %all-gather.4.cloned.1.call-done, bf16[1024,1536]{1,0:T(8,128)(2,1)} %get-tuple-element.168), kind=kOutput, calls=%fused_computation.16 | convolution fusion | flops 4833411072 | bytes 11796480 | tf_op jit(solution)/shard_map/dot_general | solution.py:31
  418.7 8.7 %convolution_convert_fusion.1 = bf16[2048,1536]{1,0:T(8,128)(2,1)} fusion(bf16[1024,2048]{1,0:T(8,128)(2,1)S(1)} %copy-done.12, bf16[1024,1536]{1,0:T(8,128)(2,1)S(1)} %copy-done.35), kind=kOutput, calls=%fused_computation.6 | convolution fusion | flops 6445596672 | bytes 13631488 | tf_op jit(solution)/shard_map/dot_general | solution.py:25
  471.4 14.6 %all_gather.19 = f32[8,9,128]{2,1,0:T(8,128)S(1)} all-gather(f32[1,9,128]{2,1,0:T(8,128)S(1)} %bitcast.60), channel_id=1, replica_groups=mesh['fsdp'=8,'seq'=4] {'fsdp'}, dimensions={0}, use_global_device_ids=true | all-gather | bytes 41472 | tf_op jit(solution)/shard_map/all_gather | solution.py:814
  504.2 8.6 %place_columns.5 = (f32[256,5120]{1,0:T(8,128)}, f32[256,5120]{1,0:T(8,128)}, f32[256,128]{1,0:T(8,128)}) custom-call(s32[1]{0:T(128)} %bitcast.place_ref, bf16[256,2560]{1,0:T(8,128)(2,1)} %reduce-scatter.7.cloned.1.call-done.refs_0_, bf16[256,2560]{1,0:T(8,128)(2,1)} %collective-permute-done.33.refs_1_, bf16[256,2560]{1,0:T(8,128)(2,1)} %collective-permute-done.34.refs_2_, ...), custom_call_target="tpu_custom_call" | custom-call | bytes 21233664 | tf_op jit(solution)/shard_map/place_columns/pallas_call | solution.py:510
  534.3 6.5 %place_columns.6 = (f32[256,2048]{1,0:T(8,128)}, f32[256,2048]{1,0:T(8,128)}, f32[256,2048]{1,0:T(8,128)}, f32[256,128]{1,0:T(8,128)}) custom-call(s32[1]{0:T(128)} %bitcast.place_ref, bf16[256,1536]{1,0:T(8,128)(2,1)} %reduce-scatter.9.cloned.1.call-done.refs_0_, bf16[256,1536]{1,0:T(8,128)(2,1)} %copy-done.17, bf16[256,1536]{1,0:T(8,128)(2,1)} %copy-done.16, ...), custom_call_target="tpu_custom_call" | custom-call | bytes 12845056 | tf_op jit(solution)/shard_map/place_columns/pallas_call | solution.py:510
  (291 shorter events, 231.4 us)
Async XLA Ops:
  7.2 92.3 %all-gather.4.cloned.1.call-start = ((), (), s32[]{:S(2)}) async-start(), calls=%async_computation.4 | async-start | bytes 9437184 | tf_op jit(solution)/shard_map/all_gather | solution.py:654
  9.7 201.9 %all-gather.8.cloned.1.call-start = ((), (), s32[]{:S(2)}) async-start(), calls=%async_computation.6 | async-start | bytes 11796480 | tf_op jit(solution)/shard_map/all_gather | solution.py:654
  9.7 26.4 %collective-permute-start.1 = (bf16[256,2048]{1,0:T(8,128)(2,1)}, bf16[256,2048]{1,0:T(8,128)(2,1)S(1)}, u32[]{:S(2)}, u32[]{:S(2)}) collective-permute-start(bf16[256,2048]{1,0:T(8,128)(2,1)} %bitcast.45), channel_id=1, source_target_pairs={{0,2},{1,3},{2,0},{3,1},{4,6},{5,7},{6,4},{7,5},{8,10},{9,11},{10,... | collective-permute-start | bytes 3145736 | tf_op jit(solution)/shard_map/ppermute | solution.py:313
  12.7 24.9 %collective-permute-start = (bf16[256,2048]{1,0:T(8,128)(2,1)}, bf16[256,2048]{1,0:T(8,128)(2,1)}, u32[]{:S(2)}, u32[]{:S(2)}) collective-permute-start(bf16[256,2048]{1,0:T(8,128)(2,1)} %bitcast.46), channel_id=1, source_target_pairs={{0,1},{1,0},{2,3},{3,2},{4,5},{5,4},{6,7},{7,6},{8,9},{9,8},{10,11... | collective-permute-start | bytes 3145736 | tf_op jit(solution)/shard_map/ppermute | solution.py:313
  58.8 193.0 %all-gather.6.cloned.1.call-start = ((), (), s32[]{:S(2)}) async-start(), calls=%async_computation.5 | async-start | bytes 5898240 | tf_op jit(solution)/shard_map/all_gather | solution.py:654
  60.5 23.8 %collective-permute-start.4 = (bf16[256,2048]{1,0:T(8,128)(2,1)}, bf16[256,2048]{1,0:T(8,128)(2,1)}, u32[]{:S(2)}, u32[]{:S(2)}) collective-permute-start(bf16[256,2048]{1,0:T(8,128)(2,1)} %bitcast.50), channel_id=1, source_target_pairs={{0,1},{1,0},{2,3},{3,2},{4,5},{5,4},{6,7},{7,6},{8,9},{9,8},{10,11... | collective-permute-start | bytes 3145736 | tf_op jit(solution)/shard_map/ppermute | solution.py:313
  110.9 218.3 %reduce-scatter.5.cloned.1.call-start = ((), (), s32[]{:S(2)}) async-start(), calls=%async_computation.7 | async-start | bytes 5898240 | tf_op jit(solution)/shard_map/reduce_scatter | solution.py:717
  240.1 191.6 %reduce-scatter.7.cloned.1.call-start = ((), (), s32[]{:S(2)}) async-start(), calls=%async_computation.8 | async-start | bytes 11796480 | tf_op jit(solution)/shard_map/reduce_scatter | solution.py:717
  294.8 26.3 %collective-permute-start.20 = (bf16[256,2048]{1,0:T(8,128)(2,1)}, bf16[256,2048]{1,0:T(8,128)(2,1)}, u32[]{:S(2)}, u32[]{:S(2)}) collective-permute-start(bf16[256,2048]{1,0:T(8,128)(2,1)} %get-tuple-element.138), channel_id=1, source_target_pairs={{0,1},{1,0},{2,3},{3,2},{4,5},{5,4},{6,7},{7,6},{8,9},{9,8},{10,11... | collective-permute-start | bytes 3145736 | tf_op jit(solution)/shard_map/ppermute | solution.py:313
  295.2 26.0 %collective-permute-start.21 = (bf16[256,2048]{1,0:T(8,128)(2,1)}, bf16[256,2048]{1,0:T(8,128)(2,1)}, u32[]{:S(2)}, u32[]{:S(2)}) collective-permute-start(bf16[256,2048]{1,0:T(8,128)(2,1)} %get-tuple-element.139), channel_id=1, source_target_pairs={{0,2},{1,3},{2,0},{3,1},{4,6},{5,7},{6,4},{7,5},{8,10},{9,11},{10,... | collective-permute-start | bytes 3145736 | tf_op jit(solution)/shard_map/ppermute | solution.py:313
  321.1 180.9 %reduce-scatter.9.cloned.1.call-start = ((), (), s32[]{:S(2)}) async-start(), calls=%async_computation.9 | async-start | bytes 7077888 | tf_op jit(solution)/shard_map/reduce_scatter | solution.py:717
  329.2 24.6 %collective-permute-start.22 = (bf16[256,2048]{1,0:T(8,128)(2,1)}, bf16[256,2048]{1,0:T(8,128)(2,1)S(1)}, u32[]{:S(2)}, u32[]{:S(2)}) collective-permute-start(bf16[256,2048]{1,0:T(8,128)(2,1)} %get-tuple-element.144), channel_id=1, source_target_pairs={{0,1},{1,0},{2,3},{3,2},{4,5},{5,4},{6,7},{7,6},{8,9},{9,8},{10,11... | collective-permute-start | bytes 3145736 | tf_op jit(solution)/shard_map/ppermute | solution.py:313
  364.4 47.8 %collective-permute-start.30 = (bf16[256,1280]{1,0:T(8,128)(2,1)S(1)}, bf16[256,1280]{1,0:T(8,128)(2,1)S(1)}, u32[]{:S(2)}, u32[]{:S(2)}) collective-permute-start(bf16[256,1280]{1,0:T(8,128)(2,1)S(1)} %copy-done.20), channel_id=1, source_target_pairs={{0,3},{1,2},{2,1},{3,0},{4,7},{5,6},{6,5},{7,4},{8,11},{9,10},{10,... | collective-permute-start | bytes 1966088 | tf_op jit(solution)/shard_map/ppermute | solution.py:313
  366.2 46.0 %collective-permute-start.29 = (bf16[256,1280]{1,0:T(8,128)(2,1)S(1)}, bf16[256,1280]{1,0:T(8,128)(2,1)S(1)}, u32[]{:S(2)}, u32[]{:S(2)}) collective-permute-start(bf16[256,1280]{1,0:T(8,128)(2,1)S(1)} %copy-done.20), channel_id=1, source_target_pairs={{0,2},{1,3},{2,0},{3,1},{4,6},{5,7},{6,4},{7,5},{8,10},{9,11},{10,... | collective-permute-start | bytes 1966088 | tf_op jit(solution)/shard_map/ppermute | solution.py:313
  367.1 45.1 %collective-permute-start.28 = (bf16[256,1280]{1,0:T(8,128)(2,1)S(1)}, bf16[256,1280]{1,0:T(8,128)(2,1)S(1)}, u32[]{:S(2)}, u32[]{:S(2)}) collective-permute-start(bf16[256,1280]{1,0:T(8,128)(2,1)S(1)} %copy-done.20), channel_id=1, source_target_pairs={{0,1},{1,0},{2,3},{3,2},{4,5},{5,4},{6,7},{7,6},{8,9},{9,8},{10,11... | collective-permute-start | bytes 1966088 | tf_op jit(solution)/shard_map/ppermute | solution.py:313
  367.9 47.5 %collective-permute-start.26 = (bf16[256,2048]{1,0:T(8,128)(2,1)S(1)}, bf16[256,2048]{1,0:T(8,128)(2,1)}, u32[]{:S(2)}, u32[]{:S(2)}) collective-permute-start(bf16[256,2048]{1,0:T(8,128)(2,1)S(1)} %get-tuple-element.153), channel_id=1, source_target_pairs={{0,1},{1,0},{2,3},{3,2},{4,5},{5,4},{6,7},{7,6},{8,9},{9,8},{10,11... | collective-permute-start | bytes 3145736 | tf_op jit(solution)/shard_map/ppermute | solution.py:313
  369.2 46.3 %collective-permute-start.27 = (bf16[256,2048]{1,0:T(8,128)(2,1)S(1)}, bf16[256,2048]{1,0:T(8,128)(2,1)}, u32[]{:S(2)}, u32[]{:S(2)}) collective-permute-start(bf16[256,2048]{1,0:T(8,128)(2,1)S(1)} %get-tuple-element.154), channel_id=1, source_target_pairs={{0,2},{1,3},{2,0},{3,1},{4,6},{5,7},{6,4},{7,5},{8,10},{9,11},{10,... | collective-permute-start | bytes 3145736 | tf_op jit(solution)/shard_map/ppermute | solution.py:313
  431.7 95.8 %reduce-scatter.11.cloned.1.call-start = ((), (), s32[]{:S(2)}) async-start(), calls=%async_computation.10 | async-start | bytes 1310720 | tf_op jit(solution)/shard_map/reduce_scatter | solution.py:717
  433.5 33.9 %collective-permute-start.34 = (bf16[256,2560]{1,0:T(8,128)(2,1)}, bf16[256,2560]{1,0:T(8,128)(2,1)}, u32[]{:S(2)}, u32[]{:S(2)}) collective-permute-start(bf16[256,2560]{1,0:T(8,128)(2,1)} %reduce-scatter.7.cloned.1.call-done.refs_0_), channel_id=1, source_target_pairs={{0,2},{1,3},{2,0},{3,1},{4,6},{5,7},{6,4},{7,5},{8,10},{9,11},{10,... | collective-permute-start | bytes 3932168 | tf_op jit(solution)/shard_map/ppermute | solution.py:313
  434.0 33.4 %collective-permute-start.33 = (bf16[256,2560]{1,0:T(8,128)(2,1)}, bf16[256,2560]{1,0:T(8,128)(2,1)}, u32[]{:S(2)}, u32[]{:S(2)}) collective-permute-start(bf16[256,2560]{1,0:T(8,128)(2,1)} %reduce-scatter.7.cloned.1.call-done.refs_0_), channel_id=1, source_target_pairs={{0,1},{1,0},{2,3},{3,2},{4,5},{5,4},{6,7},{7,6},{8,9},{9,8},{10,11... | collective-permute-start | bytes 3932168 | tf_op jit(solution)/shard_map/ppermute | solution.py:313
  439.1 48.9 %collective-permute-start.37 = (bf16[256,2048]{1,0:T(8,128)(2,1)}, bf16[256,2048]{1,0:T(8,128)(2,1)}, u32[]{:S(2)}, u32[]{:S(2)}) collective-permute-start(bf16[256,2048]{1,0:T(8,128)(2,1)} %get-tuple-element.228), channel_id=1, source_target_pairs={{0,2},{1,3},{2,0},{3,1},{4,6},{5,7},{6,4},{7,5},{8,10},{9,11},{10,... | collective-permute-start | bytes 3145736 | tf_op jit(solution)/shard_map/ppermute | solution.py:313
  439.8 48.7 %collective-permute-start.36 = (bf16[256,2048]{1,0:T(8,128)(2,1)}, bf16[256,2048]{1,0:T(8,128)(2,1)}, u32[]{:S(2)}, u32[]{:S(2)}) collective-permute-start(bf16[256,2048]{1,0:T(8,128)(2,1)} %get-tuple-element.229), channel_id=1, source_target_pairs={{0,1},{1,0},{2,3},{3,2},{4,5},{5,4},{6,7},{7,6},{8,9},{9,8},{10,11... | collective-permute-start | bytes 3145736 | tf_op jit(solution)/shard_map/ppermute | solution.py:313
  469.7 31.5 %collective-permute-start.41 = (bf16[128,2560]{1,0:T(8,128)(2,1)S(1)}, bf16[128,2560]{1,0:T(8,128)(2,1)S(1)}, u32[]{:S(2)}, u32[]{:S(2)}) collective-permute-start(bf16[128,2560]{1,0:T(8,128)(2,1)S(1)} %slice.189), channel_id=1, source_target_pairs={{0,1},{1,0},{2,3},{3,2},{4,5},{5,4},{6,7},{7,6},{8,9},{9,8},{10,11... | collective-permute-start | bytes 1966088 | tf_op jit(solution)/shard_map/ppermute | solution.py:313
  470.1 31.2 %collective-permute-start.42 = (bf16[128,2560]{1,0:T(8,128)(2,1)S(1)}, bf16[128,2560]{1,0:T(8,128)(2,1)}, u32[]{:S(2)}, u32[]{:S(2)}) collective-permute-start(bf16[128,2560]{1,0:T(8,128)(2,1)S(1)} %slice.190), channel_id=1, source_target_pairs={{0,2},{1,3},{2,0},{3,1},{4,6},{5,7},{6,4},{7,5},{8,10},{9,11},{10,... | collective-permute-start | bytes 1966088 | tf_op jit(solution)/shard_map/ppermute | solution.py:313
  (73 other events, 852.5 us)
Sparse Core Ops, SparseCore 0:
  10.2 84.7 all-gather.3
  97.2 97.9 all-gather.7
  197.4 54.4 all-gather.5
  254.6 58.6 reduce-scatter.4
  321.3 107.1 reduce-scatter.6
  431.9 67.8 reduce-scatter.8
  502.1 25.4 reduce-scatter.10

commit v7 on v6

--- a/solution.py
+++ b/solution.py
@@ -35,6 +35,51 @@
 
 def norm_back(grad_hat, normed, scale):
     return scale * (grad_hat - normed * jnp.mean(grad_hat * normed, axis=-1, keepdims=True))
+
+
+def norm_backward_kernel(lengths, own_ref, up_ref, resid_ref, gain_ref, *refs):
+    *parts, out_ref, low_ref = refs
+    resid = resid_ref[...]
+    scale = lax.rsqrt(jnp.mean(resid * resid, axis=-1, keepdims=True) + EPSILON)
+    grad = own_ref[...].astype(jnp.float32)
+    first = 0
+    for length in lengths:
+        part = parts[first][...]
+        if length == 2:
+            upper = pl.program_id(0) < pl.num_programs(0) // 2
+            part = jnp.where(upper, part, parts[first + 1][...])
+        grad = grad + part.astype(jnp.float32)
+        first += length
+    out = up_ref[...].astype(jnp.float32)
+    out = out + norm_back(grad * gain_ref[...], resid * scale, scale)
+    out_ref[...] = out
+    low_ref[...] = out.astype(jnp.bfloat16)
+
+
+def norm_backward(own, parts, upstream, resid, gain):
+    rows, width = resid.shape
+    block = min(64, rows // 2)
+    steps = rows // block
+    rowwise = pl.BlockSpec((block, width), lambda i: (i, 0))
+    halves = [
+        pl.BlockSpec((block, width), lambda i: (jnp.minimum(i, steps // 2 - 1), 0)),
+        pl.BlockSpec((block, width), lambda i: (jnp.maximum(i - steps // 2, 0), 0)),
+    ]
+    lengths = tuple(len(part) for part in parts)
+    part_specs = [spec for length in lengths for spec in (halves if length == 2 else [rowwise])]
+    return pl.pallas_call(
+        functools.partial(norm_backward_kernel, lengths),
+        grid=(steps,),
+        in_specs=[rowwise] * 3 + [pl.BlockSpec((1, width), lambda i: (0, 0))] + part_specs,
+        out_specs=[rowwise, rowwise],
+        out_shape=[
+            jax.ShapeDtypeStruct((rows, width), jnp.float32),
+            jax.ShapeDtypeStruct((rows, width), jnp.bfloat16),
+        ],
+        compiler_params=pltpu.CompilerParams(vmem_limit_bytes=VMEM_BYTES),
+        cost_estimate=NO_COST,
+        name="norm_backward",
+    )(own, upstream, resid, gain[None, :], *[piece for part in parts for piece in part])
 
 
 def half_lanes(shape, which):
@@ -369,6 +414,28 @@
     return tuple(swap(part, "seq", k + 1) for k, part in enumerate(sums))
 
 
+def scatter_early(near):
+    if lax.axis_size("seq") != 4:
+        return ()
+    size = near.shape[0] // 2
+    half = size // 2
+    return swap(near[:half], "seq", 1), swap(near[size + half :], "seq", 2)
+
+
+def scatter_late(near, passing, early):
+    if not passing:
+        return [(part,) for part in scatter_end(scatter_add(near, passing))]
+    size = near.shape[0] // 2
+    half = size // 2
+    upper, lower = (part.astype(jnp.float32) for part in passing)
+    first = near[half:size].astype(jnp.float32) + lower
+    second = near[size : size + half].astype(jnp.float32) + upper
+    first_lower = swap(first.astype(jnp.bfloat16), "seq", 1)
+    second_upper = swap(second.astype(jnp.bfloat16), "seq", 2)
+    first_upper, second_lower = early
+    return [(first_upper, first_lower), (second_upper, second_lower)]
+
+
 def add_parts(own, received):
     return own + sum(part.astype(jnp.float32) for part in received)
 
@@ -683,7 +750,6 @@
     stream = tokens[0].astype(jnp.float32)
     scale_attn = lax.rsqrt(jnp.mean(stream * stream, axis=-1, keepdims=True) + EPSILON)
     normed_attn = stream * scale_attn
-    upstream = out_grad[0].astype(jnp.float32)
 
     stream_near = gather_begin(tokens[0])
     stream_near, gains = both(stream_near, gains)
@@ -741,19 +807,14 @@
     unit_far = low_dot(unit_grad[passed:], gate_up_w) if seq_count == 4 else None
     unit_far, unit_grad, ff_passing = both(unit_far, unit_grad, ff_passing)
     unit_passing = scatter_begin(unit_far)
-    unit_near = low_dot(unit_grad[away:passed], gate_up_w)
-    unit_near, unit_grad, unit_passing = both(unit_near, unit_grad, unit_passing)
-    unit_sums = scatter_add(unit_near, unit_passing)
-    unit_sums, unit_grad = both(unit_sums, unit_grad)
-    unit_parts = scatter_end(unit_sums)
+    unit_terms = low_dot(unit_grad[:passed], gate_up_w)
+    unit_early = scatter_early(unit_terms[away:])
+    unit_terms, unit_grad, unit_passing = both(unit_terms, unit_grad, unit_passing)
+    unit_parts = scatter_late(unit_terms[away:], unit_passing, unit_early)
     gate_up_grad = rows_dot(ffn_rows, unit_grad).astype(jnp.bfloat16)
-    ffn_in_own = cols_dot(unit_grad[:away], gate_up_w)
-    ffn_in_own, gate_up_grad, unit_parts = both(ffn_in_own, gate_up_grad, unit_parts)
+    gate_up_grad, unit_parts = both(gate_up_grad, unit_parts)
     gate_up_owned = scatter_grads(gate_up_grad)
-    ffn_in_grad = add_parts(ffn_in_own, unit_parts)
-
-    resid_grad = upstream + norm_back(ffn_in_grad * ffn_gain, normed_ffn, scale_ffn)
-    attn_grad = resid_grad.astype(jnp.bfloat16)
+    resid_grad, attn_grad = norm_backward(unit_terms, unit_parts, out_grad[0], resid, ffn_gain)
     attn_grad, hidden, down_owned = both(attn_grad, hidden, down_owned)
     attn_grad_rows = gather_rows(attn_grad)
     ff_near = low_dot(hidden[away:passed], down_w)

time: 562 us -> 558 us (level)
  other arithmetic: 33.5 us -> 26.1 us
  Pallas kernels: 119 us -> 126 us
  matrix products: 114 us -> 108 us
    pallas_call x0 -> x1, Pallas kernels: none -> 6.29 us  [norm_backward(): pl.pallas_call(functools.partial(norm_backward_kernel, lengths), grid=(st...]
    dot_general x10 -> x9, matrix products: 57.7 us -> 52.2 us  [cols_dot(): lax.dot_general(left, right, (((1,), (1,)), ((), ())), preferred_element_...]
    unnamed x97 -> x115, local copies, waits for them, and re-layouts: 20.3 us -> 23.2 us
    ppermute x50 -> x52, waiting for transfers between devices: 137 us -> 135 us  [swap(): lax.ppermute(piece, axis, [(i, i ^ step) for i in range(lax.axis_size(axi...]
    ppermute x50 -> x52, starting transfers between devices: 57.6 us -> 58.4 us  [swap(): lax.ppermute(piece, axis, [(i, i ^ step) for i in range(lax.axis_size(axi...]
  transfers between devices with their start and end apart: 57 -> 59, of which waited for: 30 -> 30; matrix products, arithmetic and copies ran while one was open for 32% -> 30% of each run, Pallas kernels for 20% -> 22%
where the time goes in v7:
time: 558 us; the launch traced here: 551 us
  waiting for transfers between devices  151 us (27%)
  Pallas kernels  126 us (23%)
  matrix products  108 us (19%)
  starting transfers between devices  59.2 us (11%)
  local copies, waits for them, and re-layouts  39.5 us (7%)
  blocking collectives  26.7 us (5%)
  other arithmetic  26.1 us (5%)
  between operations  15.8 us (3%)
    ppermute x52, waiting for transfers between devices, swap(): lax.ppermute(piece, axis, [(i, i ^ step) for i in range(lax.axis_size(axi...  135 us
    ppermute x52, starting transfers between devices, swap(): lax.ppermute(piece, axis, [(i, i ^ step) for i in range(lax.axis_size(axi...  58.4 us
    dot_general x9, matrix products, cols_dot(): lax.dot_general(left, right, (((1,), (1,)), ((), ())), preferred_element_...  52.2 us
    dot_general x3, matrix products, rows_dot(): lax.dot_general(left, right, (((0,), (0,)), ((), ())), preferred_element_...  34.2 us
    pallas_call x1, Pallas kernels, attention_backward(): pl.pallas_call(functools.partial(backward_kernel, block, token_rows), gri...  28.8 us
    pallas_call x4, Pallas kernels, place_columns(): pl.pallas_call(functools.partial(place_kernel, moves, lengths, block, wid...  23.4 us
    unnamed x115, local copies, waits for them, and re-layouts  23.2 us
    pallas_call x1, Pallas kernels, attention_forward(): pl.pallas_call(functools.partial(forward_kernel, block, token_rows), grid...  22.1 us
  transfers between devices with their start and end apart: 59, of which 30 were waited for; matrix products, arithmetic and copies ran while one was open for 30% of the time, Pallas kernels for 22%

profile of v7, /device:TPU:0, one launch (start us, length us, event | category | flops | bytes accessed | tf_op | source)
XLA Modules:
  0.0 551.3 jit_solution(16492591028521571850)
XLA Ops:
  14.3 12.0 %all_gather.15 = bf16[2,2048]{1,0:T(2,128)(2,1)S(1)} all-gather(bf16[2,256]{1,0:T(2,128)(2,1)S(1)} %pad_maximum_fusion.1), channel_id=1, replica_groups=mesh['fsdp'=8,'seq'=4] {'fsdp'}, dimensions={1}, use_global_device_ids=true | all-gather | bytes 9216 | tf_op jit(solution)/shard_map/all_gather | solution.py:737
  26.3 9.8 %collective-permute-done.1 = bf16[256,2048]{1,0:T(8,128)(2,1)S(1)} collective-permute-done((bf16[256,2048]{1,0:T(8,128)(2,1)}, bf16[256,2048]{1,0:T(8,128)(2,1)S(1)}, u32[]{:S(2)}, u32[]{:S(2)}) %collective-permute-start.1) | collective-permute-done | bytes 1048608 | tf_op jit(solution)/shard_map/ppermute | solution.py:358
  64.3 17.8 %collective-permute-done.5 = bf16[256,2048]{1,0:T(8,128)(2,1)} collective-permute-done((bf16[256,2048]{1,0:T(8,128)(2,1)}, bf16[256,2048]{1,0:T(8,128)(2,1)}, u32[]{:S(2)}, u32[]{:S(2)}) %collective-permute-start.5) | collective-permute-done | bytes 1048608 | tf_op jit(solution)/shard_map/ppermute | solution.py:358
  99.4 11.4 %fusion.11.qkv_ref = bf16[1024,1536]{1,0:T(8,128)(2,1)} fusion(bf16[1024,2048]{1,0:T(8,128)(2,1)} %fusion.2, bf16[2048,2048]{1,0:T(8,128)(2,1)} %all-gather.4.cloned.1.call-done), kind=kOutput, calls=%fused_computation.16 | convolution fusion | flops 6444023808 | bytes 13631488 | tf_op jit(solution)/shard_map/dot_general | solution.py:768
  114.8 22.1 %attention_forward.1 = (bf16[1024,512]{1,0:T(8,128)(2,1)}, bf16[8,1024,1024]{2,1,0:T(8,128)(2,1)}, f32[8,1,1024]{2,1,0:T(1,128)}) custom-call(s32[1]{0:T(128)} %bitcast.place_ref, bf16[1024,1536]{1,0:T(8,128)(2,1)} %fusion.11.qkv_ref, s32[1,1024]{1,0:T(1,128)} %row_ref.1, s32[1024,128]{1,0:T(8,128)} %broadcast_in_dim.11.col_ref, f32[4,2,2048]{2,1,0:T(2,128)} %reshape.85.bias_ref), custom_call_target="tpu_custom_call" | custom-call | tf_op jit(solution)/shard_map/attention_forward/pallas_call | solution.py:212
  144.0 7.4 %collective-permute-done.8 = bf16[128,2048]{1,0:T(8,128)(2,1)S(1)} collective-permute-done((bf16[128,2048]{1,0:T(8,128)(2,1)S(1)}, bf16[128,2048]{1,0:T(8,128)(2,1)S(1)}, u32[]{:S(2)}, u32[]{:S(2)}) %collective-permute-start.8) | collective-permute-done | bytes 524320 | tf_op jit(solution)/shard_map/ppermute | solution.py:358
  158.6 15.6 %collective-permute-done.9 = bf16[256,2048]{1,0:T(8,128)(2,1)S(1)} collective-permute-done((bf16[256,2048]{1,0:T(8,128)(2,1)S(1)}, bf16[256,2048]{1,0:T(8,128)(2,1)S(1)}, u32[]{:S(2)}, u32[]{:S(2)}) %collective-permute-start.9) | collective-permute-done | bytes 1048608 | tf_op jit(solution)/shard_map/ppermute | solution.py:358
  179.2 19.4 %collective-permute-done.13 = bf16[256,2048]{1,0:T(8,128)(2,1)S(1)} collective-permute-done((bf16[256,2048]{1,0:T(8,128)(2,1)S(1)}, bf16[256,2048]{1,0:T(8,128)(2,1)S(1)}, u32[]{:S(2)}, u32[]{:S(2)}) %collective-permute-start.13) | collective-permute-done | bytes 1048608 | tf_op jit(solution)/shard_map/ppermute | solution.py:358
  212.4 18.4 %feed_forward.1 = (bf16[1024,1280]{1,0:T(8,128)(2,1)}, bf16[1024,1280]{1,0:T(8,128)(2,1)}, bf16[1024,1280]{1,0:T(8,128)(2,1)}) custom-call(bf16[1024,2048]{1,0:T(8,128)(2,1)} %constant_dynamic-update-slice_fusion.10.x_ref, bf16[2048,2560]{1,0:T(8,128)(2,1)} %all-gather.8.cloned.1.call-done.w_ref), custom_call_target="tpu_custom_call" | custom-call | tf_op jit(solution)/shard_map/feed_forward/pallas_call | solution.py:478
  230.8 9.9 %convolution_convert_fusion.2 = bf16[2048,1280]{1,0:T(8,128)(2,1)} fusion(bf16[1024,2048]{1,0:T(8,128)(2,1)} %constant_dynamic-update-slice_fusion.5.d_ref, bf16[1024,1280]{1,0:T(8,128)(2,1)} %get-tuple-element.160), kind=kOutput, calls=%fused_computation.7 | convolution fusion | flops 5371330560 | bytes 12058624 | tf_op jit(solution)/shard_map/dot_general | solution.py:25
  240.8 11.1 %all-gather.6.cloned.1.call-done.w_ref = bf16[2048,1280]{1,0:T(8,128)(2,1)} async-done(((bf16[256,1280]{1,0:T(8,128)(2,1)}), bf16[2048,1280]{1,0:T(8,128)(2,1)}) %all-gather.6.cloned.1.call-update) | async-done | bytes 5242896 | tf_op jit(solution)/shard_map/all_gather | solution.py:721
  259.2 11.9 %feed_forward_back.1 = bf16[1024,2560]{1,0:T(8,128)(2,1)} custom-call(bf16[1024,2048]{1,0:T(8,128)(2,1)} %constant_dynamic-update-slice_fusion.5.d_ref, bf16[2048,1280]{1,0:T(8,128)(2,1)} %all-gather.6.cloned.1.call-done.w_ref, bf16[1024,1280]{1,0:T(8,128)(2,1)} %get-tuple-element.128.gelu_ref, bf16[1024,1280]{1,0:T(8,128)(2,1)} %get-tuple-element.129.slope_ref), custom_call_target="tpu_custom_call" | custom-call | tf_op jit(solution)/shard_map/feed_forward_back/pallas_call | solution.py:511
  271.2 7.5 %convolution_convert_fusion.5 = bf16[256,2048]{1,0:T(8,128)(2,1)S(1)} fusion(bf16[2048,2560]{1,0:T(8,128)(2,1)} %all-gather.8.cloned.1.call-done.w_ref, bf16[1024,2560]{1,0:T(8,128)(2,1)} %feed_forward_back.1), kind=kOutput, calls=%fused_computation.25 | convolution fusion | flops 2684878848 | bytes 12845056 | tf_op jit(solution)/shard_map/dot_general | solution.py:31
  280.3 11.1 %fusion.14.own_ref = bf16[768,2048]{1,0:T(8,128)(2,1)S(1)} fusion(bf16[2048,2560]{1,0:T(8,128)(2,1)} %all-gather.8.cloned.1.call-done.w_ref, bf16[1024,2560]{1,0:T(8,128)(2,1)S(1)} %copy-done.10), kind=kOutput, calls=%fused_computation.18 | convolution fusion | flops 8054636544 | bytes 17563648 | tf_op jit(solution)/shard_map/dot_general | solution.py:31
  298.0 15.6 %convolution_convert_fusion = bf16[2048,2560]{1,0:T(8,128)(2,1)} fusion(bf16[1024,2048]{1,0:T(8,128)(2,1)} %constant_dynamic-update-slice_fusion.10.x_ref, bf16[1024,2560]{1,0:T(8,128)(2,1)S(1)} %copy-done.10), kind=kOutput, calls=%fused_computation | convolution fusion | flops 10742661120 | bytes 19922944 | tf_op jit(solution)/shard_map/dot_general | solution.py:25
  319.1 6.3 %norm_backward.1 = (f32[256,2048]{1,0:T(8,128)}, bf16[256,2048]{1,0:T(8,128)(2,1)}) custom-call(bf16[768,2048]{1,0:T(8,128)(2,1)} %copy-done.8, bf16[256,2048]{1,0:T(8,128)(2,1)} %bitcast.48, f32[256,2048]{1,0:T(8,128)} %copy-done.4, f32[1,2048]{1,0:T(1,128)} %copy-done.32, bf16[128,2048]{1,0:T(8,128)(2,1)} %copy-done.26, bf16[128,2048]{1,0:T(8,128)(2,1)} %copy-done.28, ...), custom_call_target="tpu_custom_call" | custom-call | tf_op jit(solution)/shard_map/norm_backward/pallas_call | solution.py:70
  333.5 14.7 %collective-permute-done.25 = bf16[256,2048]{1,0:T(8,128)(2,1)S(1)} collective-permute-done((bf16[256,2048]{1,0:T(8,128)(2,1)}, bf16[256,2048]{1,0:T(8,128)(2,1)S(1)}, u32[]{:S(2)}, u32[]{:S(2)}) %collective-permute-start.25) | collective-permute-done | bytes 1048608 | tf_op jit(solution)/shard_map/ppermute | solution.py:358
  351.2 8.7 %collective-permute-done.26 = bf16[128,2048]{1,0:T(8,128)(2,1)S(1)} collective-permute-done((bf16[128,2048]{1,0:T(8,128)(2,1)S(1)}, bf16[128,2048]{1,0:T(8,128)(2,1)S(1)}, u32[]{:S(2)}, u32[]{:S(2)}) %collective-permute-start.26) | collective-permute-done | bytes 524320 | tf_op jit(solution)/shard_map/ppermute | solution.py:358
  371.2 28.8 %attention_backward.1 = (bf16[1024,1536]{1,0:T(8,128)(2,1)}, f32[4,2,2048]{2,1,0:T(2,128)}) custom-call(s32[1]{0:T(128)} %bitcast.place_ref, bf16[1024,1536]{1,0:T(8,128)(2,1)} %fusion.11.qkv_ref, bf16[1024,512]{1,0:T(8,128)(2,1)} %fusion.34.d_ref, bf16[8,1024,1024]{2,1,0:T(8,128)(2,1)} %get-tuple-element.149.e_ref, f32[8,1,1024]{2,1,0:T(1,128)} %get-tuple-element.150.inv_ref), custom_call_target="tpu_custom_call" | custom-call | tf_op jit(solution)/shard_map/attention_backward/pallas_call | solution.py:329
  400.1 8.6 %fusion.17 = bf16[768,2048]{1,0:T(8,128)(2,1)S(1)} fusion(bf16[2048,2048]{1,0:T(8,128)(2,1)} %all-gather.4.cloned.1.call-done, bf16[1024,1536]{1,0:T(8,128)(2,1)} %get-tuple-element.167), kind=kOutput, calls=%fused_computation.19 | convolution fusion | flops 4833411072 | bytes 11796480 | tf_op jit(solution)/shard_map/dot_general | solution.py:31
  414.7 8.7 %convolution_convert_fusion.1 = bf16[2048,1536]{1,0:T(8,128)(2,1)} fusion(bf16[1024,2048]{1,0:T(8,128)(2,1)S(1)} %copy-done.11, bf16[1024,1536]{1,0:T(8,128)(2,1)S(1)} %copy-done.40), kind=kOutput, calls=%fused_computation.6 | convolution fusion | flops 6445596672 | bytes 13631488 | tf_op jit(solution)/shard_map/dot_general | solution.py:25
  468.1 14.7 %all_gather.19 = f32[8,9,128]{2,1,0:T(8,128)S(1)} all-gather(f32[1,9,128]{2,1,0:T(8,128)S(1)} %bitcast.56), channel_id=1, replica_groups=mesh['fsdp'=8,'seq'=4] {'fsdp'}, dimensions={0}, use_global_device_ids=true | all-gather | bytes 41472 | tf_op jit(solution)/shard_map/all_gather | solution.py:875
  499.5 8.6 %place_columns.5 = (f32[256,5120]{1,0:T(8,128)}, f32[256,5120]{1,0:T(8,128)}, f32[256,128]{1,0:T(8,128)}) custom-call(s32[1]{0:T(128)} %bitcast.place_ref, bf16[256,2560]{1,0:T(8,128)(2,1)} %reduce-scatter.7.cloned.1.call-done.refs_0_, bf16[256,2560]{1,0:T(8,128)(2,1)} %collective-permute-done.35.refs_1_, bf16[256,2560]{1,0:T(8,128)(2,1)} %collective-permute-done.36.refs_2_, ...), custom_call_target="tpu_custom_call" | custom-call | bytes 21233664 | tf_op jit(solution)/shard_map/place_columns/pallas_call | solution.py:577
  530.5 6.6 %place_columns.6 = (f32[256,2048]{1,0:T(8,128)}, f32[256,2048]{1,0:T(8,128)}, f32[256,2048]{1,0:T(8,128)}, f32[256,128]{1,0:T(8,128)}) custom-call(s32[1]{0:T(128)} %bitcast.place_ref, bf16[256,1536]{1,0:T(8,128)(2,1)} %reduce-scatter.9.cloned.1.call-done.refs_0_, bf16[256,1536]{1,0:T(8,128)(2,1)} %copy-done.16, bf16[256,1536]{1,0:T(8,128)(2,1)} %copy-done.15, ...), custom_call_target="tpu_custom_call" | custom-call | bytes 12845056 | tf_op jit(solution)/shard_map/place_columns/pallas_call | solution.py:577
  (311 shorter events, 228.8 us)
Async XLA Ops:
  7.2 92.2 %all-gather.4.cloned.1.call-start = ((), (), s32[]{:S(2)}) async-start(), calls=%async_computation.4 | async-start | bytes 9437184 | tf_op jit(solution)/shard_map/all_gather | solution.py:721
  9.7 202.7 %all-gather.8.cloned.1.call-start = ((), (), s32[]{:S(2)}) async-start(), calls=%async_computation.6 | async-start | bytes 11796480 | tf_op jit(solution)/shard_map/all_gather | solution.py:721
  9.7 26.4 %collective-permute-start.1 = (bf16[256,2048]{1,0:T(8,128)(2,1)}, bf16[256,2048]{1,0:T(8,128)(2,1)S(1)}, u32[]{:S(2)}, u32[]{:S(2)}) collective-permute-start(bf16[256,2048]{1,0:T(8,128)(2,1)} %bitcast.42), channel_id=1, source_target_pairs={{0,2},{1,3},{2,0},{3,1},{4,6},{5,7},{6,4},{7,5},{8,10},{9,11},{10,... | collective-permute-start | bytes 3145736 | tf_op jit(solution)/shard_map/ppermute | solution.py:358
  12.7 24.9 %collective-permute-start = (bf16[256,2048]{1,0:T(8,128)(2,1)}, bf16[256,2048]{1,0:T(8,128)(2,1)}, u32[]{:S(2)}, u32[]{:S(2)}) collective-permute-start(bf16[256,2048]{1,0:T(8,128)(2,1)} %bitcast.43), channel_id=1, source_target_pairs={{0,1},{1,0},{2,3},{3,2},{4,5},{5,4},{6,7},{7,6},{8,9},{9,8},{10,11... | collective-permute-start | bytes 3145736 | tf_op jit(solution)/shard_map/ppermute | solution.py:358
  58.8 193.1 %all-gather.6.cloned.1.call-start = ((), (), s32[]{:S(2)}) async-start(), calls=%async_computation.5 | async-start | bytes 5898240 | tf_op jit(solution)/shard_map/all_gather | solution.py:721
  58.8 23.2 %collective-permute-start.5 = (bf16[256,2048]{1,0:T(8,128)(2,1)}, bf16[256,2048]{1,0:T(8,128)(2,1)}, u32[]{:S(2)}, u32[]{:S(2)}) collective-permute-start(bf16[256,2048]{1,0:T(8,128)(2,1)} %bitcast.46), channel_id=1, source_target_pairs={{0,2},{1,3},{2,0},{3,1},{4,6},{5,7},{6,4},{7,5},{8,10},{9,11},{10,... | collective-permute-start | bytes 3145736 | tf_op jit(solution)/shard_map/ppermute | solution.py:358
  60.4 23.8 %collective-permute-start.4 = (bf16[256,2048]{1,0:T(8,128)(2,1)}, bf16[256,2048]{1,0:T(8,128)(2,1)}, u32[]{:S(2)}, u32[]{:S(2)}) collective-permute-start(bf16[256,2048]{1,0:T(8,128)(2,1)} %bitcast.47), channel_id=1, source_target_pairs={{0,1},{1,0},{2,3},{3,2},{4,5},{5,4},{6,7},{7,6},{8,9},{9,8},{10,11... | collective-permute-start | bytes 3145736 | tf_op jit(solution)/shard_map/ppermute | solution.py:358
  110.8 214.5 %reduce-scatter.5.cloned.1.call-start = ((), (), s32[]{:S(2)}) async-start(), calls=%async_computation.7 | async-start | bytes 5898240 | tf_op jit(solution)/shard_map/reduce_scatter | solution.py:783
  178.0 24.2 %collective-permute-start.12 = (bf16[256,2048]{1,0:T(8,128)(2,1)S(1)}, bf16[256,2048]{1,0:T(8,128)(2,1)S(1)}, u32[]{:S(2)}, u32[]{:S(2)}) collective-permute-start(bf16[256,2048]{1,0:T(8,128)(2,1)S(1)} %get-tuple-element.222), channel_id=1, source_target_pairs={{0,1},{1,0},{2,3},{3,2},{4,5},{5,4},{6,7},{7,6},{8,9},{9,8},{10,11... | collective-permute-start | bytes 3145736 | tf_op jit(solution)/shard_map/ppermute | solution.py:358
  240.8 187.1 %reduce-scatter.7.cloned.1.call-start = ((), (), s32[]{:S(2)}) async-start(), calls=%async_computation.8 | async-start | bytes 11796480 | tf_op jit(solution)/shard_map/reduce_scatter | solution.py:783
  319.1 179.0 %reduce-scatter.9.cloned.1.call-start = ((), (), s32[]{:S(2)}) async-start(), calls=%async_computation.9 | async-start | bytes 7077888 | tf_op jit(solution)/shard_map/reduce_scatter | solution.py:783
  325.5 24.3 %collective-permute-start.24 = (bf16[256,2048]{1,0:T(8,128)(2,1)}, bf16[256,2048]{1,0:T(8,128)(2,1)S(1)}, u32[]{:S(2)}, u32[]{:S(2)}) collective-permute-start(bf16[256,2048]{1,0:T(8,128)(2,1)} %get-tuple-element.143), channel_id=1, source_target_pairs={{0,1},{1,0},{2,3},{3,2},{4,5},{5,4},{6,7},{7,6},{8,9},{9,8},{10,11... | collective-permute-start | bytes 3145736 | tf_op jit(solution)/shard_map/ppermute | solution.py:358
  360.4 48.4 %collective-permute-start.32 = (bf16[256,1280]{1,0:T(8,128)(2,1)S(1)}, bf16[256,1280]{1,0:T(8,128)(2,1)S(1)}, u32[]{:S(2)}, u32[]{:S(2)}) collective-permute-start(bf16[256,1280]{1,0:T(8,128)(2,1)S(1)} %copy-done.20), channel_id=1, source_target_pairs={{0,3},{1,2},{2,1},{3,0},{4,7},{5,6},{6,5},{7,4},{8,11},{9,10},{10,... | collective-permute-start | bytes 1966088 | tf_op jit(solution)/shard_map/ppermute | solution.py:358
  362.3 46.5 %collective-permute-start.31 = (bf16[256,1280]{1,0:T(8,128)(2,1)S(1)}, bf16[256,1280]{1,0:T(8,128)(2,1)S(1)}, u32[]{:S(2)}, u32[]{:S(2)}) collective-permute-start(bf16[256,1280]{1,0:T(8,128)(2,1)S(1)} %copy-done.20), channel_id=1, source_target_pairs={{0,2},{1,3},{2,0},{3,1},{4,6},{5,7},{6,4},{7,5},{8,10},{9,11},{10,... | collective-permute-start | bytes 1966088 | tf_op jit(solution)/shard_map/ppermute | solution.py:358
  363.0 45.8 %collective-permute-start.30 = (bf16[256,1280]{1,0:T(8,128)(2,1)S(1)}, bf16[256,1280]{1,0:T(8,128)(2,1)S(1)}, u32[]{:S(2)}, u32[]{:S(2)}) collective-permute-start(bf16[256,1280]{1,0:T(8,128)(2,1)S(1)} %copy-done.20), channel_id=1, source_target_pairs={{0,1},{1,0},{2,3},{3,2},{4,5},{5,4},{6,7},{7,6},{8,9},{9,8},{10,11... | collective-permute-start | bytes 1966088 | tf_op jit(solution)/shard_map/ppermute | solution.py:358
  363.9 47.5 %collective-permute-start.28 = (bf16[256,2048]{1,0:T(8,128)(2,1)S(1)}, bf16[256,2048]{1,0:T(8,128)(2,1)S(1)}, u32[]{:S(2)}, u32[]{:S(2)}) collective-permute-start(bf16[256,2048]{1,0:T(8,128)(2,1)S(1)} %get-tuple-element.152), channel_id=1, source_target_pairs={{0,1},{1,0},{2,3},{3,2},{4,5},{5,4},{6,7},{7,6},{8,9},{9,8},{10,11... | collective-permute-start | bytes 3145736 | tf_op jit(solution)/shard_map/ppermute | solution.py:358
  365.0 46.5 %collective-permute-start.29 = (bf16[256,2048]{1,0:T(8,128)(2,1)S(1)}, bf16[256,2048]{1,0:T(8,128)(2,1)S(1)}, u32[]{:S(2)}, u32[]{:S(2)}) collective-permute-start(bf16[256,2048]{1,0:T(8,128)(2,1)S(1)} %get-tuple-element.153), channel_id=1, source_target_pairs={{0,2},{1,3},{2,0},{3,1},{4,6},{5,7},{6,4},{7,5},{8,10},{9,11},{10,... | collective-permute-start | bytes 3145736 | tf_op jit(solution)/shard_map/ppermute | solution.py:358
  427.9 96.5 %reduce-scatter.11.cloned.1.call-start = ((), (), s32[]{:S(2)}) async-start(), calls=%async_computation.10 | async-start | bytes 1310720 | tf_op jit(solution)/shard_map/reduce_scatter | solution.py:783
  429.4 34.2 %collective-permute-start.36 = (bf16[256,2560]{1,0:T(8,128)(2,1)}, bf16[256,2560]{1,0:T(8,128)(2,1)}, u32[]{:S(2)}, u32[]{:S(2)}) collective-permute-start(bf16[256,2560]{1,0:T(8,128)(2,1)} %reduce-scatter.7.cloned.1.call-done.refs_0_), channel_id=1, source_target_pairs={{0,2},{1,3},{2,0},{3,1},{4,6},{5,7},{6,4},{7,5},{8,10},{9,11},{10,... | collective-permute-start | bytes 3932168 | tf_op jit(solution)/shard_map/ppermute | solution.py:358
  429.7 33.8 %collective-permute-start.35 = (bf16[256,2560]{1,0:T(8,128)(2,1)}, bf16[256,2560]{1,0:T(8,128)(2,1)}, u32[]{:S(2)}, u32[]{:S(2)}) collective-permute-start(bf16[256,2560]{1,0:T(8,128)(2,1)} %reduce-scatter.7.cloned.1.call-done.refs_0_), channel_id=1, source_target_pairs={{0,1},{1,0},{2,3},{3,2},{4,5},{5,4},{6,7},{7,6},{8,9},{9,8},{10,11... | collective-permute-start | bytes 3932168 | tf_op jit(solution)/shard_map/ppermute | solution.py:358
  435.1 48.8 %collective-permute-start.39 = (bf16[256,2048]{1,0:T(8,128)(2,1)}, bf16[256,2048]{1,0:T(8,128)(2,1)}, u32[]{:S(2)}, u32[]{:S(2)}) collective-permute-start(bf16[256,2048]{1,0:T(8,128)(2,1)} %get-tuple-element.226), channel_id=1, source_target_pairs={{0,2},{1,3},{2,0},{3,1},{4,6},{5,7},{6,4},{7,5},{8,10},{9,11},{10,... | collective-permute-start | bytes 3145736 | tf_op jit(solution)/shard_map/ppermute | solution.py:358
  435.2 49.1 %collective-permute-start.38 = (bf16[256,2048]{1,0:T(8,128)(2,1)}, bf16[256,2048]{1,0:T(8,128)(2,1)}, u32[]{:S(2)}, u32[]{:S(2)}) collective-permute-start(bf16[256,2048]{1,0:T(8,128)(2,1)} %get-tuple-element.227), channel_id=1, source_target_pairs={{0,1},{1,0},{2,3},{3,2},{4,5},{5,4},{6,7},{7,6},{8,9},{9,8},{10,11... | collective-permute-start | bytes 3145736 | tf_op jit(solution)/shard_map/ppermute | solution.py:358
  465.8 31.4 %collective-permute-start.43 = (bf16[128,2560]{1,0:T(8,128)(2,1)S(1)}, bf16[128,2560]{1,0:T(8,128)(2,1)S(1)}, u32[]{:S(2)}, u32[]{:S(2)}) collective-permute-start(bf16[128,2560]{1,0:T(8,128)(2,1)S(1)} %slice.199), channel_id=1, source_target_pairs={{0,1},{1,0},{2,3},{3,2},{4,5},{5,4},{6,7},{7,6},{8,9},{9,8},{10,11... | collective-permute-start | bytes 1966088 | tf_op jit(solution)/shard_map/ppermute | solution.py:358
  466.2 31.1 %collective-permute-start.44 = (bf16[128,2560]{1,0:T(8,128)(2,1)S(1)}, bf16[128,2560]{1,0:T(8,128)(2,1)}, u32[]{:S(2)}, u32[]{:S(2)}) collective-permute-start(bf16[128,2560]{1,0:T(8,128)(2,1)S(1)} %slice.200), channel_id=1, source_target_pairs={{0,2},{1,3},{2,0},{3,1},{4,6},{5,7},{6,4},{7,5},{8,10},{9,11},{10,... | collective-permute-start | bytes 1966088 | tf_op jit(solution)/shard_map/ppermute | solution.py:358
  (84 other events, 1100.6 us)
Sparse Core Ops, SparseCore 0:
  10.2 84.7 all-gather.3
  97.2 97.9 all-gather.7
  197.4 54.4 all-gather.5
  254.6 58.6 reduce-scatter.4
  318.4 107.2 reduce-scatter.6
  428.0 68.4 reduce-scatter.8
  498.8 25.4 reduce-scatter.10

commit v8 on v7

--- a/solution.py
+++ b/solution.py
@@ -897,13 +897,13 @@
         [column_count] * 3,
         (w_query, w_key, w_value),
     )
-    output_near, attn_outs = both(output_near, attn_outs)
     query_out, key_out, value_out, attn_sums = attn_outs
+    gain_attn_grad = jnp.sum(attn_sums, axis=1) / gain_attn.astype(jnp.float32)
+    gain_ffn_grad = jnp.sum(ffn_sums, axis=1) / gain_ffn.astype(jnp.float32)
+    output_near, gain_attn_grad, gain_ffn_grad = both(output_near, gain_attn_grad, gain_ffn_grad)
     (output_out,) = place_columns(
         gather_end(output_owned, output_near), place, [(0, 0, 0, column_count)], [column_count]
     )
-    gain_attn_grad = jnp.sum(attn_sums, axis=1) / gain_attn.astype(jnp.float32)
-    gain_ffn_grad = jnp.sum(ffn_sums, axis=1) / gain_ffn.astype(jnp.float32)
     stat_totals = summed[rel_table.size : rel_table.size + 4]
     rms_stats = jnp.sqrt(stat_totals[0:3] / (stat_totals[3] * model_width))
     table_share = rel_table.shape[0] // fsdp_count

time: 558 us -> 557 us (level)
  transfers between devices with their start and end apart: 59 -> 59, of which waited for: 30 -> 30; matrix products, arithmetic and copies ran while one was open for 30% -> 31% of each run, Pallas kernels for 22% -> 22%
where the time goes in v8:
time: 557 us; the launch traced here: 550 us
  waiting for transfers between devices  150 us (27%)
  Pallas kernels  125 us (22%)
  matrix products  108 us (19%)
  starting transfers between devices  59.3 us (11%)
  local copies, waits for them, and re-layouts  39.6 us (7%)
  blocking collectives  26.7 us (5%)
  other arithmetic  25.6 us (5%)
  between operations  15.8 us (3%)
    ppermute x52, waiting for transfers between devices, swap(): lax.ppermute(piece, axis, [(i, i ^ step) for i in range(lax.axis_size(axi...  135 us
    ppermute x52, starting transfers between devices, swap(): lax.ppermute(piece, axis, [(i, i ^ step) for i in range(lax.axis_size(axi...  58.5 us
    dot_general x9, matrix products, cols_dot(): lax.dot_general(left, right, (((1,), (1,)), ((), ())), preferred_element_...  52.2 us
    dot_general x3, matrix products, rows_dot(): lax.dot_general(left, right, (((0,), (0,)), ((), ())), preferred_element_...  34.3 us
    pallas_call x1, Pallas kernels, attention_backward(): pl.pallas_call(functools.partial(backward_kernel, block, token_rows), gri...  28.8 us
    pallas_call x4, Pallas kernels, place_columns(): pl.pallas_call(functools.partial(place_kernel, moves, lengths, block, wid...  23.4 us
    unnamed x115, local copies, waits for them, and re-layouts  23.2 us
    pallas_call x1, Pallas kernels, attention_forward(): pl.pallas_call(functools.partial(forward_kernel, block, token_rows), grid...  22.1 us
  transfers between devices with their start and end apart: 59, of which 30 were waited for; matrix products, arithmetic and copies ran while one was open for 31% of the time, Pallas kernels for 22%

profile of v8, /device:TPU:0, one launch (start us, length us, event | category | flops | bytes accessed | tf_op | source)
XLA Modules:
  0.0 549.7 jit_solution(2423179728669631207)
XLA Ops:
  14.3 12.0 %all_gather.15 = bf16[2,2048]{1,0:T(2,128)(2,1)S(1)} all-gather(bf16[2,256]{1,0:T(2,128)(2,1)S(1)} %pad_maximum_fusion.1), channel_id=1, replica_groups=mesh['fsdp'=8,'seq'=4] {'fsdp'}, dimensions={1}, use_global_device_ids=true | all-gather | bytes 9216 | tf_op jit(solution)/shard_map/all_gather | solution.py:737
  26.3 9.8 %collective-permute-done.1 = bf16[256,2048]{1,0:T(8,128)(2,1)S(1)} collective-permute-done((bf16[256,2048]{1,0:T(8,128)(2,1)}, bf16[256,2048]{1,0:T(8,128)(2,1)S(1)}, u32[]{:S(2)}, u32[]{:S(2)}) %collective-permute-start.1) | collective-permute-done | bytes 1048608 | tf_op jit(solution)/shard_map/ppermute | solution.py:358
  64.3 17.8 %collective-permute-done.5 = bf16[256,2048]{1,0:T(8,128)(2,1)} collective-permute-done((bf16[256,2048]{1,0:T(8,128)(2,1)}, bf16[256,2048]{1,0:T(8,128)(2,1)}, u32[]{:S(2)}, u32[]{:S(2)}) %collective-permute-start.5) | collective-permute-done | bytes 1048608 | tf_op jit(solution)/shard_map/ppermute | solution.py:358
  99.4 11.4 %fusion.11.qkv_ref = bf16[1024,1536]{1,0:T(8,128)(2,1)} fusion(bf16[1024,2048]{1,0:T(8,128)(2,1)} %fusion.2, bf16[2048,2048]{1,0:T(8,128)(2,1)} %all-gather.4.cloned.1.call-done), kind=kOutput, calls=%fused_computation.16 | convolution fusion | flops 6444023808 | bytes 13631488 | tf_op jit(solution)/shard_map/dot_general | solution.py:768
  114.8 22.1 %attention_forward.1 = (bf16[1024,512]{1,0:T(8,128)(2,1)}, bf16[8,1024,1024]{2,1,0:T(8,128)(2,1)}, f32[8,1,1024]{2,1,0:T(1,128)}) custom-call(s32[1]{0:T(128)} %bitcast.place_ref, bf16[1024,1536]{1,0:T(8,128)(2,1)} %fusion.11.qkv_ref, s32[1,1024]{1,0:T(1,128)} %row_ref.1, s32[1024,128]{1,0:T(8,128)} %broadcast_in_dim.11.col_ref, f32[4,2,2048]{2,1,0:T(2,128)} %reshape.85.bias_ref), custom_call_target="tpu_custom_call" | custom-call | tf_op jit(solution)/shard_map/attention_forward/pallas_call | solution.py:212
  144.0 7.3 %collective-permute-done.8 = bf16[128,2048]{1,0:T(8,128)(2,1)S(1)} collective-permute-done((bf16[128,2048]{1,0:T(8,128)(2,1)S(1)}, bf16[128,2048]{1,0:T(8,128)(2,1)S(1)}, u32[]{:S(2)}, u32[]{:S(2)}) %collective-permute-start.8) | collective-permute-done | bytes 524320 | tf_op jit(solution)/shard_map/ppermute | solution.py:358
  158.5 15.6 %collective-permute-done.9 = bf16[256,2048]{1,0:T(8,128)(2,1)S(1)} collective-permute-done((bf16[256,2048]{1,0:T(8,128)(2,1)S(1)}, bf16[256,2048]{1,0:T(8,128)(2,1)S(1)}, u32[]{:S(2)}, u32[]{:S(2)}) %collective-permute-start.9) | collective-permute-done | bytes 1048608 | tf_op jit(solution)/shard_map/ppermute | solution.py:358
  179.1 19.3 %collective-permute-done.13 = bf16[256,2048]{1,0:T(8,128)(2,1)S(1)} collective-permute-done((bf16[256,2048]{1,0:T(8,128)(2,1)S(1)}, bf16[256,2048]{1,0:T(8,128)(2,1)S(1)}, u32[]{:S(2)}, u32[]{:S(2)}) %collective-permute-start.13) | collective-permute-done | bytes 1048608 | tf_op jit(solution)/shard_map/ppermute | solution.py:358
  212.5 18.2 %feed_forward.1 = (bf16[1024,1280]{1,0:T(8,128)(2,1)}, bf16[1024,1280]{1,0:T(8,128)(2,1)}, bf16[1024,1280]{1,0:T(8,128)(2,1)}) custom-call(bf16[1024,2048]{1,0:T(8,128)(2,1)} %constant_dynamic-update-slice_fusion.10.x_ref, bf16[2048,2560]{1,0:T(8,128)(2,1)} %all-gather.8.cloned.1.call-done.w_ref), custom_call_target="tpu_custom_call" | custom-call | tf_op jit(solution)/shard_map/feed_forward/pallas_call | solution.py:478
  230.7 9.9 %convolution_convert_fusion.2 = bf16[2048,1280]{1,0:T(8,128)(2,1)} fusion(bf16[1024,2048]{1,0:T(8,128)(2,1)} %constant_dynamic-update-slice_fusion.5.d_ref, bf16[1024,1280]{1,0:T(8,128)(2,1)} %get-tuple-element.158), kind=kOutput, calls=%fused_computation.7 | convolution fusion | flops 5371330560 | bytes 12058624 | tf_op jit(solution)/shard_map/dot_general | solution.py:25
  240.7 11.2 %all-gather.6.cloned.1.call-done.w_ref = bf16[2048,1280]{1,0:T(8,128)(2,1)} async-done(((bf16[256,1280]{1,0:T(8,128)(2,1)}), bf16[2048,1280]{1,0:T(8,128)(2,1)}) %all-gather.6.cloned.1.call-update) | async-done | bytes 5242896 | tf_op jit(solution)/shard_map/all_gather | solution.py:721
  259.2 11.9 %feed_forward_back.1 = bf16[1024,2560]{1,0:T(8,128)(2,1)} custom-call(bf16[1024,2048]{1,0:T(8,128)(2,1)} %constant_dynamic-update-slice_fusion.5.d_ref, bf16[2048,1280]{1,0:T(8,128)(2,1)} %all-gather.6.cloned.1.call-done.w_ref, bf16[1024,1280]{1,0:T(8,128)(2,1)} %get-tuple-element.126.gelu_ref, bf16[1024,1280]{1,0:T(8,128)(2,1)} %get-tuple-element.127.slope_ref), custom_call_target="tpu_custom_call" | custom-call | tf_op jit(solution)/shard_map/feed_forward_back/pallas_call | solution.py:511
  271.2 7.5 %convolution_convert_fusion.5 = bf16[256,2048]{1,0:T(8,128)(2,1)S(1)} fusion(bf16[2048,2560]{1,0:T(8,128)(2,1)} %all-gather.8.cloned.1.call-done.w_ref, bf16[1024,2560]{1,0:T(8,128)(2,1)} %feed_forward_back.1), kind=kOutput, calls=%fused_computation.25 | convolution fusion | flops 2684878848 | bytes 12845056 | tf_op jit(solution)/shard_map/dot_general | solution.py:31
  280.3 11.1 %fusion.14.own_ref = bf16[768,2048]{1,0:T(8,128)(2,1)S(1)} fusion(bf16[2048,2560]{1,0:T(8,128)(2,1)} %all-gather.8.cloned.1.call-done.w_ref, bf16[1024,2560]{1,0:T(8,128)(2,1)S(1)} %copy-done.10), kind=kOutput, calls=%fused_computation.18 | convolution fusion | flops 8054636544 | bytes 17563648 | tf_op jit(solution)/shard_map/dot_general | solution.py:31
  298.0 15.7 %convolution_convert_fusion = bf16[2048,2560]{1,0:T(8,128)(2,1)} fusion(bf16[1024,2048]{1,0:T(8,128)(2,1)} %constant_dynamic-update-slice_fusion.10.x_ref, bf16[1024,2560]{1,0:T(8,128)(2,1)S(1)} %copy-done.10), kind=kOutput, calls=%fused_computation | convolution fusion | flops 10742661120 | bytes 19922944 | tf_op jit(solution)/shard_map/dot_general | solution.py:25
  319.1 6.3 %norm_backward.1 = (f32[256,2048]{1,0:T(8,128)}, bf16[256,2048]{1,0:T(8,128)(2,1)}) custom-call(bf16[768,2048]{1,0:T(8,128)(2,1)} %copy-done.8, bf16[256,2048]{1,0:T(8,128)(2,1)} %bitcast.48, f32[256,2048]{1,0:T(8,128)} %copy-done.4, f32[1,2048]{1,0:T(1,128)} %copy-done.32, bf16[128,2048]{1,0:T(8,128)(2,1)} %copy-done.26, bf16[128,2048]{1,0:T(8,128)(2,1)} %copy-done.28, ...), custom_call_target="tpu_custom_call" | custom-call | tf_op jit(solution)/shard_map/norm_backward/pallas_call | solution.py:70
  333.5 14.7 %collective-permute-done.25 = bf16[256,2048]{1,0:T(8,128)(2,1)S(1)} collective-permute-done((bf16[256,2048]{1,0:T(8,128)(2,1)}, bf16[256,2048]{1,0:T(8,128)(2,1)S(1)}, u32[]{:S(2)}, u32[]{:S(2)}) %collective-permute-start.25) | collective-permute-done | bytes 1048608 | tf_op jit(solution)/shard_map/ppermute | solution.py:358
  351.2 8.7 %collective-permute-done.26 = bf16[128,2048]{1,0:T(8,128)(2,1)S(1)} collective-permute-done((bf16[128,2048]{1,0:T(8,128)(2,1)S(1)}, bf16[128,2048]{1,0:T(8,128)(2,1)S(1)}, u32[]{:S(2)}, u32[]{:S(2)}) %collective-permute-start.26) | collective-permute-done | bytes 524320 | tf_op jit(solution)/shard_map/ppermute | solution.py:358
  371.2 28.8 %attention_backward.1 = (bf16[1024,1536]{1,0:T(8,128)(2,1)}, f32[4,2,2048]{2,1,0:T(2,128)}) custom-call(s32[1]{0:T(128)} %bitcast.place_ref, bf16[1024,1536]{1,0:T(8,128)(2,1)} %fusion.11.qkv_ref, bf16[1024,512]{1,0:T(8,128)(2,1)} %fusion.34.d_ref, bf16[8,1024,1024]{2,1,0:T(8,128)(2,1)} %get-tuple-element.147.e_ref, f32[8,1,1024]{2,1,0:T(1,128)} %get-tuple-element.148.inv_ref), custom_call_target="tpu_custom_call" | custom-call | tf_op jit(solution)/shard_map/attention_backward/pallas_call | solution.py:329
  400.1 8.6 %fusion.17 = bf16[768,2048]{1,0:T(8,128)(2,1)S(1)} fusion(bf16[2048,2048]{1,0:T(8,128)(2,1)} %all-gather.4.cloned.1.call-done, bf16[1024,1536]{1,0:T(8,128)(2,1)} %get-tuple-element.165), kind=kOutput, calls=%fused_computation.19 | convolution fusion | flops 4833411072 | bytes 11796480 | tf_op jit(solution)/shard_map/dot_general | solution.py:31
  414.7 8.7 %convolution_convert_fusion.1 = bf16[2048,1536]{1,0:T(8,128)(2,1)} fusion(bf16[1024,2048]{1,0:T(8,128)(2,1)S(1)} %copy-done.11, bf16[1024,1536]{1,0:T(8,128)(2,1)S(1)} %copy-done.40), kind=kOutput, calls=%fused_computation.6 | convolution fusion | flops 6445596672 | bytes 13631488 | tf_op jit(solution)/shard_map/dot_general | solution.py:25
  468.1 14.7 %all_gather.19 = f32[8,9,128]{2,1,0:T(8,128)S(1)} all-gather(f32[1,9,128]{2,1,0:T(8,128)S(1)} %bitcast.56), channel_id=1, replica_groups=mesh['fsdp'=8,'seq'=4] {'fsdp'}, dimensions={0}, use_global_device_ids=true | all-gather | bytes 41472 | tf_op jit(solution)/shard_map/all_gather | solution.py:875
  499.5 8.6 %place_columns.5 = (f32[256,5120]{1,0:T(8,128)}, f32[256,5120]{1,0:T(8,128)}, f32[256,128]{1,0:T(8,128)}) custom-call(s32[1]{0:T(128)} %bitcast.place_ref, bf16[256,2560]{1,0:T(8,128)(2,1)} %reduce-scatter.7.cloned.1.call-done.refs_0_, bf16[256,2560]{1,0:T(8,128)(2,1)} %collective-permute-done.35.refs_1_, bf16[256,2560]{1,0:T(8,128)(2,1)} %collective-permute-done.36.refs_2_, ...), custom_call_target="tpu_custom_call" | custom-call | bytes 21233664 | tf_op jit(solution)/shard_map/place_columns/pallas_call | solution.py:577
  528.9 6.5 %place_columns.6 = (f32[256,2048]{1,0:T(8,128)}, f32[256,2048]{1,0:T(8,128)}, f32[256,2048]{1,0:T(8,128)}, f32[256,128]{1,0:T(8,128)}) custom-call(s32[1]{0:T(128)} %bitcast.place_ref, bf16[256,1536]{1,0:T(8,128)(2,1)} %reduce-scatter.9.cloned.1.call-done.refs_0_, bf16[256,1536]{1,0:T(8,128)(2,1)} %copy-done.16, bf16[256,1536]{1,0:T(8,128)(2,1)} %copy-done.15, ...), custom_call_target="tpu_custom_call" | custom-call | bytes 12845056 | tf_op jit(solution)/shard_map/place_columns/pallas_call | solution.py:577
  (310 shorter events, 227.4 us)
Async XLA Ops:
  7.2 92.2 %all-gather.4.cloned.1.call-start = ((), (), s32[]{:S(2)}) async-start(), calls=%async_computation.4 | async-start | bytes 9437184 | tf_op jit(solution)/shard_map/all_gather | solution.py:721
  9.7 202.8 %all-gather.8.cloned.1.call-start = ((), (), s32[]{:S(2)}) async-start(), calls=%async_computation.6 | async-start | bytes 11796480 | tf_op jit(solution)/shard_map/all_gather | solution.py:721
  9.7 26.4 %collective-permute-start.1 = (bf16[256,2048]{1,0:T(8,128)(2,1)}, bf16[256,2048]{1,0:T(8,128)(2,1)S(1)}, u32[]{:S(2)}, u32[]{:S(2)}) collective-permute-start(bf16[256,2048]{1,0:T(8,128)(2,1)} %bitcast.42), channel_id=1, source_target_pairs={{0,2},{1,3},{2,0},{3,1},{4,6},{5,7},{6,4},{7,5},{8,10},{9,11},{10,... | collective-permute-start | bytes 3145736 | tf_op jit(solution)/shard_map/ppermute | solution.py:358
  12.7 24.9 %collective-permute-start = (bf16[256,2048]{1,0:T(8,128)(2,1)}, bf16[256,2048]{1,0:T(8,128)(2,1)}, u32[]{:S(2)}, u32[]{:S(2)}) collective-permute-start(bf16[256,2048]{1,0:T(8,128)(2,1)} %bitcast.43), channel_id=1, source_target_pairs={{0,1},{1,0},{2,3},{3,2},{4,5},{5,4},{6,7},{7,6},{8,9},{9,8},{10,11... | collective-permute-start | bytes 3145736 | tf_op jit(solution)/shard_map/ppermute | solution.py:358
  58.8 193.1 %all-gather.6.cloned.1.call-start = ((), (), s32[]{:S(2)}) async-start(), calls=%async_computation.5 | async-start | bytes 5898240 | tf_op jit(solution)/shard_map/all_gather | solution.py:721
  58.8 23.2 %collective-permute-start.5 = (bf16[256,2048]{1,0:T(8,128)(2,1)}, bf16[256,2048]{1,0:T(8,128)(2,1)}, u32[]{:S(2)}, u32[]{:S(2)}) collective-permute-start(bf16[256,2048]{1,0:T(8,128)(2,1)} %bitcast.46), channel_id=1, source_target_pairs={{0,2},{1,3},{2,0},{3,1},{4,6},{5,7},{6,4},{7,5},{8,10},{9,11},{10,... | collective-permute-start | bytes 3145736 | tf_op jit(solution)/shard_map/ppermute | solution.py:358
  60.4 23.8 %collective-permute-start.4 = (bf16[256,2048]{1,0:T(8,128)(2,1)}, bf16[256,2048]{1,0:T(8,128)(2,1)}, u32[]{:S(2)}, u32[]{:S(2)}) collective-permute-start(bf16[256,2048]{1,0:T(8,128)(2,1)} %bitcast.47), channel_id=1, source_target_pairs={{0,1},{1,0},{2,3},{3,2},{4,5},{5,4},{6,7},{7,6},{8,9},{9,8},{10,11... | collective-permute-start | bytes 3145736 | tf_op jit(solution)/shard_map/ppermute | solution.py:358
  110.8 214.6 %reduce-scatter.5.cloned.1.call-start = ((), (), s32[]{:S(2)}) async-start(), calls=%async_computation.7 | async-start | bytes 5898240 | tf_op jit(solution)/shard_map/reduce_scatter | solution.py:783
  178.0 24.4 %collective-permute-start.12 = (bf16[256,2048]{1,0:T(8,128)(2,1)S(1)}, bf16[256,2048]{1,0:T(8,128)(2,1)S(1)}, u32[]{:S(2)}, u32[]{:S(2)}) collective-permute-start(bf16[256,2048]{1,0:T(8,128)(2,1)S(1)} %get-tuple-element.218), channel_id=1, source_target_pairs={{0,1},{1,0},{2,3},{3,2},{4,5},{5,4},{6,7},{7,6},{8,9},{9,8},{10,11... | collective-permute-start | bytes 3145736 | tf_op jit(solution)/shard_map/ppermute | solution.py:358
  240.6 187.3 %reduce-scatter.7.cloned.1.call-start = ((), (), s32[]{:S(2)}) async-start(), calls=%async_computation.8 | async-start | bytes 11796480 | tf_op jit(solution)/shard_map/reduce_scatter | solution.py:783
  319.1 179.0 %reduce-scatter.9.cloned.1.call-start = ((), (), s32[]{:S(2)}) async-start(), calls=%async_computation.9 | async-start | bytes 7077888 | tf_op jit(solution)/shard_map/reduce_scatter | solution.py:783
  325.6 24.3 %collective-permute-start.24 = (bf16[256,2048]{1,0:T(8,128)(2,1)}, bf16[256,2048]{1,0:T(8,128)(2,1)S(1)}, u32[]{:S(2)}, u32[]{:S(2)}) collective-permute-start(bf16[256,2048]{1,0:T(8,128)(2,1)} %get-tuple-element.141), channel_id=1, source_target_pairs={{0,1},{1,0},{2,3},{3,2},{4,5},{5,4},{6,7},{7,6},{8,9},{9,8},{10,11... | collective-permute-start | bytes 3145736 | tf_op jit(solution)/shard_map/ppermute | solution.py:358
  360.4 48.4 %collective-permute-start.32 = (bf16[256,1280]{1,0:T(8,128)(2,1)S(1)}, bf16[256,1280]{1,0:T(8,128)(2,1)S(1)}, u32[]{:S(2)}, u32[]{:S(2)}) collective-permute-start(bf16[256,1280]{1,0:T(8,128)(2,1)S(1)} %copy-done.20), channel_id=1, source_target_pairs={{0,3},{1,2},{2,1},{3,0},{4,7},{5,6},{6,5},{7,4},{8,11},{9,10},{10,... | collective-permute-start | bytes 1966088 | tf_op jit(solution)/shard_map/ppermute | solution.py:358
  362.3 46.5 %collective-permute-start.31 = (bf16[256,1280]{1,0:T(8,128)(2,1)S(1)}, bf16[256,1280]{1,0:T(8,128)(2,1)S(1)}, u32[]{:S(2)}, u32[]{:S(2)}) collective-permute-start(bf16[256,1280]{1,0:T(8,128)(2,1)S(1)} %copy-done.20), channel_id=1, source_target_pairs={{0,2},{1,3},{2,0},{3,1},{4,6},{5,7},{6,4},{7,5},{8,10},{9,11},{10,... | collective-permute-start | bytes 1966088 | tf_op jit(solution)/shard_map/ppermute | solution.py:358
  363.0 45.8 %collective-permute-start.30 = (bf16[256,1280]{1,0:T(8,128)(2,1)S(1)}, bf16[256,1280]{1,0:T(8,128)(2,1)S(1)}, u32[]{:S(2)}, u32[]{:S(2)}) collective-permute-start(bf16[256,1280]{1,0:T(8,128)(2,1)S(1)} %copy-done.20), channel_id=1, source_target_pairs={{0,1},{1,0},{2,3},{3,2},{4,5},{5,4},{6,7},{7,6},{8,9},{9,8},{10,11... | collective-permute-start | bytes 1966088 | tf_op jit(solution)/shard_map/ppermute | solution.py:358
  363.9 47.5 %collective-permute-start.28 = (bf16[256,2048]{1,0:T(8,128)(2,1)S(1)}, bf16[256,2048]{1,0:T(8,128)(2,1)S(1)}, u32[]{:S(2)}, u32[]{:S(2)}) collective-permute-start(bf16[256,2048]{1,0:T(8,128)(2,1)S(1)} %get-tuple-element.150), channel_id=1, source_target_pairs={{0,1},{1,0},{2,3},{3,2},{4,5},{5,4},{6,7},{7,6},{8,9},{9,8},{10,11... | collective-permute-start | bytes 3145736 | tf_op jit(solution)/shard_map/ppermute | solution.py:358
  365.0 46.5 %collective-permute-start.29 = (bf16[256,2048]{1,0:T(8,128)(2,1)S(1)}, bf16[256,2048]{1,0:T(8,128)(2,1)S(1)}, u32[]{:S(2)}, u32[]{:S(2)}) collective-permute-start(bf16[256,2048]{1,0:T(8,128)(2,1)S(1)} %get-tuple-element.151), channel_id=1, source_target_pairs={{0,2},{1,3},{2,0},{3,1},{4,6},{5,7},{6,4},{7,5},{8,10},{9,11},{10,... | collective-permute-start | bytes 3145736 | tf_op jit(solution)/shard_map/ppermute | solution.py:358
  427.9 96.5 %reduce-scatter.11.cloned.1.call-start = ((), (), s32[]{:S(2)}) async-start(), calls=%async_computation.10 | async-start | bytes 1310720 | tf_op jit(solution)/shard_map/reduce_scatter | solution.py:783
  429.4 34.2 %collective-permute-start.36 = (bf16[256,2560]{1,0:T(8,128)(2,1)}, bf16[256,2560]{1,0:T(8,128)(2,1)}, u32[]{:S(2)}, u32[]{:S(2)}) collective-permute-start(bf16[256,2560]{1,0:T(8,128)(2,1)} %reduce-scatter.7.cloned.1.call-done.refs_0_), channel_id=1, source_target_pairs={{0,2},{1,3},{2,0},{3,1},{4,6},{5,7},{6,4},{7,5},{8,10},{9,11},{10,... | collective-permute-start | bytes 3932168 | tf_op jit(solution)/shard_map/ppermute | solution.py:358
  429.7 33.8 %collective-permute-start.35 = (bf16[256,2560]{1,0:T(8,128)(2,1)}, bf16[256,2560]{1,0:T(8,128)(2,1)}, u32[]{:S(2)}, u32[]{:S(2)}) collective-permute-start(bf16[256,2560]{1,0:T(8,128)(2,1)} %reduce-scatter.7.cloned.1.call-done.refs_0_), channel_id=1, source_target_pairs={{0,1},{1,0},{2,3},{3,2},{4,5},{5,4},{6,7},{7,6},{8,9},{9,8},{10,11... | collective-permute-start | bytes 3932168 | tf_op jit(solution)/shard_map/ppermute | solution.py:358
  435.1 48.8 %collective-permute-start.39 = (bf16[256,2048]{1,0:T(8,128)(2,1)}, bf16[256,2048]{1,0:T(8,128)(2,1)}, u32[]{:S(2)}, u32[]{:S(2)}) collective-permute-start(bf16[256,2048]{1,0:T(8,128)(2,1)} %get-tuple-element.222), channel_id=1, source_target_pairs={{0,2},{1,3},{2,0},{3,1},{4,6},{5,7},{6,4},{7,5},{8,10},{9,11},{10,... | collective-permute-start | bytes 3145736 | tf_op jit(solution)/shard_map/ppermute | solution.py:358
  435.2 49.1 %collective-permute-start.38 = (bf16[256,2048]{1,0:T(8,128)(2,1)}, bf16[256,2048]{1,0:T(8,128)(2,1)}, u32[]{:S(2)}, u32[]{:S(2)}) collective-permute-start(bf16[256,2048]{1,0:T(8,128)(2,1)} %get-tuple-element.223), channel_id=1, source_target_pairs={{0,1},{1,0},{2,3},{3,2},{4,5},{5,4},{6,7},{7,6},{8,9},{9,8},{10,11... | collective-permute-start | bytes 3145736 | tf_op jit(solution)/shard_map/ppermute | solution.py:358
  465.8 31.4 %collective-permute-start.43 = (bf16[128,2560]{1,0:T(8,128)(2,1)S(1)}, bf16[128,2560]{1,0:T(8,128)(2,1)S(1)}, u32[]{:S(2)}, u32[]{:S(2)}) collective-permute-start(bf16[128,2560]{1,0:T(8,128)(2,1)S(1)} %slice.199), channel_id=1, source_target_pairs={{0,1},{1,0},{2,3},{3,2},{4,5},{5,4},{6,7},{7,6},{8,9},{9,8},{10,11... | collective-permute-start | bytes 1966088 | tf_op jit(solution)/shard_map/ppermute | solution.py:358
  466.2 31.1 %collective-permute-start.44 = (bf16[128,2560]{1,0:T(8,128)(2,1)S(1)}, bf16[128,2560]{1,0:T(8,128)(2,1)}, u32[]{:S(2)}, u32[]{:S(2)}) collective-permute-start(bf16[128,2560]{1,0:T(8,128)(2,1)S(1)} %slice.200), channel_id=1, source_target_pairs={{0,2},{1,3},{2,0},{3,1},{4,6},{5,7},{6,4},{7,5},{8,10},{9,11},{10,... | collective-permute-start | bytes 1966088 | tf_op jit(solution)/shard_map/ppermute | solution.py:358
  (84 other events, 1118.5 us)
Sparse Core Ops, SparseCore 0:
  10.2 84.7 all-gather.3
  97.2 97.9 all-gather.7
  197.4 54.4 all-gather.5
  254.6 58.6 reduce-scatter.4
  318.4 107.2 reduce-scatter.6
  428.0 68.4 reduce-scatter.8
  498.8 25.4 reduce-scatter.10
